TPU v7x, 256 devices: a whole 4x4x8 slice. The times are simulated.
256 devices in a mesh: dp: 2 (over core), section: 4 (over x), tensor: 32 (over z, y).
Axes of the slice: x: 4, y: 4, z: 8, core: 2. Of those that a mesh axis runs over, the one named last changes fastest.
Arguments:
- hidden: bfloat16 [3, 4, 1024, 8192], P(None, 'section', ('dp', 'tensor')), parts along dimension 2, may hold values from -6 to 6
- exits: int32 [3, 1024], P(None, 'dp'), parts along dimension 1, may hold values from 0 to 2
- lengths: int32 [1024], P('dp'), parts along dimension 0, may hold values from 1 to 4092
- norm_gain: bfloat16 [4, 8192], P('section'), may hold values from 0.5 to 1.5
- w_key: bfloat16 [4, 2, 512, 8192], P('section', None, 'tensor'), may hold values from -0.0625 to 0.0625
- w_value: bfloat16 [4, 2, 512, 8192], P('section', None, 'tensor'), may hold values from -0.0625 to 0.0625
- w_query: bfloat16 [4, 2, 2048, 8192], P('section', None, 'tensor'), may hold values from -0.0625 to 0.0625
Outputs:
- new_keys: bfloat16 [3, 4, 2, 512, 1024], P(None, 'section', None, 'tensor', 'dp'), parts along dimension 4
- new_values: bfloat16 [3, 4, 2, 512, 1024], P(None, 'section', None, 'tensor', 'dp'), parts along dimension 4
- new_queries: bfloat16 [3, 4, 2, 2048, 1024], P(None, 'section', None, 'tensor', 'dp'), parts along dimension 4
There are 2 independent parts, one for each index of `dp`. A program takes and returns all parts, laid end to end along the dimension named above; an argument that names none is the same for every part. Nothing has to cross between parts.
Inputs may be any that keep to these rules, and one draw needn't show every extreme that they name: 0: the row runs through all layers; 1: it exits after 4 // 4 layers; 2: after 4 // 2 layers.
All inputs are finite; a program needn't handle non-finite values.
Results may differ from a plain program's by a relative error of at most 0.0049.
Values may be sent and summed in bfloat16 or wider, within the bound.
No kernel may reach another device: no remote copies, remote signals or barrier semaphores. Data moves between devices by JAX's collectives and lax.ppermute only.
A program may use at most 128 MiB of HBM per device.

v0:
```python
import jax
import jax.numpy as jnp
from jax import lax
from jax.sharding import PartitionSpec as P

HEAD = 128


eps = 1e-05
theta = 10000.0


def rotate(pairs, positions, first, head):
    count = pairs.shape[1]
    index = ((jnp.arange(count, dtype=jnp.int32) + first) % (head // 2)).astype(jnp.float32)
    freqs = theta ** (-(index * 2.0) / head)
    angles = freqs[:, None] * positions.astype(jnp.float32)[None, :]
    cosine = jnp.cos(angles)
    sine = jnp.sin(angles)
    upper = pairs[0]
    lower = pairs[1]
    return jnp.stack([upper * cosine - lower * sine, lower * cosine + upper * sine], axis=0)


def apply_weight(weight, normed):
    dim = weight.shape[2]
    flat = weight.reshape(-1, dim)
    out = lax.dot_general(
        flat, normed, (((1,), (1,)), ((), ())), preferred_element_type=jnp.float32
    )
    return out.reshape(2, weight.shape[1], normed.shape[0])


def project(rows_in, gain, key_w, value_w, query_w, positions, first_kv, first_q, head):
    wide = rows_in.astype(jnp.float32)
    scale = lax.rsqrt(jnp.mean(wide * wide, axis=-1, keepdims=True) + eps)
    normed = (wide * scale * gain.astype(jnp.float32)).astype(jnp.bfloat16)
    keys = apply_weight(key_w, normed)
    values = apply_weight(value_w, normed)
    queries = apply_weight(query_w, normed)
    keys = rotate(keys, positions, first_kv, head)
    queries = rotate(queries, positions, first_q, head)
    return (keys.astype(jnp.bfloat16), values.astype(jnp.bfloat16), queries.astype(jnp.bfloat16))


def on_device(hidden, exits, lengths, norm_gain, w_key, w_value, w_query):
    segment = lax.axis_index("section")
    segments = lax.axis_size("section")
    shard = hidden.shape[2]
    tensor_index = lax.axis_index("tensor")
    first_row = tensor_index * shard
    gain = norm_gain[0]
    key_w = w_key[0]
    value_w = w_value[0]
    query_w = w_query[0]
    kv_cols = key_w.shape[1]
    q_cols = query_w.shape[1]
    first_kv = tensor_index * kv_cols
    first_q = tensor_index * q_cols
    key_steps = []
    value_steps = []
    query_steps = []
    for step in range(hidden.shape[0]):
        own = hidden[step, 0]
        code = lax.dynamic_slice_in_dim(exits[step], first_row, shard)
        depth = jnp.where(
            code == 1, segments // 4, jnp.where(code == 2, segments // 2, segments)
        ).astype(jnp.int32)
        pieces = lax.all_gather(own[None], "section", axis=0, tiled=True)
        source = jnp.minimum(depth, segment)
        picked = (jnp.arange(segments, dtype=jnp.int32)[:, None] == source[None, :]).astype(
            jnp.bfloat16
        )
        chosen = jnp.einsum(
            "kr,krd->rd", picked, pieces, preferred_element_type=jnp.float32
        ).astype(jnp.bfloat16)
        positions = lengths + step
        keys, values, queries = project(
            lax.all_gather(chosen, "tensor", axis=0, tiled=True),
            gain,
            key_w,
            value_w,
            query_w,
            positions,
            first_kv,
            first_q,
            HEAD,
        )
        joined = jnp.concatenate([keys, values, queries], axis=1)
        key_steps.append(joined[:, :kv_cols])
        value_steps.append(joined[:, kv_cols : 2 * kv_cols])
        query_steps.append(joined[:, 2 * kv_cols :])
    return (
        jnp.stack(key_steps)[:, None],
        jnp.stack(value_steps)[:, None],
        jnp.stack(query_steps)[:, None],
    )


def solution(mesh):
    return jax.shard_map(
        on_device,
        mesh=mesh,
        in_specs=(
            P(None, "section", ("dp", "tensor"), None),
            P(None, "dp"),
            P("dp"),
            P("section", None),
            P("section", None, "tensor", None),
            P("section", None, "tensor", None),
            P("section", None, "tensor", None),
        ),
        out_specs=(
            P(None, "section", None, "tensor", "dp"),
            P(None, "section", None, "tensor", "dp"),
            P(None, "section", None, "tensor", "dp"),
        ),
        check_vma=False,
    )
```

profile of v0, /device:TPU:1, one launch (start us, length us, event | category | flops | bytes accessed | tf_op | source)
XLA Modules:
  0.0 450.5 jit_solution(6439637991906178633)
XLA Ops:
  7.2 2.1 fusion.96
  9.5 0.7 all-gather.16.cloned.1.call-update
  10.2 0.7 all-gather.20.cloned.1.call-update
  10.9 0.8 fusion.97
  12.0 27.3 %all-gather.18.cloned.1.call-done = bf16[4,1,16,8192]{3,2,1,0:T(8,128)(2,1)} async-done(((bf16[1,1,16,8192]{3,2,1,0:T(8,128)(2,1)}), bf16[4,1,16,8192]{3,2,1,0:T(8,128)(2,1)}) %all-gather.18.cloned.1.call-update) | async-done | bytes 1048592 | tf_op jit(solution)/shard_map/all_gather | solution.py:69
  39.3 2.6 fusion.11
  41.9 1.0 copy.35
  43.1 25.4 %all-gather.16.cloned.1.call-done = bf16[4,1,16,8192]{3,2,1,0:T(8,128)(2,1)} async-done(((bf16[1,1,16,8192]{3,2,1,0:T(8,128)(2,1)}), bf16[4,1,16,8192]{3,2,1,0:T(8,128)(2,1)}) %all-gather.16.cloned.1.call-update) | async-done | bytes 1048592 | tf_op jit(solution)/shard_map/all_gather | solution.py:69
  68.5 2.6 fusion.13
  71.2 1.0 copy.36
  72.6 24.6 %all-gather.20.cloned.1.call-done = bf16[4,1,16,8192]{3,2,1,0:T(8,128)(2,1)} async-done(((bf16[1,1,16,8192]{3,2,1,0:T(8,128)(2,1)}), bf16[4,1,16,8192]{3,2,1,0:T(8,128)(2,1)}) %all-gather.20.cloned.1.call-update) | async-done | bytes 1048592 | tf_op jit(solution)/shard_map/all_gather | solution.py:69
  97.2 2.6 fusion.9
  99.9 1.0 copy.34
  101.0 98.1 %all-gather.12.cloned.1.call-done = bf16[512,8192]{1,0:T(8,128)(2,1)} async-done(((bf16[16,8192]{1,0:T(8,128)(2,1)}), bf16[512,8192]{1,0:T(8,128)(2,1)}) %all-gather.12.cloned.1.call-update) | async-done | bytes 8388624 | tf_op jit(solution)/shard_map/all_gather | solution.py:79
  199.1 5.1 %fusion.3 = f32[512]{0:T(512)S(1)} fusion(bf16[512,8192]{1,0:T(8,128)(2,1)} %all-gather.12.cloned.1.call-done), kind=kLoop, calls=%fused_computation.9 | loop fusion | flops 12582400 | bytes 8390656 | tf_op jit(solution)/shard_map/reduce_sum | solution.py:36
  204.2 93.5 %all-gather.10.cloned.1.call-done = bf16[512,8192]{1,0:T(8,128)(2,1)} async-done(((bf16[16,8192]{1,0:T(8,128)(2,1)}), bf16[512,8192]{1,0:T(8,128)(2,1)}) %all-gather.10.cloned.1.call-update) | async-done | bytes 8388624 | tf_op jit(solution)/shard_map/all_gather | solution.py:79
  297.8 5.1 %fusion = f32[512]{0:T(512)S(1)} fusion(bf16[512,8192]{1,0:T(8,128)(2,1)} %all-gather.10.cloned.1.call-done), kind=kLoop, calls=%fused_computation.6 | loop fusion | flops 12582400 | bytes 8390656 | tf_op jit(solution)/shard_map/reduce_sum | solution.py:36
  302.9 93.0 %all-gather.14.cloned.1.call-done = bf16[512,8192]{1,0:T(8,128)(2,1)} async-done(((bf16[16,8192]{1,0:T(8,128)(2,1)}), bf16[512,8192]{1,0:T(8,128)(2,1)}) %all-gather.14.cloned.1.call-update) | async-done | bytes 8388624 | tf_op jit(solution)/shard_map/all_gather | solution.py:79
  395.9 5.3 %fusion.6 = f32[512]{0:T(512)S(1)} fusion(bf16[512,8192]{1,0:T(8,128)(2,1)} %all-gather.14.cloned.1.call-done), kind=kLoop, calls=%fused_computation.12 | loop fusion | flops 12582400 | bytes 8390656 | tf_op jit(solution)/shard_map/reduce_sum | solution.py:36
  401.7 12.9 %fusion.2 = (bf16[512,8192]{1,0:T(8,128)(2,1)S(1)}, bf16[512,8192]{1,0:T(8,128)(2,1)S(1)}, bf16[512,8192]{1,0:T(8,128)(2,1)}) fusion(bf16[512,8192]{1,0:T(8,128)(2,1)S(1)} %copy-done.1, f32[8192]{0:T(1024)S(1)} %bitcast.121, f32[512]{0:T(512)S(1)} %add_rsqrt_fusion.2, f32[512]{0:T(512)S(1)} %add_rsqrt_fusion.1, ...), kind=kLoop, calls=%fused_computation.8 | loop fusion | flops 50331648 | bytes 50370560 | tf_op jit(solution)/shard_map/convert_element_type | solution.py:37
  414.6 2.9 convolution_bitcast_fusion.1
  417.5 2.9 convolution_bitcast_fusion.2
  420.5 2.6 convolution_convert_fusion.2
  423.1 2.6 convolution_convert_fusion.1
  425.8 2.9 convolution_bitcast_fusion
  428.7 2.9 convolution_convert_fusion
  431.6 2.6 convolution_bitcast_fusion.3
  434.2 2.6 convolution_bitcast_fusion.4
  436.8 2.6 convolution_bitcast_fusion.5
  439.4 0.7 maximum_bitcast_fusion.2
  440.1 1.6 fusion.40
  442.2 0.8 maximum_bitcast_fusion
  (44 shorter events, 2.8 us)
Async XLA Ops:
  7.2 407.4 %copy-start = (bf16[1,2,64,8192]{3,2,1,0:T(8,128)(2,1)S(1)}, bf16[1,2,64,8192]{3,2,1,0:T(8,128)(2,1)}, u32[]{:S(2)}) copy-start(bf16[1,2,64,8192]{3,2,1,0:T(8,128)(2,1)} %param.13) | copy-start | bytes 6291460
  7.2 93.8 %copy-start.4 = (bf16[1,8192]{1,0:T(2,128)(2,1)S(1)}, bf16[1,8192]{1,0:T(2,128)(2,1)}, u32[]{:S(2)}) copy-start(bf16[1,8192]{1,0:T(2,128)(2,1)} %param.10) | copy-start | bytes 49156
  7.2 93.8 %copy-start.5 = (s32[512]{0:T(512)S(1)}, s32[512]{0:T(512)}, u32[]{:S(2)}) copy-start(s32[512]{0:T(512)} %param.9) | copy-start | bytes 6148
  7.2 32.1 %all-gather.18.cloned.1.call-start = ((), (), s32[]{:S(2)}) async-start(), calls=%async_computation.4 | async-start | bytes 1310720 | tf_op jit(solution)/shard_map/all_gather | solution.py:69
  9.4 59.1 %all-gather.16.cloned.1.call-start = ((), (), s32[]{:S(2)}) async-start(), calls=%async_computation.3 | async-start | bytes 1310720 | tf_op jit(solution)/shard_map/all_gather | solution.py:69
  10.2 87.1 %all-gather.20.cloned.1.call-start = ((), (), s32[]{:S(2)}) async-start(), calls=%async_computation.5 | async-start | bytes 1310720 | tf_op jit(solution)/shard_map/all_gather | solution.py:69
  10.9 188.2 %all-gather.12.cloned.1.call-start = ((), (), s32[]{:S(2)}) async-start(), calls=%async_computation.1 | async-start | bytes 8650752 | tf_op jit(solution)/shard_map/all_gather | solution.py:79
  42.9 254.9 %all-gather.10.cloned.1.call-start = ((), (), s32[]{:S(2)}) async-start(), calls=%async_computation | async-start | bytes 8650752 | tf_op jit(solution)/shard_map/all_gather | solution.py:79
  72.2 323.7 %all-gather.14.cloned.1.call-start = ((), (), s32[]{:S(2)}) async-start(), calls=%async_computation.2 | async-start | bytes 8650752 | tf_op jit(solution)/shard_map/all_gather | solution.py:79
  395.9 5.8 %copy-start.1 = (bf16[512,8192]{1,0:T(8,128)(2,1)S(1)}, bf16[512,8192]{1,0:T(8,128)(2,1)}, u32[]{:S(2)}) copy-start(bf16[512,8192]{1,0:T(8,128)(2,1)} %all-gather.10.cloned.1.call-done) | copy-start | bytes 25165828
  414.6 5.9 %copy-start.2 = (bf16[1,2,16,8192]{3,2,1,0:T(8,128)(2,1)S(1)}, bf16[1,2,16,8192]{3,2,1,0:T(8,128)(2,1)}, u32[]{:S(2)}) copy-start(bf16[1,2,16,8192]{3,2,1,0:T(8,128)(2,1)} %param.12) | copy-start | bytes 1572868
  420.4 5.3 %slice-start = ((s8[8388608]{0:T(1024)(128)(4,1)}), s8[4194304]{0:T(1024)(128)(4,1)S(1)}, s32[]{:S(2)}) async-start(s8[8388608]{0:T(1024)(128)(4,1)} %bitcast.107), calls=%async_computation.6 | async-start | bytes 8388608
  423.1 2.7 slice-start.1
  425.8 5.8 %copy-start.3 = (bf16[1,2,16,8192]{3,2,1,0:T(8,128)(2,1)S(1)}, bf16[1,2,16,8192]{3,2,1,0:T(8,128)(2,1)}, u32[]{:S(2)}) copy-start(bf16[1,2,16,8192]{3,2,1,0:T(8,128)(2,1)} %param.11) | copy-start | bytes 1572868
Sparse Core Ops, SparseCore 0:
  9.8 29.3 all-gather.17
  41.6 26.8 all-gather.15
  70.4 26.8 all-gather.19
  99.7 99.3 all-gather.11
  202.1 95.6 all-gather.9
  300.2 95.6 all-gather.13
where the time goes:
time: 451 us; the launch traced here: 450 us
  waiting for transfers between devices  363 us (80%)
  other arithmetic  32.9 us (7%)
  matrix products  32.6 us (7%)
  between operations  14.3 us (3%)
  local copies, waits for them, and re-layouts  6.86 us (2%)
    all_gather x3, waiting for transfers between devices, on_device(): lax.all_gather(chosen, 'tensor', axis=0, tiled=True)  285 us
    all_gather x3, waiting for transfers between devices, on_device(): pieces = lax.all_gather(own[None], 'section', axis=0, tiled=True)  77.4 us
    dot_general x9, matrix products, apply_weight(): lax.dot_general(flat, normed, (((1,), (1,)), ((), ())), preferred_element...  24.7 us
    reduce_sum x3, other arithmetic, project(): scale = lax.rsqrt(jnp.mean(wide * wide, axis=-1, keepdims=True) + eps)  15.5 us
    convert_element_type x1, other arithmetic, project(): normed = (wide * scale * gain.astype(jnp.float32)).astype(jnp.bfloat16)  12.9 us
  transfers between devices with their start and end apart: 6, of which 6 were waited for; matrix products, arithmetic and copies ran while one was open for 5% of the time, Pallas kernels for 0%

commit v1 on v0

v1 whole, which is shorter than its diff:
```python
import functools

import jax
import jax.numpy as jnp
from jax import lax
from jax.experimental import pallas as pl
from jax.experimental.pallas import tpu as pltpu
from jax.sharding import PartitionSpec as P

HEAD = 128
EPS = 1e-05
THETA = 10000.0

STEPS = 3
DIM = 8192
HALF = DIM // 2
SHARD = 16
NZ = 8
NY = 4
KV = 16
Q = 64
SIDE = Q + 2 * KV
COLS = 2 * SIDE
ROWS = STEPS * SHARD
LANES = NZ * SHARD
PARTS = 2
PART = DIM // PARTS
MEBI = 1024 * 1024
VMEM_PROJECT = 16 * MEBI
EXTRA = 128
CHUNK = 512
WEIGHT_GROUPS = [
    [core * NZ * NY + z * NY + y for y in range(NY) for core in range(2)] for z in range(NZ)
]


def shift_z(value, by):
    pairs = [(z * NY + y, ((z + by) % NZ) * NY + y) for z in range(NZ) for y in range(NY)]
    return lax.ppermute(value, "tensor", pairs)


def shift_y(value, by):
    pairs = [(z * NY + y, z * NY + (y + by) % NY) for z in range(NZ) for y in range(NY)]
    return lax.ppermute(value, "tensor", pairs)


def copies(pairs, sems):
    started = []
    for i, (source, target) in enumerate(pairs):
        copy = pltpu.make_async_copy(source, target, sems.at[i])
        copy.start()
        started.append(copy)
    return started


def fetch_kernel(*refs):
    weight_ref, low_refs, high_refs = refs[0], refs[1:NZ], refs[NZ : 2 * NZ - 1]
    weight_out, low_out, high_out, sems = refs[2 * NZ - 1 :]
    pairs = [(weight_ref.at[:, at], weight_out.at[:, at]) for at in (slice(0, HALF), slice(HALF, DIM))]
    pairs += [(ref, low_out.at[i]) for i, ref in enumerate(low_refs)]
    pairs += [(ref, high_out.at[i]) for i, ref in enumerate(high_refs)]
    for copy in copies(pairs, sems):
        copy.wait()


def fetch(weight, low, high):
    operands = [pltpu.with_memory_space_constraint(x, pltpu.HBM) for x in (weight, *low, *high)]
    shapes = [
        weight.shape,
        (NZ - 1, ROWS, HALF),
        (NZ - 1, ROWS, HALF + EXTRA),
    ]
    return pl.pallas_call(
        fetch_kernel,
        out_shape=[jax.ShapeDtypeStruct(shape, jnp.bfloat16) for shape in shapes],
        in_specs=[pl.BlockSpec(memory_space=pltpu.HBM)] * len(operands),
        out_specs=[pl.BlockSpec(memory_space=pltpu.VMEM)] * 3,
        scratch_shapes=[pltpu.SemaphoreType.DMA((2 * NZ,))],
        compiler_params=pltpu.CompilerParams(vmem_limit_bytes=VMEM_PROJECT),
        cost_estimate=pl.CostEstimate(
            flops=0, bytes_accessed=2 * DIM * (NY * COLS + 2 * NZ * ROWS), transcendentals=0
        ),
    )(*operands)


def weigh_kernel(first, own_ref, one_ref, two_ref, back_ref, gain_ref, *refs):
    out_ref = refs[0] if first else refs[1]
    for t in range(STEPS):
        rows = slice(t * SHARD, (t + 1) * SHARD)
        back = back_ref[rows]
        squares = jnp.zeros((SHARD, CHUNK), jnp.float32)
        for start in range(0, HALF, CHUNK):
            at = slice(start, start + CHUNK)
            own, one, two = (ref[rows, at].astype(jnp.float32) for ref in (own_ref, one_ref, two_ref))
            wide = jnp.where(back == 2, two, jnp.where(back == 1, one, own))
            squares += wide * wide
            out_ref[rows, at] = (wide * gain_ref[:, at].astype(jnp.float32)).astype(jnp.bfloat16)
        square = jnp.sum(squares, axis=-1, keepdims=True)
        if first:
            refs[1][rows] = square
            continue
        rest = lax.rsqrt((refs[0][rows] + square) / DIM + EPS)
        lane = lax.broadcasted_iota(jnp.int32, (SHARD, EXTRA), 1)
        tail = jnp.zeros((SHARD, EXTRA), jnp.float32)
        for i in range(3):
            term = rest.astype(jnp.bfloat16).astype(jnp.float32)
            tail = jnp.where(lane == i, term, tail)
            rest = rest - term
        out_ref[rows, HALF:] = tail.astype(jnp.bfloat16)


def weigh_rows(states, back, gain, earlier):
    whole = pl.BlockSpec(memory_space=pltpu.VMEM)
    first = earlier is None
    out_shape = [jax.ShapeDtypeStruct((ROWS, HALF + (0 if first else EXTRA)), jnp.bfloat16)]
    if first:
        out_shape.append(jax.ShapeDtypeStruct((ROWS, 1), jnp.float32))
    operands = [*states, back, gain] + ([] if first else [earlier])
    return pl.pallas_call(
        functools.partial(weigh_kernel, first),
        out_shape=out_shape,
        in_specs=[whole] * len(operands),
        out_specs=[whole] * len(out_shape),
        compiler_params=pltpu.CompilerParams(vmem_limit_bytes=16 * MEBI),
        cost_estimate=pl.CostEstimate(
            flops=6 * ROWS * HALF, bytes_accessed=8 * ROWS * HALF, transcendentals=0
        ),
    )(*operands)


def project_kernel(half, place_ref, weight_ref, near_ref, far_ref, *refs):
    far, sems = refs[-2:]

    waiting = []
    for part in range(HALF // PART):
        last = half == 1 and part == HALF // PART - 1
        at = slice(part * PART, (part + 1) * PART + (EXTRA if last else 0))
        waiting.append(copies([(far_ref.at[:, at], far.at[:, at])], sems.at[part : part + 1]))

    def piece(d, rows, columns):
        if d == 4:
            return far[rows, columns]
        return near_ref[d if d < 4 else d - 1, rows, columns]

    def in_order(first, width):
        rows = []
        for t in range(STEPS):
            at = slice(t * SHARD, (t + 1) * SHARD)
            rows += [piece(d, at, slice(first, first + width)) for d in range(NZ)]
        return jnp.concatenate(rows, axis=0)

    def multiply(part):
        for copy in waiting[part]:
            copy.wait()
        first = part * PART
        return lax.dot_general(
            weight_ref[:, half * HALF + first : half * HALF + first + PART],
            in_order(first, PART),
            (((1,), (1,)), ((), ())),
            preferred_element_type=jnp.float32,
        )

    if half == 0:
        total = refs[0]
        total[...] = multiply(0)
        for part in range(1, HALF // PART):
            total[...] += multiply(part)
        return

    carried, cos_ref, sin_ref, *outs, total = refs[:-2]
    total[...] = carried[...] + multiply(0)
    for part in range(1, HALF // PART):
        total[...] += multiply(part)
    y = place_ref[1]
    ones = jnp.where(lax.broadcasted_iota(jnp.int32, (8, EXTRA), 1) < 3, 1.0, 0.0)
    scale = lax.dot_general(
        ones.astype(jnp.bfloat16),
        in_order(HALF, EXTRA),
        (((1,), (1,)), ((), ())),
        preferred_element_type=jnp.float32,
    )[0:1]

    for by in range(NY):
        to = lax.rem(y + by, NY)
        kv_rows = pl.ds(pl.multiple_of(to * KV, KV), KV)
        low = to * COLS
        high = low + SIDE

        def part(base, offset, rows):
            return total[pl.ds(pl.multiple_of(base + offset, KV), rows), :] * scale

        def put(offset, value):
            outs[by][offset : offset + value.shape[0], :] = value.astype(jnp.bfloat16)

        a, b = part(low, Q, KV), part(high, Q, KV)
        cosine, sine = cos_ref[kv_rows, :], sin_ref[kv_rows, :]
        put(0, a * cosine - b * sine)
        put(KV, b * cosine + a * sine)
        put(2 * KV, part(low, Q + KV, KV))
        put(3 * KV, part(high, Q + KV, KV))
        a, b = part(low, 0, Q), part(high, 0, Q)
        cosine, sine = cos_ref[...], sin_ref[...]
        put(4 * KV, a * cosine - b * sine)
        put(4 * KV + Q, b * cosine + a * sine)


def project(place, weight, half, near, far, local=()):
    lanes = STEPS * LANES
    whole = pl.BlockSpec(memory_space=pltpu.VMEM)
    total = (NY * COLS, lanes)
    scratch = [
        pltpu.VMEM(far.shape, jnp.bfloat16),
        pltpu.SemaphoreType.DMA((HALF // PART,)),
    ]
    if half == 0:
        out_shape = [jax.ShapeDtypeStruct(total, jnp.float32)]
    else:
        out_shape = [jax.ShapeDtypeStruct((COLS, lanes), jnp.bfloat16)] * NY
        scratch = [pltpu.VMEM(total, jnp.float32)] + scratch
    return pl.pallas_call(
        functools.partial(project_kernel, half),
        out_shape=out_shape,
        in_specs=[pl.BlockSpec(memory_space=pltpu.SMEM), whole, whole]
        + [pl.BlockSpec(memory_space=pltpu.HBM)]
        + [whole] * len(local),
        out_specs=[whole] * len(out_shape),
        scratch_shapes=scratch,
        compiler_params=pltpu.CompilerParams(vmem_limit_bytes=VMEM_PROJECT),
        cost_estimate=pl.CostEstimate(
            flops=2 * NY * COLS * HALF * lanes,
            bytes_accessed=4 * HALF * (NY * COLS + lanes),
            transcendentals=0,
        ),
    )(place, weight, near, pltpu.with_memory_space_constraint(far, pltpu.HBM), *local)


def place_kernel(place_ref, *refs):
    pieces, (keys, values, queries) = refs[:NY], refs[NY:]
    y, z = place_ref[1], place_ref[2]
    width = NZ * NY * SHARD
    lane = lax.broadcasted_iota(jnp.int32, (LANES, 1), 0)
    column = lax.broadcasted_iota(jnp.int32, (LANES, width), 1)
    plane = lax.rem(z + NZ - lane // SHARD, NZ)
    chosen = []
    for by in range(NY):
        source = lax.rem(y + NY - by, NY)
        at = plane * (NY * SHARD) + source * SHARD + lane % SHARD
        chosen.append(jnp.where(at == column, 1.0, 0.0).astype(jnp.bfloat16))
    chosen = jnp.concatenate(chosen, axis=0)
    for t in range(STEPS):
        lanes = slice(t * LANES, (t + 1) * LANES)
        rows = [ref[:, lanes] for ref in pieces]
        full = jnp.dot(
            jnp.concatenate(rows, axis=1), chosen, preferred_element_type=jnp.float32
        ).astype(jnp.bfloat16)
        keys[t, 0] = full[: 2 * KV].reshape(2, KV, width)
        values[t, 0] = full[2 * KV : 4 * KV].reshape(2, KV, width)
        queries[t, 0] = full[4 * KV :].reshape(2, Q, width)


def place_outputs(place, pieces):
    width = NZ * NY * SHARD
    whole = pl.BlockSpec(memory_space=pltpu.VMEM)
    return pl.pallas_call(
        place_kernel,
        out_shape=[
            jax.ShapeDtypeStruct((STEPS, 1, 2, KV, width), jnp.bfloat16),
            jax.ShapeDtypeStruct((STEPS, 1, 2, KV, width), jnp.bfloat16),
            jax.ShapeDtypeStruct((STEPS, 1, 2, Q, width), jnp.bfloat16),
        ],
        in_specs=[pl.BlockSpec(memory_space=pltpu.SMEM)] + [whole] * len(pieces),
        out_specs=[whole] * 3,
        compiler_params=pltpu.CompilerParams(vmem_limit_bytes=16 * MEBI),
    )(place, *pieces)


def after(value, *earlier):
    return lax.optimization_barrier((value, *earlier))[0]


def on_device(hidden, exits, lengths, norm_gain, w_key, w_value, w_query):
    core = lax.axis_index("dp").astype(jnp.int32)
    layer = lax.axis_index("section").astype(jnp.int32)
    index = lax.axis_index("tensor").astype(jnp.int32)
    z, y = index // NY, index % NY
    place = jnp.stack([core, y, z])

    code = lax.dynamic_slice_in_dim(exits, index * SHARD, SHARD, axis=1)
    depth = jnp.where(code == 1, 1, jnp.where(code == 2, 2, 4))
    back = (layer - jnp.minimum(depth, layer)).reshape(ROWS, 1)

    everyone = jnp.arange(lengths.shape[0], dtype=jnp.int32)
    pair = jnp.arange(HEAD // 2, dtype=jnp.int32).astype(jnp.float32)
    freqs = THETA ** (-(pair * 2.0) / HEAD)

    def tables(planes):
        delta = jnp.array(list(planes), dtype=jnp.int32)
        rows = ((z + NZ - delta) % NZ) * (NY * SHARD) + y * SHARD
        rows = (rows[:, None] + jnp.arange(SHARD, dtype=jnp.int32)[None, :]).reshape(-1)
        mine = jnp.sum(jnp.where(rows[:, None] == everyone[None, :], lengths[None, :], 0), axis=1)
        positions = mine[None, :] + jnp.arange(STEPS, dtype=jnp.int32)[:, None]
        angles = freqs[:, None] * positions.reshape(-1).astype(jnp.float32)[None, :]
        return jnp.cos(angles), jnp.sin(angles)

    own = hidden.reshape(ROWS, DIM)
    moved = []
    for half in range(2):
        mine = own[:, half * HALF : (half + 1) * HALF]
        one = lax.ppermute(mine, "section", [(1, 2), (2, 3)])
        two = lax.ppermute(mine, "section", [(1, 3)])
        moved.append((mine, one, two))
    def half_of(w):
        return lax.dynamic_index_in_dim(w[0], core, axis=0, keepdims=False)

    w_query, w_key, w_value, _ = lax.optimization_barrier((w_query, w_key, w_value, moved[0][0]))
    half = jnp.concatenate([half_of(w_query), half_of(w_key), half_of(w_value)], axis=0)
    weight = lax.all_gather(
        half, ("dp", "tensor"), axis_index_groups=WEIGHT_GROUPS, tiled=True
    )

    low, square = weigh_rows(moved[0], back, norm_gain[:, :HALF], None)
    (high,) = weigh_rows(moved[1], back, norm_gain[:, HALF:], square)

    chains = []
    for half, rows in enumerate((low, high)):
        up, down = [rows], [rows]
        for _ in range(3):
            here = lax.optimization_barrier((up[-1], down[-1]))
            up.append(shift_z(here[0], 1))
            down.append(shift_z(here[1], -1))
        here = lax.optimization_barrier((up[-1], down[-1]))
        last = shift_z(after(here[half], weight) if half else here[half], 1 - 2 * half)
        chains.append(up + [last] + down[:0:-1])

    low, high = chains
    weight, low_near, high_near = fetch(weight, low[:4] + low[5:], high[:4] + high[5:])
    (carried,) = project(place, weight, 0, low_near, low[4])
    outs = project(place, weight, 1, high_near, high[4], (carried, *tables(range(NZ))))
    pieces = [outs[0], shift_y(outs[1], 1), shift_y(outs[2], 2), shift_y(outs[3], -1)]
    return tuple(place_outputs(place, pieces))


def solution(mesh):
    return jax.shard_map(
        on_device,
        mesh=mesh,
        in_specs=(
            P(None, "section", ("dp", "tensor"), None),
            P(None, "dp"),
            P("dp"),
            P("section", None),
            P("section", None, "tensor", None),
            P("section", None, "tensor", None),
            P("section", None, "tensor", None),
        ),
        out_specs=(
            P(None, "section", None, "tensor", "dp"),
            P(None, "section", None, "tensor", "dp"),
            P(None, "section", None, "tensor", "dp"),
        ),
        check_vma=False,
    )
```

time: 451 us -> 126 us (0.28)
  waiting for transfers between devices: 363 us -> 50.5 us
  matrix products: 32.6 us -> 0 us
  starting transfers between devices: 0.42 us -> 32 us
  other arithmetic: 32.9 us -> 2.78 us
  Pallas kernels: 0 us -> 21.2 us
    all_gather x6 -> x1, waiting for transfers between devices: 362 us -> 8.61 us  [on_device(): lax.all_gather(half, ('dp', 'tensor'), axis_index_groups=WEIGHT_GROUPS, t...]
    ppermute x0 -> x21, waiting for transfers between devices: none -> 41.9 us  [the longest x14 36.3 us: shift_z(): return lax.ppermute(value, 'tensor', pairs)]
    dot_general x12 -> x0, matrix products: 32.6 us -> none  [the longest x9 24.7 us: apply_weight(): lax.dot_general(flat, normed, (((1,), (1,)), ((), ())), preferred_element...]
    ppermute x0 -> x21, starting transfers between devices: none -> 32 us  [the longest x14 23.1 us: shift_z(): return lax.ppermute(value, 'tensor', pairs)]
    pallas_call x0 -> x6, Pallas kernels: none -> 21.2 us  [the longest x2 10.2 us: project(): pl.pallas_call(functools.partial(project_kernel, half), out_shape=out_sha...]
    reduce_sum x3 -> x1, other arithmetic: 15.5 us -> 0.18 us  [tables(): jnp.sum(jnp.where(rows[:, None] == everyone[None, :], lengths[None, :], 0...]
    convert_element_type x2 -> x1, other arithmetic: 12.9 us -> 0.01 us  [tables(): angles = freqs[:, None] * positions.reshape(-1).astype(jnp.float32)[None, :]]
  transfers between devices with their start and end apart: 6 -> 22, of which waited for: 6 -> 10; matrix products, arithmetic and copies ran while one was open for 5% -> 1% of each run, Pallas kernels for 0% -> 11%
where the time goes in v1:
time: 126 us; the launch traced here: 125 us
  waiting for transfers between devices  50.5 us (40%)
  starting transfers between devices  32 us (25%)
  Pallas kernels  21.2 us (17%)
  between operations  14.3 us (11%)
  local copies, waits for them, and re-layouts  3.82 us (3%)
  other arithmetic  2.78 us (2%)
    ppermute x14, waiting for transfers between devices, shift_z(): return lax.ppermute(value, 'tensor', pairs)  36.3 us
    ppermute x14, starting transfers between devices, shift_z(): return lax.ppermute(value, 'tensor', pairs)  23.1 us
    pallas_call x2, Pallas kernels, project(): pl.pallas_call(functools.partial(project_kernel, half), out_shape=out_sha...  10.2 us
    all_gather x1, waiting for transfers between devices, on_device(): lax.all_gather(half, ('dp', 'tensor'), axis_index_groups=WEIGHT_GROUPS, t...  8.61 us
    pallas_call x1, Pallas kernels, fetch(): pl.pallas_call(fetch_kernel, out_shape=[jax.ShapeDtypeStruct(shape, jnp.b...  6.23 us
    ppermute x3, waiting for transfers between devices, shift_y(): return lax.ppermute(value, 'tensor', pairs)  5.61 us
    ppermute x3, starting transfers between devices, shift_y(): return lax.ppermute(value, 'tensor', pairs)  3.98 us
    pallas_call x2, Pallas kernels, weigh_rows(): pl.pallas_call(functools.partial(weigh_kernel, first), out_shape=out_shap...  2.95 us
  transfers between devices with their start and end apart: 22, of which 10 were waited for; matrix products, arithmetic and copies ran while one was open for 1% of the time, Pallas kernels for 11%

profile of v1, /device:TPU:1, one launch (start us, length us, event | category | flops | bytes accessed | tf_op | source)
XLA Modules:
  0.0 124.7 jit_solution(15750619312764780705)
XLA Ops:
  7.2 1.3 %fusion.3 = (bf16[48,4096]{1,0:T(8,128)(2,1)S(1)}, bf16[48,4096]{1,0:T(8,128)(2,1)S(1)}) fusion(bf16[48,8192]{1,0:T(8,128)(2,1)} %bitcast.12), kind=kLoop, calls=%fused_computation.19 | loop fusion | bytes 1572864 | tf_op jit(solution)/shard_map/slice | solution.py:308
  9.1 1.0 dynamic-slice_bitcast_fusion.1
  10.1 1.2 %pad_maximum_fusion = bf16[96,8192]{1,0:T(8,128)(2,1)} fusion(bf16[16,8192]{1,0:T(8,128)(2,1)S(1)} %get-tuple-element.63, bf16[16,8192]{1,0:T(8,128)(2,1)S(1)} %get-tuple-element.64, bf16[64,8192]{1,0:T(8,128)(2,1)S(1)} %dynamic-slice_bitcast_fusion), kind=kLoop, calls=%fused_computation | loop fusion | flops 4718592 | bytes 3145728 | tf_op jit(solution)/shard_map/concatenate | solution.py:316
  11.4 1.4 %collective-permute-start = (bf16[48,4096]{1,0:T(8,128)(2,1)S(1)}, bf16[48,4096]{1,0:T(8,128)(2,1)}, u32[]{:S(2)}, u32[]{:S(2)}) collective-permute-start(bf16[48,4096]{1,0:T(8,128)(2,1)S(1)} %get-tuple-element.58.own_ref), channel_id=1, source_target_pairs={{32,64},{64,96},{33,65},{65,97},{34,66},{66,98},{35,67},{67,99},{3... | collective-permute-start | bytes 1179656 | tf_op jit(solution)/shard_map/ppermute | solution.py:309
  12.8 1.4 %collective-permute-start.1 = (bf16[48,4096]{1,0:T(8,128)(2,1)S(1)}, bf16[48,4096]{1,0:T(8,128)(2,1)}, u32[]{:S(2)}, u32[]{:S(2)}) collective-permute-start(bf16[48,4096]{1,0:T(8,128)(2,1)S(1)} %get-tuple-element.58.own_ref), channel_id=1, source_target_pairs={{32,96},{33,97},{34,98},{35,99},{36,100},{37,101},{38,102},{39,103... | collective-permute-start | bytes 1179656 | tf_op jit(solution)/shard_map/ppermute | solution.py:310
  14.9 1.4 %collective-permute-start.9 = (bf16[48,4096]{1,0:T(8,128)(2,1)S(1)}, bf16[48,4096]{1,0:T(8,128)(2,1)}, u32[]{:S(2)}, u32[]{:S(2)}) collective-permute-start(bf16[48,4096]{1,0:T(8,128)(2,1)S(1)} %get-tuple-element.57.own_ref), channel_id=1, source_target_pairs={{32,96},{33,97},{34,98},{35,99},{36,100},{37,101},{38,102},{39,103... | collective-permute-start | bytes 1179656 | tf_op jit(solution)/shard_map/ppermute | solution.py:310
  17.3 1.5 %shard_map.103 = (bf16[48,4096]{1,0:T(8,128)(2,1)S(1)}, f32[48,1]{1,0:T(8,128)S(1)}) custom-call(bf16[48,4096]{1,0:T(8,128)(2,1)S(1)} %get-tuple-element.58.own_ref, bf16[48,4096]{1,0:T(8,128)(2,1)} %collective-permute-done.one_ref, bf16[48,4096]{1,0:T(8,128)(2,1)} %collective-permute-done.1.two_ref, s32[48,1]{1,0:T(8,128)S(1)} %reshape.60.back_ref, ...), custom_call_target="tpu_custom_call" | custom-call | flops 1179648 | bytes 1572864 | tf_op jit(solution)/shard_map/pallas_call | solution.py:119
  18.8 2.5 %collective-permute-start.2 = (bf16[48,4096]{1,0:T(8,128)(2,1)S(1)}, bf16[48,4096]{1,0:T(8,128)(2,1)}, u32[]{:S(2)}, u32[]{:S(2)}) collective-permute-start(bf16[48,4096]{1,0:T(8,128)(2,1)S(1)} %get-tuple-element.35.refs_1_), channel_id=1, source_target_pairs={{0,4},{1,5},{2,6},{3,7},{4,8},{5,9},{6,10},{7,11},{8,12},{9,13},{1... | collective-permute-start | bytes 1179656 | tf_op jit(solution)/shard_map/ppermute | solution.py:39
  21.3 4.0 %collective-permute-start.3 = (bf16[48,4096]{1,0:T(8,128)(2,1)S(1)}, bf16[48,4096]{1,0:T(8,128)(2,1)}, u32[]{:S(2)}, u32[]{:S(2)}) collective-permute-start(bf16[48,4096]{1,0:T(8,128)(2,1)S(1)} %get-tuple-element.35.refs_1_), channel_id=1, source_target_pairs={{0,28},{1,29},{2,30},{3,31},{4,0},{5,1},{6,2},{7,3},{8,4},{9,5},{1... | collective-permute-start | bytes 1179656 | tf_op jit(solution)/shard_map/ppermute | solution.py:39
  25.3 1.5 %shard_map.104.refs_8_ = bf16[48,4224]{1,0:T(8,128)(2,1)S(1)} custom-call(bf16[48,4096]{1,0:T(8,128)(2,1)S(1)} %get-tuple-element.57.own_ref, bf16[48,4096]{1,0:T(8,128)(2,1)S(1)} %collective-permute-done.8.one_ref, bf16[48,4096]{1,0:T(8,128)(2,1)} %collective-permute-done.9.two_ref, s32[48,1]{1,0:T(8,128)S(1)} %reshape.60.back_ref, ...), custom_call_target="tpu_custom_call" | custom-call | flops 1179648 | bytes 1572864 | tf_op jit(solution)/shard_map/pallas_call | solution.py:119
  26.9 2.7 %collective-permute-start.11 = (bf16[48,4224]{1,0:T(8,128)(2,1)S(1)}, bf16[48,4224]{1,0:T(8,128)(2,1)S(1)}, u32[]{:S(2)}, u32[]{:S(2)}) collective-permute-start(bf16[48,4224]{1,0:T(8,128)(2,1)S(1)} %shard_map.104.refs_8_), channel_id=1, source_target_pairs={{0,28},{1,29},{2,30},{3,31},{4,0},{5,1},{6,2},{7,3},{8,4},{9,5},{1... | collective-permute-start | bytes 1216520 | tf_op jit(solution)/shard_map/ppermute | solution.py:39
  29.5 4.6 %collective-permute-done.2.refs_2_ = bf16[48,4096]{1,0:T(8,128)(2,1)} collective-permute-done((bf16[48,4096]{1,0:T(8,128)(2,1)S(1)}, bf16[48,4096]{1,0:T(8,128)(2,1)}, u32[]{:S(2)}, u32[]{:S(2)}) %collective-permute-start.2) | collective-permute-done | bytes 393248 | tf_op jit(solution)/shard_map/ppermute | solution.py:39
  34.1 2.7 %collective-permute-start.5 = (bf16[48,4096]{1,0:T(8,128)(2,1)}, bf16[48,4096]{1,0:T(8,128)(2,1)}, u32[]{:S(2)}, u32[]{:S(2)}) collective-permute-start(bf16[48,4096]{1,0:T(8,128)(2,1)} %collective-permute-done.3.refs_7_), channel_id=1, source_target_pairs={{0,28},{1,29},{2,30},{3,31},{4,0},{5,1},{6,2},{7,3},{8,4},{9,5},{1... | collective-permute-start | bytes 1179656 | tf_op jit(solution)/shard_map/ppermute | solution.py:39
  36.8 6.0 %collective-permute-done.10.refs_9_ = bf16[48,4224]{1,0:T(8,128)(2,1)S(1)} collective-permute-done((bf16[48,4224]{1,0:T(8,128)(2,1)S(1)}, bf16[48,4224]{1,0:T(8,128)(2,1)S(1)}, u32[]{:S(2)}, u32[]{:S(2)}) %collective-permute-start.10) | collective-permute-done | bytes 405536 | tf_op jit(solution)/shard_map/ppermute | solution.py:39
  42.9 2.7 %collective-permute-start.13 = (bf16[48,4224]{1,0:T(8,128)(2,1)S(1)}, bf16[48,4224]{1,0:T(8,128)(2,1)}, u32[]{:S(2)}, u32[]{:S(2)}) collective-permute-start(bf16[48,4224]{1,0:T(8,128)(2,1)S(1)} %collective-permute-done.11.refs_14_), channel_id=1, source_target_pairs={{0,28},{1,29},{2,30},{3,31},{4,0},{5,1},{6,2},{7,3},{8,4},{9,5},{1... | collective-permute-start | bytes 1216520 | tf_op jit(solution)/shard_map/ppermute | solution.py:39
  45.6 5.7 %collective-permute-done.4.refs_3_ = bf16[48,4096]{1,0:T(8,128)(2,1)} collective-permute-done((bf16[48,4096]{1,0:T(8,128)(2,1)}, bf16[48,4096]{1,0:T(8,128)(2,1)}, u32[]{:S(2)}, u32[]{:S(2)}) %collective-permute-start.4) | collective-permute-done | bytes 393248 | tf_op jit(solution)/shard_map/ppermute | solution.py:39
  51.3 2.7 %collective-permute-start.7 = (bf16[48,4096]{1,0:T(8,128)(2,1)}, bf16[48,4096]{1,0:T(8,128)(2,1)}, u32[]{:S(2)}, u32[]{:S(2)}) collective-permute-start(bf16[48,4096]{1,0:T(8,128)(2,1)} %collective-permute-done.5.refs_6_), channel_id=1, source_target_pairs={{0,28},{1,29},{2,30},{3,31},{4,0},{5,1},{6,2},{7,3},{8,4},{9,5},{1... | collective-permute-start | bytes 1179656 | tf_op jit(solution)/shard_map/ppermute | solution.py:39
  54.3 5.7 %collective-permute-done.12.refs_10_ = bf16[48,4224]{1,0:T(8,128)(2,1)} collective-permute-done((bf16[48,4224]{1,0:T(8,128)(2,1)S(1)}, bf16[48,4224]{1,0:T(8,128)(2,1)}, u32[]{:S(2)}, u32[]{:S(2)}) %collective-permute-start.12) | collective-permute-done | bytes 405536 | tf_op jit(solution)/shard_map/ppermute | solution.py:39
  60.0 2.7 %collective-permute-start.15 = (bf16[48,4224]{1,0:T(8,128)(2,1)}, bf16[48,4224]{1,0:T(8,128)(2,1)}, u32[]{:S(2)}, u32[]{:S(2)}) collective-permute-start(bf16[48,4224]{1,0:T(8,128)(2,1)} %collective-permute-done.13.refs_13_), channel_id=1, source_target_pairs={{0,28},{1,29},{2,30},{3,31},{4,0},{5,1},{6,2},{7,3},{8,4},{9,5},{1... | collective-permute-start | bytes 1216520 | tf_op jit(solution)/shard_map/ppermute | solution.py:39
  62.6 5.7 %collective-permute-done.6.refs_4_ = bf16[48,4096]{1,0:T(8,128)(2,1)} collective-permute-done((bf16[48,4096]{1,0:T(8,128)(2,1)}, bf16[48,4096]{1,0:T(8,128)(2,1)}, u32[]{:S(2)}, u32[]{:S(2)}) %collective-permute-start.6) | collective-permute-done | bytes 393248 | tf_op jit(solution)/shard_map/ppermute | solution.py:39
  68.5 8.6 %collective-permute-done.14.refs_11_ = bf16[48,4224]{1,0:T(8,128)(2,1)} collective-permute-done((bf16[48,4224]{1,0:T(8,128)(2,1)}, bf16[48,4224]{1,0:T(8,128)(2,1)}, u32[]{:S(2)}, u32[]{:S(2)}) %collective-permute-start.14) | collective-permute-done | bytes 405536 | tf_op jit(solution)/shard_map/ppermute | solution.py:39
  77.1 8.6 %all-gather.2.cloned.1.call-done.refs_0_ = bf16[768,8192]{1,0:T(8,128)(2,1)} async-done(((bf16[96,8192]{1,0:T(8,128)(2,1)}), bf16[768,8192]{1,0:T(8,128)(2,1)}) %all-gather.2.cloned.1.call-update) | async-done | bytes 12582928 | tf_op jit(solution)/shard_map/all_gather | solution.py:317
  85.7 3.0 %collective-permute-start.16 = (bf16[48,4224]{1,0:T(8,128)(2,1)}, bf16[48,4224]{1,0:T(8,128)(2,1)S(1)}, u32[]{:S(2)}, u32[]{:S(2)}) collective-permute-start(bf16[48,4224]{1,0:T(8,128)(2,1)} %collective-permute-done.15.refs_12_), channel_id=1, source_target_pairs={{0,28},{1,29},{2,30},{3,31},{4,0},{5,1},{6,2},{7,3},{8,4},{9,5},{1... | collective-permute-start | bytes 1216520 | tf_op jit(solution)/shard_map/ppermute | solution.py:39
  89.2 6.2 %shard_map.105 = (bf16[768,8192]{1,0:T(8,128)(2,1)S(1)}, bf16[7,48,4096]{2,1,0:T(8,128)(2,1)S(1)}, bf16[7,48,4224]{2,1,0:T(8,128)(2,1)S(1)}) custom-call(bf16[768,8192]{1,0:T(8,128)(2,1)} %all-gather.2.cloned.1.call-done.refs_0_, bf16[48,4096]{1,0:T(8,128)(2,1)} %copy-done.2, bf16[48,4096]{1,0:T(8,128)(2,1)} %collective-permute-done.2.refs_2_, ...), custom_call_target="tpu_custom_call" | custom-call | bytes 25165824 | tf_op jit(solution)/shard_map/pallas_call | solution.py:73
  95.4 5.0 %shard_map.106.refs_0_ = f32[768,384]{1,0:T(8,128)S(1)} custom-call(s32[3]{0:T(128)S(1)} %pad_add_fusion.place_ref, bf16[768,8192]{1,0:T(8,128)(2,1)S(1)} %get-tuple-element.47.weight_ref, bf16[7,48,4096]{2,1,0:T(8,128)(2,1)S(1)} %get-tuple-element.51.near_ref, bf16[48,4096]{1,0:T(8,128)(2,1)} %collective-permute-done.17.far_ref), custom_call_target="tpu_custom_call" | custom-call | flops 2415919104 | bytes 18874368 | tf_op jit(solution)/shard_map/pallas_call | solution.py:220
  101.1 5.2 %shard_map.107 = (bf16[192,384]{1,0:T(8,128)(2,1)S(1)}, bf16[192,384]{1,0:T(8,128)(2,1)S(1)}, bf16[192,384]{1,0:T(8,128)(2,1)S(1)}, bf16[192,384]{1,0:T(8,128)(2,1)S(1)}) custom-call(s32[3]{0:T(128)S(1)} %pad_add_fusion.place_ref, bf16[768,8192]{1,0:T(8,128)(2,1)S(1)} %get-tuple-element.47.weight_ref, bf16[7,48,4224]{2,1,0:T(8,128)(2,1)S(1)} %get-tuple-element.48.near_ref, ...), custom_call_target="tpu_custom_call" | custom-call | flops 2415919104 | bytes 18874368 | tf_op jit(solution)/shard_map/pallas_call | solution.py:220
  107.1 1.5 %collective-permute-start.19 = (bf16[192,384]{1,0:T(8,128)(2,1)S(1)}, bf16[192,384]{1,0:T(8,128)(2,1)S(1)}, u32[]{:S(2)}, u32[]{:S(2)}) collective-permute-start(bf16[192,384]{1,0:T(8,128)(2,1)S(1)} %get-tuple-element.55), channel_id=1, source_target_pairs={{0,2},{1,3},{2,0},{3,1},{4,6},{5,7},{6,4},{7,5},{8,10},{9,11},{10,... | collective-permute-start | bytes 442376 | tf_op jit(solution)/shard_map/ppermute | solution.py:44
  108.5 1.8 %collective-permute-start.20 = (bf16[192,384]{1,0:T(8,128)(2,1)S(1)}, bf16[192,384]{1,0:T(8,128)(2,1)S(1)}, u32[]{:S(2)}, u32[]{:S(2)}) collective-permute-start(bf16[192,384]{1,0:T(8,128)(2,1)S(1)} %get-tuple-element.56), channel_id=1, source_target_pairs={{0,3},{1,0},{2,1},{3,2},{4,7},{5,4},{6,5},{7,6},{8,11},{9,8},{10,9... | collective-permute-start | bytes 442376 | tf_op jit(solution)/shard_map/ppermute | solution.py:44
  110.4 2.8 %collective-permute-done.18.refs_1_ = bf16[192,384]{1,0:T(8,128)(2,1)S(1)} collective-permute-done((bf16[192,384]{1,0:T(8,128)(2,1)S(1)}, bf16[192,384]{1,0:T(8,128)(2,1)S(1)}, u32[]{:S(2)}, u32[]{:S(2)}) %collective-permute-start.18) | collective-permute-done | bytes 147488 | tf_op jit(solution)/shard_map/ppermute | solution.py:44
  113.2 2.0 %collective-permute-done.19.refs_2_ = bf16[192,384]{1,0:T(8,128)(2,1)S(1)} collective-permute-done((bf16[192,384]{1,0:T(8,128)(2,1)S(1)}, bf16[192,384]{1,0:T(8,128)(2,1)S(1)}, u32[]{:S(2)}, u32[]{:S(2)}) %collective-permute-start.19) | collective-permute-done | bytes 147488 | tf_op jit(solution)/shard_map/ppermute | solution.py:44
  115.1 0.8 collective-permute-done.20.refs_3_
  116.0 1.8 %shard_map.108 = (bf16[3,1,2,16,512]{4,3,2,1,0:T(8,128)(2,1)}, bf16[3,1,2,16,512]{4,3,2,1,0:T(8,128)(2,1)}, bf16[3,1,2,64,512]{4,3,2,1,0:T(8,128)(2,1)}) custom-call(s32[3]{0:T(128)S(1)} %pad_add_fusion.place_ref, bf16[192,384]{1,0:T(8,128)(2,1)S(1)} %get-tuple-element.53.refs_0_, bf16[192,384]{1,0:T(8,128)(2,1)S(1)} %collective-permute-done.18.refs_1_, ...), custom_call_target="tpu_custom_call" | custom-call | tf_op jit(solution)/shard_map/pallas_call | solution.py:264
  (52 shorter events, 4.6 us)
Async XLA Ops:
  7.2 1.8 %copy-start = (bf16[1,2,64,8192]{3,2,1,0:T(8,128)(2,1)S(1)}, bf16[1,2,64,8192]{3,2,1,0:T(8,128)(2,1)}, u32[]{:S(2)}) copy-start(bf16[1,2,64,8192]{3,2,1,0:T(8,128)(2,1)} %param.14) | copy-start | bytes 6291460
  7.2 1.9 %copy-start.6 = (bf16[1,2,16,8192]{3,2,1,0:T(8,128)(2,1)S(1)}, bf16[1,2,16,8192]{3,2,1,0:T(8,128)(2,1)}, u32[]{:S(2)}) copy-start(bf16[1,2,16,8192]{3,2,1,0:T(8,128)(2,1)} %param.13) | copy-start | bytes 1572868
  7.2 78.5 %all-gather.2.cloned.1.call-start = ((), (), s32[]{:S(2)}) async-start(), calls=%async_computation | async-start | bytes 14155776 | tf_op jit(solution)/shard_map/all_gather | solution.py:317
  9.1 7.3 %copy-start.7 = (bf16[1,8192]{1,0:T(2,128)(2,1)S(1)}, bf16[1,8192]{1,0:T(2,128)(2,1)}, u32[]{:S(2)}) copy-start(bf16[1,8192]{1,0:T(2,128)(2,1)} %param.11) | copy-start | bytes 49156
  11.4 42.7 %copy-start.8 = (s32[512]{0:T(512)S(1)}, s32[512]{0:T(512)}, u32[]{:S(2)}) copy-start(s32[512]{0:T(512)} %param.10) | copy-start | bytes 6148
  11.4 5.9 %collective-permute-start = (bf16[48,4096]{1,0:T(8,128)(2,1)S(1)}, bf16[48,4096]{1,0:T(8,128)(2,1)}, u32[]{:S(2)}, u32[]{:S(2)}) collective-permute-start(bf16[48,4096]{1,0:T(8,128)(2,1)S(1)} %get-tuple-element.58.own_ref), channel_id=1, source_target_pairs={{32,64},{64,96},{33,65},{65,97},{34,66},{66,98},{35,67},{67,99},{3... | collective-permute-start | bytes 1179656 | tf_op jit(solution)/shard_map/ppermute | solution.py:309
  12.8 4.5 %collective-permute-start.1 = (bf16[48,4096]{1,0:T(8,128)(2,1)S(1)}, bf16[48,4096]{1,0:T(8,128)(2,1)}, u32[]{:S(2)}, u32[]{:S(2)}) collective-permute-start(bf16[48,4096]{1,0:T(8,128)(2,1)S(1)} %get-tuple-element.58.own_ref), channel_id=1, source_target_pairs={{32,96},{33,97},{34,98},{35,99},{36,100},{37,101},{38,102},{39,103... | collective-permute-start | bytes 1179656 | tf_op jit(solution)/shard_map/ppermute | solution.py:310
  14.2 11.0 %collective-permute-start.8 = (bf16[48,4096]{1,0:T(8,128)(2,1)S(1)}, bf16[48,4096]{1,0:T(8,128)(2,1)S(1)}, u32[]{:S(2)}, u32[]{:S(2)}) collective-permute-start(bf16[48,4096]{1,0:T(8,128)(2,1)S(1)} %get-tuple-element.57.own_ref), channel_id=1, source_target_pairs={{32,64},{64,96},{33,65},{65,97},{34,66},{66,98},{35,67},{67,99},{3... | collective-permute-start | bytes 1179656 | tf_op jit(solution)/shard_map/ppermute | solution.py:309
  14.9 10.4 %collective-permute-start.9 = (bf16[48,4096]{1,0:T(8,128)(2,1)S(1)}, bf16[48,4096]{1,0:T(8,128)(2,1)}, u32[]{:S(2)}, u32[]{:S(2)}) collective-permute-start(bf16[48,4096]{1,0:T(8,128)(2,1)S(1)} %get-tuple-element.57.own_ref), channel_id=1, source_target_pairs={{32,96},{33,97},{34,98},{35,99},{36,100},{37,101},{38,102},{39,103... | collective-permute-start | bytes 1179656 | tf_op jit(solution)/shard_map/ppermute | solution.py:310
  18.8 8.0 %copy-start.2 = (bf16[48,4096]{1,0:T(8,128)(2,1)}, bf16[48,4096]{1,0:T(8,128)(2,1)S(1)}, u32[]{:S(2)}) copy-start(bf16[48,4096]{1,0:T(8,128)(2,1)S(1)} %get-tuple-element.35.refs_1_) | copy-start | bytes 1179652
  18.8 15.4 %collective-permute-start.2 = (bf16[48,4096]{1,0:T(8,128)(2,1)S(1)}, bf16[48,4096]{1,0:T(8,128)(2,1)}, u32[]{:S(2)}, u32[]{:S(2)}) collective-permute-start(bf16[48,4096]{1,0:T(8,128)(2,1)S(1)} %get-tuple-element.35.refs_1_), channel_id=1, source_target_pairs={{0,4},{1,5},{2,6},{3,7},{4,8},{5,9},{6,10},{7,11},{8,12},{9,13},{1... | collective-permute-start | bytes 1179656 | tf_op jit(solution)/shard_map/ppermute | solution.py:39
  21.3 12.9 %collective-permute-start.3 = (bf16[48,4096]{1,0:T(8,128)(2,1)S(1)}, bf16[48,4096]{1,0:T(8,128)(2,1)}, u32[]{:S(2)}, u32[]{:S(2)}) collective-permute-start(bf16[48,4096]{1,0:T(8,128)(2,1)S(1)} %get-tuple-element.35.refs_1_), channel_id=1, source_target_pairs={{0,28},{1,29},{2,30},{3,31},{4,0},{5,1},{6,2},{7,3},{8,4},{9,5},{1... | collective-permute-start | bytes 1179656 | tf_op jit(solution)/shard_map/ppermute | solution.py:39
  26.8 62.4 %copy-start.1 = (bf16[48,4224]{1,0:T(8,128)(2,1)}, bf16[48,4224]{1,0:T(8,128)(2,1)S(1)}, u32[]{:S(2)}) copy-start(bf16[48,4224]{1,0:T(8,128)(2,1)S(1)} %shard_map.104.refs_8_) | copy-start | bytes 1216516
  26.8 16.1 %collective-permute-start.10 = (bf16[48,4224]{1,0:T(8,128)(2,1)S(1)}, bf16[48,4224]{1,0:T(8,128)(2,1)S(1)}, u32[]{:S(2)}, u32[]{:S(2)}) collective-permute-start(bf16[48,4224]{1,0:T(8,128)(2,1)S(1)} %shard_map.104.refs_8_), channel_id=1, source_target_pairs={{0,4},{1,5},{2,6},{3,7},{4,8},{5,9},{6,10},{7,11},{8,12},{9,13},{1... | collective-permute-start | bytes 1216520 | tf_op jit(solution)/shard_map/ppermute | solution.py:39
  26.9 16.0 %collective-permute-start.11 = (bf16[48,4224]{1,0:T(8,128)(2,1)S(1)}, bf16[48,4224]{1,0:T(8,128)(2,1)S(1)}, u32[]{:S(2)}, u32[]{:S(2)}) collective-permute-start(bf16[48,4224]{1,0:T(8,128)(2,1)S(1)} %shard_map.104.refs_8_), channel_id=1, source_target_pairs={{0,28},{1,29},{2,30},{3,31},{4,0},{5,1},{6,2},{7,3},{8,4},{9,5},{1... | collective-permute-start | bytes 1216520 | tf_op jit(solution)/shard_map/ppermute | solution.py:39
  34.1 17.1 %collective-permute-start.4 = (bf16[48,4096]{1,0:T(8,128)(2,1)}, bf16[48,4096]{1,0:T(8,128)(2,1)}, u32[]{:S(2)}, u32[]{:S(2)}) collective-permute-start(bf16[48,4096]{1,0:T(8,128)(2,1)} %collective-permute-done.2.refs_2_), channel_id=1, source_target_pairs={{0,4},{1,5},{2,6},{3,7},{4,8},{5,9},{6,10},{7,11},{8,12},{9,13},{1... | collective-permute-start | bytes 1179656 | tf_op jit(solution)/shard_map/ppermute | solution.py:39
  34.1 17.1 %collective-permute-start.5 = (bf16[48,4096]{1,0:T(8,128)(2,1)}, bf16[48,4096]{1,0:T(8,128)(2,1)}, u32[]{:S(2)}, u32[]{:S(2)}) collective-permute-start(bf16[48,4096]{1,0:T(8,128)(2,1)} %collective-permute-done.3.refs_7_), channel_id=1, source_target_pairs={{0,28},{1,29},{2,30},{3,31},{4,0},{5,1},{6,2},{7,3},{8,4},{9,5},{1... | collective-permute-start | bytes 1179656 | tf_op jit(solution)/shard_map/ppermute | solution.py:39
  42.8 46.3 %copy-start.3 = (bf16[48,4224]{1,0:T(8,128)(2,1)}, bf16[48,4224]{1,0:T(8,128)(2,1)S(1)}, u32[]{:S(2)}) copy-start(bf16[48,4224]{1,0:T(8,128)(2,1)S(1)} %collective-permute-done.10.refs_9_) | copy-start | bytes 1216516
  42.8 46.3 %copy-start.4 = (bf16[48,4224]{1,0:T(8,128)(2,1)}, bf16[48,4224]{1,0:T(8,128)(2,1)S(1)}, u32[]{:S(2)}) copy-start(bf16[48,4224]{1,0:T(8,128)(2,1)S(1)} %collective-permute-done.11.refs_14_) | copy-start | bytes 1216516
  42.8 17.1 %collective-permute-start.12 = (bf16[48,4224]{1,0:T(8,128)(2,1)S(1)}, bf16[48,4224]{1,0:T(8,128)(2,1)}, u32[]{:S(2)}, u32[]{:S(2)}) collective-permute-start(bf16[48,4224]{1,0:T(8,128)(2,1)S(1)} %collective-permute-done.10.refs_9_), channel_id=1, source_target_pairs={{0,4},{1,5},{2,6},{3,7},{4,8},{5,9},{6,10},{7,11},{8,12},{9,13},{1... | collective-permute-start | bytes 1216520 | tf_op jit(solution)/shard_map/ppermute | solution.py:39
  42.9 17.0 %collective-permute-start.13 = (bf16[48,4224]{1,0:T(8,128)(2,1)S(1)}, bf16[48,4224]{1,0:T(8,128)(2,1)}, u32[]{:S(2)}, u32[]{:S(2)}) collective-permute-start(bf16[48,4224]{1,0:T(8,128)(2,1)S(1)} %collective-permute-done.11.refs_14_), channel_id=1, source_target_pairs={{0,28},{1,29},{2,30},{3,31},{4,0},{5,1},{6,2},{7,3},{8,4},{9,5},{1... | collective-permute-start | bytes 1216520 | tf_op jit(solution)/shard_map/ppermute | solution.py:39
  51.3 17.1 %collective-permute-start.6 = (bf16[48,4096]{1,0:T(8,128)(2,1)}, bf16[48,4096]{1,0:T(8,128)(2,1)}, u32[]{:S(2)}, u32[]{:S(2)}) collective-permute-start(bf16[48,4096]{1,0:T(8,128)(2,1)} %collective-permute-done.4.refs_3_), channel_id=1, source_target_pairs={{0,4},{1,5},{2,6},{3,7},{4,8},{5,9},{6,10},{7,11},{8,12},{9,13},{1... | collective-permute-start | bytes 1179656 | tf_op jit(solution)/shard_map/ppermute | solution.py:39
  51.3 17.1 %collective-permute-start.7 = (bf16[48,4096]{1,0:T(8,128)(2,1)}, bf16[48,4096]{1,0:T(8,128)(2,1)}, u32[]{:S(2)}, u32[]{:S(2)}) collective-permute-start(bf16[48,4096]{1,0:T(8,128)(2,1)} %collective-permute-done.5.refs_6_), channel_id=1, source_target_pairs={{0,28},{1,29},{2,30},{3,31},{4,0},{5,1},{6,2},{7,3},{8,4},{9,5},{1... | collective-permute-start | bytes 1179656 | tf_op jit(solution)/shard_map/ppermute | solution.py:39
  59.9 17.1 %collective-permute-start.14 = (bf16[48,4224]{1,0:T(8,128)(2,1)}, bf16[48,4224]{1,0:T(8,128)(2,1)}, u32[]{:S(2)}, u32[]{:S(2)}) collective-permute-start(bf16[48,4224]{1,0:T(8,128)(2,1)} %collective-permute-done.12.refs_10_), channel_id=1, source_target_pairs={{0,4},{1,5},{2,6},{3,7},{4,8},{5,9},{6,10},{7,11},{8,12},{9,13},{1... | collective-permute-start | bytes 1216520 | tf_op jit(solution)/shard_map/ppermute | solution.py:39
  60.0 17.1 %collective-permute-start.15 = (bf16[48,4224]{1,0:T(8,128)(2,1)}, bf16[48,4224]{1,0:T(8,128)(2,1)}, u32[]{:S(2)}, u32[]{:S(2)}) collective-permute-start(bf16[48,4224]{1,0:T(8,128)(2,1)} %collective-permute-done.13.refs_13_), channel_id=1, source_target_pairs={{0,28},{1,29},{2,30},{3,31},{4,0},{5,1},{6,2},{7,3},{8,4},{9,5},{1... | collective-permute-start | bytes 1216520 | tf_op jit(solution)/shard_map/ppermute | solution.py:39
  68.4 27.0 %collective-permute-start.17 = (bf16[48,4096]{1,0:T(8,128)(2,1)}, bf16[48,4096]{1,0:T(8,128)(2,1)}, u32[]{:S(2)}, u32[]{:S(2)}) collective-permute-start(bf16[48,4096]{1,0:T(8,128)(2,1)} %collective-permute-done.6.refs_4_), channel_id=1, source_target_pairs={{0,4},{1,5},{2,6},{3,7},{4,8},{5,9},{6,10},{7,11},{8,12},{9,13},{1... | collective-permute-start | bytes 1179656 | tf_op jit(solution)/shard_map/ppermute | solution.py:39
  85.7 14.7 %collective-permute-start.16 = (bf16[48,4224]{1,0:T(8,128)(2,1)}, bf16[48,4224]{1,0:T(8,128)(2,1)S(1)}, u32[]{:S(2)}, u32[]{:S(2)}) collective-permute-start(bf16[48,4224]{1,0:T(8,128)(2,1)} %collective-permute-done.15.refs_12_), channel_id=1, source_target_pairs={{0,28},{1,29},{2,30},{3,31},{4,0},{5,1},{6,2},{7,3},{8,4},{9,5},{1... | collective-permute-start | bytes 1216520 | tf_op jit(solution)/shard_map/ppermute | solution.py:39
  100.4 0.7 copy-start.5
  106.4 6.8 %collective-permute-start.18 = (bf16[192,384]{1,0:T(8,128)(2,1)S(1)}, bf16[192,384]{1,0:T(8,128)(2,1)S(1)}, u32[]{:S(2)}, u32[]{:S(2)}) collective-permute-start(bf16[192,384]{1,0:T(8,128)(2,1)S(1)} %get-tuple-element.54), channel_id=1, source_target_pairs={{0,1},{1,2},{2,3},{3,0},{4,5},{5,6},{6,7},{7,4},{8,9},{9,10},{10,1... | collective-permute-start | bytes 442376 | tf_op jit(solution)/shard_map/ppermute | solution.py:44
  107.1 8.1 %collective-permute-start.19 = (bf16[192,384]{1,0:T(8,128)(2,1)S(1)}, bf16[192,384]{1,0:T(8,128)(2,1)S(1)}, u32[]{:S(2)}, u32[]{:S(2)}) collective-permute-start(bf16[192,384]{1,0:T(8,128)(2,1)S(1)} %get-tuple-element.55), channel_id=1, source_target_pairs={{0,2},{1,3},{2,0},{3,1},{4,6},{5,7},{6,4},{7,5},{8,10},{9,11},{10,... | collective-permute-start | bytes 442376 | tf_op jit(solution)/shard_map/ppermute | solution.py:44
  108.5 7.5 %collective-permute-start.20 = (bf16[192,384]{1,0:T(8,128)(2,1)S(1)}, bf16[192,384]{1,0:T(8,128)(2,1)S(1)}, u32[]{:S(2)}, u32[]{:S(2)}) collective-permute-start(bf16[192,384]{1,0:T(8,128)(2,1)S(1)} %get-tuple-element.56), channel_id=1, source_target_pairs={{0,3},{1,0},{2,1},{3,2},{4,7},{5,4},{6,5},{7,6},{8,11},{9,8},{10,9... | collective-permute-start | bytes 442376 | tf_op jit(solution)/shard_map/ppermute | solution.py:44
Sparse Core Ops, SparseCore 0:
  11.5 74.1 all-gather.1

commit v2 on v1

v2 whole, which is shorter than its diff:
```python
import functools

import jax
import jax.numpy as jnp
from jax import lax
from jax.experimental import pallas as pl
from jax.experimental.pallas import tpu as pltpu
from jax.sharding import PartitionSpec as P

HEAD = 128
EPS = 1e-05
THETA = 10000.0

STEPS = 3
DIM = 8192
HALF = DIM // 2
SHARD = 16
NZ = 8
NY = 4
KV = 16
Q = 64
SIDE = Q + 2 * KV
COLS = 2 * SIDE
ROWS = STEPS * SHARD
LANES = NZ * SHARD
PARTS = 2
PART = DIM // PARTS
MEBI = 1024 * 1024
VMEM_PROJECT = 16 * MEBI
EXTRA = 128
ORDER = (0, 1, 2, 3, 5, 6, 7, 4)
CHUNK = 512
WEIGHT_GROUPS = [
    [core * NZ * NY + z * NY + y for y in range(NY) for core in range(2)] for z in range(NZ)
]


def shift_z(value, by):
    pairs = [(z * NY + y, ((z + by) % NZ) * NY + y) for z in range(NZ) for y in range(NY)]
    return lax.ppermute(value, "tensor", pairs)


def shift_y(value, by):
    pairs = [(z * NY + y, z * NY + (y + by) % NY) for z in range(NZ) for y in range(NY)]
    return lax.ppermute(value, "tensor", pairs)


def copies(pairs, sems):
    started = []
    for i, (source, target) in enumerate(pairs):
        copy = pltpu.make_async_copy(source, target, sems.at[i])
        copy.start()
        started.append(copy)
    return started


def split_kernel(place_ref, rows_ref, query_ref, key_ref, value_ref, low_ref, high_ref, half_ref):
    k = pl.program_id(0)
    steps = pl.num_programs(0) // 2

    @pl.when(k < steps)
    def _():
        low_ref[...] = rows_ref[...]

    @pl.when(k >= steps)
    def _():
        high_ref[...] = rows_ref[...]

    half_ref[:Q] = query_ref[0, 0]
    half_ref[Q : Q + KV] = key_ref[0, 0]
    half_ref[Q + KV :] = value_ref[0, 0]


def split(place, rows, query, key, value):
    steps = HALF // PART

    def mine(count):
        return pl.BlockSpec((1, 1, count, PART), lambda k, p: (0, p[0], 0, k))

    return pl.pallas_call(
        split_kernel,
        out_shape=[
            jax.ShapeDtypeStruct((ROWS, HALF), jnp.bfloat16),
            jax.ShapeDtypeStruct((ROWS, HALF), jnp.bfloat16),
            jax.ShapeDtypeStruct((SIDE, DIM), jnp.bfloat16),
        ],
        grid_spec=pltpu.PrefetchScalarGridSpec(
            num_scalar_prefetch=1,
            grid=(2 * steps,),
            in_specs=[
                pl.BlockSpec((ROWS, PART), lambda k, p: (0, k)),
                mine(Q),
                mine(KV),
                mine(KV),
            ],
            out_specs=[
                pl.BlockSpec((ROWS, PART), lambda k, p: (0, jnp.minimum(k, steps - 1))),
                pl.BlockSpec((ROWS, PART), lambda k, p: (0, jnp.maximum(k - steps, 0))),
                pl.BlockSpec((SIDE, PART), lambda k, p: (0, k)),
            ],
        ),
        compiler_params=pltpu.CompilerParams(vmem_limit_bytes=16 * MEBI),
        cost_estimate=pl.CostEstimate(
            flops=0, bytes_accessed=4 * (ROWS + SIDE) * DIM, transcendentals=0
        ),
    )(place, *(pltpu.with_memory_space_constraint(x, pltpu.HBM) for x in (rows, query, key, value)))


def weigh_kernel(first, own_ref, one_ref, two_ref, back_ref, gain_ref, *refs):
    out_ref = refs[0] if first else refs[1]
    for t in range(STEPS):
        rows = slice(t * SHARD, (t + 1) * SHARD)
        back = back_ref[rows]
        squares = jnp.zeros((SHARD, CHUNK), jnp.float32)
        for start in range(0, HALF, CHUNK):
            at = slice(start, start + CHUNK)
            own, one, two = (ref[rows, at].astype(jnp.float32) for ref in (own_ref, one_ref, two_ref))
            wide = jnp.where(back == 2, two, jnp.where(back == 1, one, own))
            squares += wide * wide
            out_ref[rows, at] = (wide * gain_ref[:, at].astype(jnp.float32)).astype(jnp.bfloat16)
        square = jnp.sum(squares, axis=-1, keepdims=True)
        if first:
            refs[1][rows] = square
            continue
        rest = lax.rsqrt((refs[0][rows] + square) / DIM + EPS)
        lane = lax.broadcasted_iota(jnp.int32, (SHARD, EXTRA), 1)
        tail = jnp.zeros((SHARD, EXTRA), jnp.float32)
        for i in range(3):
            term = rest.astype(jnp.bfloat16).astype(jnp.float32)
            tail = jnp.where(lane == i, term, tail)
            rest = rest - term
        out_ref[rows, HALF:] = tail.astype(jnp.bfloat16)


def weigh_rows(states, back, gain, earlier):
    whole = pl.BlockSpec(memory_space=pltpu.VMEM)
    first = earlier is None
    out_shape = [jax.ShapeDtypeStruct((ROWS, HALF + (0 if first else EXTRA)), jnp.bfloat16)]
    if first:
        out_shape.append(jax.ShapeDtypeStruct((ROWS, 1), jnp.float32))
    operands = [*states, back, gain] + ([] if first else [earlier])
    return pl.pallas_call(
        functools.partial(weigh_kernel, first),
        out_shape=out_shape,
        in_specs=[whole] * len(operands),
        out_specs=[whole] * len(out_shape),
        compiler_params=pltpu.CompilerParams(vmem_limit_bytes=16 * MEBI),
        cost_estimate=pl.CostEstimate(
            flops=6 * ROWS * HALF, bytes_accessed=8 * ROWS * HALF, transcendentals=0
        ),
    )(*operands)


def ordered(piece):
    rows = []
    for t in range(STEPS):
        at = slice(t * SHARD, (t + 1) * SHARD)
        rows += [piece(i, at) for i in range(NZ)]
    return jnp.concatenate(rows, axis=0)


def times(weight, rows):
    return lax.dot_general(
        weight, rows, (((1,), (1,)), ((), ())), preferred_element_type=jnp.float32
    )


def first_kernel(weight_ref, *refs):
    near = NZ - 1
    low_refs, high_refs = refs[:near], refs[near : 2 * near]
    total, weight_out, high_out, low, sems = refs[2 * near :]
    waiting = []
    for part in range(HALF // PART):
        at = slice(part * PART, (part + 1) * PART)
        pairs = [(weight_ref.at[:, at], weight_out.at[:, at])]
        pairs += [(ref.at[:, at], low.at[i, :, at]) for i, ref in enumerate(low_refs)]
        waiting.append(copies(pairs, sems.at[part]))
    pairs = [(weight_ref.at[:, HALF:], weight_out.at[:, HALF:])]
    pairs += [(ref, high_out.at[i]) for i, ref in enumerate(high_refs)]
    waiting.append(copies(pairs, sems.at[HALF // PART]))
    for part in range(HALF // PART):
        for copy in waiting[part]:
            copy.wait()
        at = slice(part * PART, (part + 1) * PART)
        nothing = jnp.zeros((SHARD, PART), jnp.bfloat16)
        rows = ordered(lambda i, rows: low[i, rows, at] if i < near else nothing)
        product = times(weight_out[:, at], rows)
        if part == 0:
            total[...] = product
        else:
            total[...] += product
    for copy in waiting[-1]:
        copy.wait()


def project_first(weight, low, high):
    near = NZ - 1
    lanes = STEPS * LANES
    operands = [pltpu.with_memory_space_constraint(x, pltpu.HBM) for x in (weight, *low, *high)]
    return pl.pallas_call(
        first_kernel,
        out_shape=[
            jax.ShapeDtypeStruct((NY * COLS, lanes), jnp.float32),
            jax.ShapeDtypeStruct(weight.shape, jnp.bfloat16),
            jax.ShapeDtypeStruct((near, ROWS, HALF + EXTRA), jnp.bfloat16),
        ],
        in_specs=[pl.BlockSpec(memory_space=pltpu.HBM)] * len(operands),
        out_specs=[pl.BlockSpec(memory_space=pltpu.VMEM)] * 3,
        scratch_shapes=[
            pltpu.VMEM((near, ROWS, HALF), jnp.bfloat16),
            pltpu.SemaphoreType.DMA((HALF // PART + 1, NZ)),
        ],
        compiler_params=pltpu.CompilerParams(vmem_limit_bytes=VMEM_PROJECT),
        cost_estimate=pl.CostEstimate(
            flops=2 * NY * COLS * HALF * lanes,
            bytes_accessed=2 * DIM * (NY * COLS + 2 * NZ * ROWS),
            transcendentals=0,
        ),
    )(*operands)


def second_kernel(weight_ref, far_ref, carried_ref, total_ref):
    rows = jnp.concatenate(
        [far_ref[...], jnp.zeros((LANES - ROWS, HALF), jnp.bfloat16)], axis=0
    )
    product = times(weight_ref[:, :HALF], rows)
    lane = lax.broadcasted_iota(jnp.int32, product.shape, 1)
    for t in range(STEPS):
        at = slice(t * LANES, (t + 1) * LANES)
        moved = pltpu.roll(product, LANES - SHARD - t * SHARD, 1)
        total_ref[:, at] = carried_ref[:, at] + jnp.where(lane >= LANES - SHARD, moved, 0.0)


def project_second(weight, far, carried):
    whole = pl.BlockSpec(memory_space=pltpu.VMEM)
    return pl.pallas_call(
        second_kernel,
        out_shape=jax.ShapeDtypeStruct(carried.shape, jnp.float32),
        in_specs=[whole] * 3,
        out_specs=whole,
        compiler_params=pltpu.CompilerParams(vmem_limit_bytes=VMEM_PROJECT),
        cost_estimate=pl.CostEstimate(
            flops=2 * NY * COLS * HALF * LANES,
            bytes_accessed=2 * HALF * NY * COLS,
            transcendentals=0,
        ),
    )(weight, far, carried)


def last_kernel(place_ref, weight_ref, near_ref, far_ref, carried, cos_ref, sin_ref, *refs):
    *outs, total = refs

    def part(first, width):
        at = slice(first, first + width)
        return ordered(
            lambda i, rows: near_ref[i, rows, at] if i < NZ - 1 else far_ref[rows, at]
        )

    for first in range(0, HALF, PART):
        at = HALF + first
        product = times(weight_ref[:, at : at + PART], part(first, PART))
        total[...] = (carried if first == 0 else total)[...] + product
    ones = jnp.where(lax.broadcasted_iota(jnp.int32, (8, EXTRA), 1) < 3, 1.0, 0.0)
    scale = times(ones.astype(jnp.bfloat16), part(HALF, EXTRA))[0:1]
    y = place_ref[1]

    for by in range(NY):
        to = lax.rem(y + by, NY)
        kv_rows = pl.ds(pl.multiple_of(to * KV, KV), KV)
        low = to * COLS
        high = low + SIDE

        def result(base, offset, rows):
            return total[pl.ds(pl.multiple_of(base + offset, KV), rows), :] * scale

        def put(offset, value):
            outs[by][offset : offset + value.shape[0], :] = value.astype(jnp.bfloat16)

        a, b = result(low, Q, KV), result(high, Q, KV)
        cosine, sine = cos_ref[kv_rows, :], sin_ref[kv_rows, :]
        put(0, a * cosine - b * sine)
        put(KV, b * cosine + a * sine)
        put(2 * KV, result(low, Q + KV, KV))
        put(3 * KV, result(high, Q + KV, KV))
        a, b = result(low, 0, Q), result(high, 0, Q)
        cosine, sine = cos_ref[...], sin_ref[...]
        put(4 * KV, a * cosine - b * sine)
        put(4 * KV + Q, b * cosine + a * sine)


def project_last(place, weight, near, far, carried, cosine, sine):
    lanes = STEPS * LANES
    whole = pl.BlockSpec(memory_space=pltpu.VMEM)
    return pl.pallas_call(
        last_kernel,
        out_shape=[jax.ShapeDtypeStruct((COLS, lanes), jnp.bfloat16)] * NY,
        in_specs=[pl.BlockSpec(memory_space=pltpu.SMEM)] + [whole] * 6,
        out_specs=[whole] * NY,
        scratch_shapes=[pltpu.VMEM((NY * COLS, lanes), jnp.float32)],
        compiler_params=pltpu.CompilerParams(vmem_limit_bytes=VMEM_PROJECT),
        cost_estimate=pl.CostEstimate(
            flops=2 * NY * COLS * HALF * lanes,
            bytes_accessed=2 * HALF * (NY * COLS + lanes),
            transcendentals=0,
        ),
    )(place, weight, near, far, carried, cosine, sine)


def chosen_kernel(place_ref, out_ref):
    y, z = place_ref[1], place_ref[2]
    width = NZ * NY * SHARD
    lane = lax.broadcasted_iota(jnp.int32, (LANES, 1), 0)
    column = lax.broadcasted_iota(jnp.int32, (LANES, width), 1)
    group = lane // SHARD
    distance = jnp.zeros((LANES, 1), jnp.int32)
    for i, d in enumerate(ORDER):
        distance = jnp.where(group == i, d, distance)
    plane = lax.rem(z + NZ - distance, NZ)
    for by in range(NY):
        source = lax.rem(y + NY - by, NY)
        at = plane * (NY * SHARD) + source * SHARD + lane % SHARD
        chosen = jnp.where(at == column, 1.0, 0.0).astype(jnp.bfloat16)
        out_ref[by * LANES : (by + 1) * LANES, :] = chosen


def choose_places(place):
    return pl.pallas_call(
        chosen_kernel,
        out_shape=jax.ShapeDtypeStruct((NY * LANES, NZ * NY * SHARD), jnp.bfloat16),
        in_specs=[pl.BlockSpec(memory_space=pltpu.SMEM)],
        out_specs=pl.BlockSpec(memory_space=pltpu.VMEM),
    )(place)


def place_kernel(chosen_ref, *refs):
    pieces, (keys, values, queries) = refs[:NY], refs[NY:]
    width = NZ * NY * SHARD
    for t in range(STEPS):
        lanes = slice(t * LANES, (t + 1) * LANES)
        full = jnp.dot(
            jnp.concatenate([ref[:, lanes] for ref in pieces], axis=1),
            chosen_ref[...],
            preferred_element_type=jnp.float32,
        ).astype(jnp.bfloat16)
        keys[t, 0] = full[: 2 * KV].reshape(2, KV, width)
        values[t, 0] = full[2 * KV : 4 * KV].reshape(2, KV, width)
        queries[t, 0] = full[4 * KV :].reshape(2, Q, width)


def place_outputs(chosen, pieces):
    width = NZ * NY * SHARD
    whole = pl.BlockSpec(memory_space=pltpu.VMEM)
    return pl.pallas_call(
        place_kernel,
        out_shape=[
            jax.ShapeDtypeStruct((STEPS, 1, 2, KV, width), jnp.bfloat16),
            jax.ShapeDtypeStruct((STEPS, 1, 2, KV, width), jnp.bfloat16),
            jax.ShapeDtypeStruct((STEPS, 1, 2, Q, width), jnp.bfloat16),
        ],
        in_specs=[whole] * (1 + len(pieces)),
        out_specs=[whole] * 3,
        compiler_params=pltpu.CompilerParams(vmem_limit_bytes=16 * MEBI),
    )(chosen, *pieces)


def after(value, *earlier):
    return lax.optimization_barrier((value, *earlier))[0]


def on_device(hidden, exits, lengths, norm_gain, w_key, w_value, w_query):
    core = lax.axis_index("dp").astype(jnp.int32)
    layer = lax.axis_index("section").astype(jnp.int32)
    index = lax.axis_index("tensor").astype(jnp.int32)
    z, y = index // NY, index % NY
    place = jnp.stack([core, y, z])

    code = lax.dynamic_slice_in_dim(exits, index * SHARD, SHARD, axis=1)
    depth = jnp.where(code == 1, 1, jnp.where(code == 2, 2, 4))
    back = (layer - jnp.minimum(depth, layer)).reshape(ROWS, 1)

    everyone = jnp.arange(lengths.shape[0], dtype=jnp.int32)
    pair = jnp.arange(HEAD // 2, dtype=jnp.int32).astype(jnp.float32)
    freqs = THETA ** (-(pair * 2.0) / HEAD)

    def tables(planes):
        delta = jnp.array(list(planes), dtype=jnp.int32)
        rows = ((z + NZ - delta) % NZ) * (NY * SHARD) + y * SHARD
        rows = (rows[:, None] + jnp.arange(SHARD, dtype=jnp.int32)[None, :]).reshape(-1)
        mine = jnp.sum(jnp.where(rows[:, None] == everyone[None, :], lengths[None, :], 0), axis=1)
        positions = mine[None, :] + jnp.arange(STEPS, dtype=jnp.int32)[:, None]
        angles = freqs[:, None] * positions.reshape(-1).astype(jnp.float32)[None, :]
        return jnp.cos(angles), jnp.sin(angles)

    *own, half = split(place, hidden.reshape(ROWS, DIM), w_query, w_key, w_value)

    weight = lax.all_gather(
        half, ("dp", "tensor"), axis_index_groups=WEIGHT_GROUPS, tiled=True
    )

    moved = []
    for mine in own:
        two = lax.ppermute(mine, "section", [(1, 3)])
        one = lax.ppermute(mine, "section", [(1, 2), (2, 3)])
        moved.append((mine, one, two))
    low, square = weigh_rows(moved[0], back, norm_gain[:, :HALF], None)
    (high,) = weigh_rows(moved[1], back, norm_gain[:, HALF:], square)

    early = (*tables(ORDER), choose_places(place))
    chains = []
    for half, rows in enumerate((low, high)):
        up, down = [rows], [rows]
        for hop in range(3):
            here = (up[-1], down[-1])
            if half == 1 and hop == 2:
                *here, cosine, sine, chosen = lax.optimization_barrier((*here, *early))
            else:
                here = lax.optimization_barrier(here)
            up.append(shift_z(here[0], 1))
            down.append(shift_z(here[1], -1))
        here = lax.optimization_barrier((up[-1], down[-1]))
        last = shift_z(after(here[half], weight) if half else here[half], 1 - 2 * half)
        chains.append(up + [last] + down[:0:-1])

    low, high = ([chain[d] for d in ORDER] for chain in chains)
    carried, weight, near = project_first(weight, low[:-1], high[:-1])
    carried = project_second(weight, low[-1], carried)
    outs = project_last(place, weight, near, high[-1], carried, cosine, sine)
    pieces = [outs[0], shift_y(outs[1], 1), shift_y(outs[2], 2), shift_y(outs[3], -1)]
    return tuple(place_outputs(chosen, pieces))


def solution(mesh):
    return jax.shard_map(
        on_device,
        mesh=mesh,
        in_specs=(
            P(None, "section", ("dp", "tensor"), None),
            P(None, "dp"),
            P("dp"),
            P("section", None),
            P("section", None, "tensor", None),
            P("section", None, "tensor", None),
            P("section", None, "tensor", None),
        ),
        out_specs=(
            P(None, "section", None, "tensor", "dp"),
            P(None, "section", None, "tensor", "dp"),
            P(None, "section", None, "tensor", "dp"),
        ),
        check_vma=False,
    )
```

time: 126 us -> 120 us (0.952)
  local copies, waits for them, and re-layouts: 3.82 us -> 1.02 us
  starting transfers between devices: 32 us -> 29.9 us
  waiting for transfers between devices: 50.5 us -> 51.8 us
    all_gather x1, waiting for transfers between devices: 8.61 us -> 11.1 us  [on_device(): lax.all_gather(half, ('dp', 'tensor'), axis_index_groups=WEIGHT_GROUPS, t...]
    pallas_call x2, Pallas kernels: 2.95 us -> 0.82 us  [weigh_rows(): pl.pallas_call(functools.partial(weigh_kernel, first), out_shape=out_shap...]
    pallas_call x3 -> x5, Pallas kernels: 16.4 us -> 17.9 us  [the longest x1 7.07 us: project_first(): pl.pallas_call(first_kernel, out_shape=[jax.ShapeDtypeStruct((NY * COLS,...]
    ppermute x2, starting transfers between devices: 2.85 us -> 1.37 us  [on_device(): two = lax.ppermute(mine, 'section', [(1, 3)])]
    slice x2 -> x1, local copies, waits for them, and re-layouts: 1.35 us -> 0.04 us  [on_device(): low, square = weigh_rows(moved[0], back, norm_gain[:, :HALF], None)]
  transfers between devices with their start and end apart: 22 -> 22, of which waited for: 10 -> 10; matrix products, arithmetic and copies ran while one was open for 1% -> 1% of each run, Pallas kernels for 11% -> 10%
where the time goes in v2:
time: 120 us; the launch traced here: 119 us
  waiting for transfers between devices  51.8 us (43%)
  starting transfers between devices  29.9 us (25%)
  Pallas kernels  20 us (17%)
  between operations  14.3 us (12%)
  other arithmetic  1.53 us (1%)
    ppermute x14, waiting for transfers between devices, shift_z(): return lax.ppermute(value, 'tensor', pairs)  35.3 us
    ppermute x14, starting transfers between devices, shift_z(): return lax.ppermute(value, 'tensor', pairs)  23.1 us
    all_gather x1, waiting for transfers between devices, on_device(): lax.all_gather(half, ('dp', 'tensor'), axis_index_groups=WEIGHT_GROUPS, t...  11.1 us
    pallas_call x1, Pallas kernels, project_first(): pl.pallas_call(first_kernel, out_shape=[jax.ShapeDtypeStruct((NY * COLS,...  7.07 us
    ppermute x3, waiting for transfers between devices, shift_y(): return lax.ppermute(value, 'tensor', pairs)  5.33 us
    pallas_call x1, Pallas kernels, project_last(): pl.pallas_call(last_kernel, out_shape=[jax.ShapeDtypeStruct((COLS, lanes)...  4.24 us
    ppermute x3, starting transfers between devices, shift_y(): return lax.ppermute(value, 'tensor', pairs)  3.97 us
    pallas_call x1, Pallas kernels, split(): pl.pallas_call(split_kernel, out_shape=[jax.ShapeDtypeStruct((ROWS, HALF)...  3.09 us
  transfers between devices with their start and end apart: 22, of which 10 were waited for; matrix products, arithmetic and copies ran while one was open for 1% of the time, Pallas kernels for 10%

profile of v2, /device:TPU:1, one launch (start us, length us, event | category | flops | bytes accessed | tf_op | source)
XLA Modules:
  0.0 118.5 jit_solution(1619679553063935156)
XLA Ops:
  7.3 3.1 %shard_map.103 = (bf16[48,4096]{1,0:T(8,128)(2,1)S(1)}, bf16[48,4096]{1,0:T(8,128)(2,1)S(1)}, bf16[96,8192]{1,0:T(8,128)(2,1)}) custom-call(s32[3]{0:T(128)S(1)} %pad_add_fusion.place_ref, bf16[48,8192]{1,0:T(8,128)(2,1)} %bitcast.6, bf16[1,2,64,8192]{3,2,1,0:T(8,128)(2,1)} %query_ref.1, bf16[1,2,16,8192]{3,2,1,0:T(8,128)(2,1)} %key_ref.1, ...), custom_call_target="tpu_custom_call" | custom-call | bytes 4718592 | tf_op jit(solution)/shard_map/pallas_call | solution.py:80
  10.4 0.7 collective-permute-start.2
  11.1 0.7 collective-permute-start.3
  11.8 0.7 collective-permute-start
  12.5 0.7 collective-permute-start.1
  13.3 0.8 minimum_subtract_fusion
  14.5 2.5 %collective-permute-start.8 = (bf16[48,4096]{1,0:T(8,128)(2,1)S(1)}, bf16[48,4096]{1,0:T(8,128)(2,1)}, u32[]{:S(2)}, u32[]{:S(2)}) collective-permute-start(bf16[48,4096]{1,0:T(8,128)(2,1)S(1)} %get-tuple-element.44.refs_0_), channel_id=1, source_target_pairs={{0,4},{1,5},{2,6},{3,7},{4,8},{5,9},{6,10},{7,11},{8,12},{9,13},{1... | collective-permute-start | bytes 1179656 | tf_op jit(solution)/shard_map/ppermute | solution.py:40
  17.0 4.0 %collective-permute-start.9 = (bf16[48,4096]{1,0:T(8,128)(2,1)S(1)}, bf16[48,4096]{1,0:T(8,128)(2,1)}, u32[]{:S(2)}, u32[]{:S(2)}) collective-permute-start(bf16[48,4096]{1,0:T(8,128)(2,1)S(1)} %get-tuple-element.44.refs_0_), channel_id=1, source_target_pairs={{0,28},{1,29},{2,30},{3,31},{4,0},{5,1},{6,2},{7,3},{8,4},{9,5},{1... | collective-permute-start | bytes 1179656 | tf_op jit(solution)/shard_map/ppermute | solution.py:40
  21.6 2.7 %collective-permute-start.5 = (bf16[48,4224]{1,0:T(8,128)(2,1)S(1)}, bf16[48,4224]{1,0:T(8,128)(2,1)S(1)}, u32[]{:S(2)}, u32[]{:S(2)}) collective-permute-start(bf16[48,4224]{1,0:T(8,128)(2,1)S(1)} %shard_map.105.refs_7_), channel_id=1, source_target_pairs={{0,28},{1,29},{2,30},{3,31},{4,0},{5,1},{6,2},{7,3},{8,4},{9,5},{1... | collective-permute-start | bytes 1216520 | tf_op jit(solution)/shard_map/ppermute | solution.py:40
  24.4 5.5 %collective-permute-done.8.refs_1_ = bf16[48,4096]{1,0:T(8,128)(2,1)} collective-permute-done((bf16[48,4096]{1,0:T(8,128)(2,1)S(1)}, bf16[48,4096]{1,0:T(8,128)(2,1)}, u32[]{:S(2)}, u32[]{:S(2)}) %collective-permute-start.8) | collective-permute-done | bytes 393248 | tf_op jit(solution)/shard_map/ppermute | solution.py:40
  29.9 2.7 %collective-permute-start.11 = (bf16[48,4096]{1,0:T(8,128)(2,1)}, bf16[48,4096]{1,0:T(8,128)(2,1)}, u32[]{:S(2)}, u32[]{:S(2)}) collective-permute-start(bf16[48,4096]{1,0:T(8,128)(2,1)} %collective-permute-done.9.refs_6_), channel_id=1, source_target_pairs={{0,28},{1,29},{2,30},{3,31},{4,0},{5,1},{6,2},{7,3},{8,4},{9,5},{1... | collective-permute-start | bytes 1179656 | tf_op jit(solution)/shard_map/ppermute | solution.py:40
  32.9 5.7 %collective-permute-done.4.refs_8_ = bf16[48,4224]{1,0:T(8,128)(2,1)S(1)} collective-permute-done((bf16[48,4224]{1,0:T(8,128)(2,1)S(1)}, bf16[48,4224]{1,0:T(8,128)(2,1)S(1)}, u32[]{:S(2)}, u32[]{:S(2)}) %collective-permute-start.4) | collective-permute-done | bytes 405536 | tf_op jit(solution)/shard_map/ppermute | solution.py:40
  38.7 2.7 %collective-permute-start.7 = (bf16[48,4224]{1,0:T(8,128)(2,1)S(1)}, bf16[48,4224]{1,0:T(8,128)(2,1)S(1)}, u32[]{:S(2)}, u32[]{:S(2)}) collective-permute-start(bf16[48,4224]{1,0:T(8,128)(2,1)S(1)} %collective-permute-done.5.refs_13_), channel_id=1, source_target_pairs={{0,28},{1,29},{2,30},{3,31},{4,0},{5,1},{6,2},{7,3},{8,4},{9,5},{1... | collective-permute-start | bytes 1216520 | tf_op jit(solution)/shard_map/ppermute | solution.py:40
  41.4 5.7 %collective-permute-done.10.refs_2_ = bf16[48,4096]{1,0:T(8,128)(2,1)S(1)} collective-permute-done((bf16[48,4096]{1,0:T(8,128)(2,1)}, bf16[48,4096]{1,0:T(8,128)(2,1)S(1)}, u32[]{:S(2)}, u32[]{:S(2)}) %collective-permute-start.10) | collective-permute-done | bytes 393248 | tf_op jit(solution)/shard_map/ppermute | solution.py:40
  47.0 2.7 %collective-permute-start.13 = (bf16[48,4096]{1,0:T(8,128)(2,1)}, bf16[48,4096]{1,0:T(8,128)(2,1)}, u32[]{:S(2)}, u32[]{:S(2)}) collective-permute-start(bf16[48,4096]{1,0:T(8,128)(2,1)} %collective-permute-done.11.refs_5_), channel_id=1, source_target_pairs={{0,28},{1,29},{2,30},{3,31},{4,0},{5,1},{6,2},{7,3},{8,4},{9,5},{1... | collective-permute-start | bytes 1179656 | tf_op jit(solution)/shard_map/ppermute | solution.py:40
  50.1 1.6 %shard_map.106.chosen_ref = bf16[512,512]{1,0:T(8,128)(2,1)} custom-call(s32[3]{0:T(128)} %copy-done.3), custom_call_target="tpu_custom_call" | custom-call | tf_op jit(solution)/shard_map/pallas_call | solution.py:327
  51.7 4.0 %collective-permute-done.6.refs_9_ = bf16[48,4224]{1,0:T(8,128)(2,1)S(1)} collective-permute-done((bf16[48,4224]{1,0:T(8,128)(2,1)S(1)}, bf16[48,4224]{1,0:T(8,128)(2,1)S(1)}, u32[]{:S(2)}, u32[]{:S(2)}) %collective-permute-start.6) | collective-permute-done | bytes 405536 | tf_op jit(solution)/shard_map/ppermute | solution.py:40
  55.8 2.7 %collective-permute-start.15 = (bf16[48,4224]{1,0:T(8,128)(2,1)S(1)}, bf16[48,4224]{1,0:T(8,128)(2,1)}, u32[]{:S(2)}, u32[]{:S(2)}) collective-permute-start(bf16[48,4224]{1,0:T(8,128)(2,1)S(1)} %collective-permute-done.7.refs_12_), channel_id=1, source_target_pairs={{0,28},{1,29},{2,30},{3,31},{4,0},{5,1},{6,2},{7,3},{8,4},{9,5},{1... | collective-permute-start | bytes 1216520 | tf_op jit(solution)/shard_map/ppermute | solution.py:40
  58.5 5.7 %collective-permute-done.12.refs_3_ = bf16[48,4096]{1,0:T(8,128)(2,1)} collective-permute-done((bf16[48,4096]{1,0:T(8,128)(2,1)S(1)}, bf16[48,4096]{1,0:T(8,128)(2,1)}, u32[]{:S(2)}, u32[]{:S(2)}) %collective-permute-start.12) | collective-permute-done | bytes 393248 | tf_op jit(solution)/shard_map/ppermute | solution.py:40
  64.2 8.7 %collective-permute-done.14.refs_10_ = bf16[48,4224]{1,0:T(8,128)(2,1)S(1)} collective-permute-done((bf16[48,4224]{1,0:T(8,128)(2,1)S(1)}, bf16[48,4224]{1,0:T(8,128)(2,1)S(1)}, u32[]{:S(2)}, u32[]{:S(2)}) %collective-permute-start.14) | collective-permute-done | bytes 405536 | tf_op jit(solution)/shard_map/ppermute | solution.py:40
  72.8 0.8 copy-done.9
  73.6 11.1 %all-gather.2.cloned.1.call-done.weight_ref = bf16[768,8192]{1,0:T(8,128)(2,1)} async-done(((bf16[96,8192]{1,0:T(8,128)(2,1)}), bf16[768,8192]{1,0:T(8,128)(2,1)}) %all-gather.2.cloned.1.call-update) | async-done | bytes 12582928 | tf_op jit(solution)/shard_map/all_gather | solution.py:396
  84.7 3.0 %collective-permute-start.16 = (bf16[48,4224]{1,0:T(8,128)(2,1)}, bf16[48,4224]{1,0:T(8,128)(2,1)S(1)}, u32[]{:S(2)}, u32[]{:S(2)}) collective-permute-start(bf16[48,4224]{1,0:T(8,128)(2,1)} %collective-permute-done.15.refs_11_), channel_id=1, source_target_pairs={{0,28},{1,29},{2,30},{3,31},{4,0},{5,1},{6,2},{7,3},{8,4},{9,5},{1... | collective-permute-start | bytes 1216520 | tf_op jit(solution)/shard_map/ppermute | solution.py:40
  87.8 7.1 %shard_map.107 = (f32[768,384]{1,0:T(8,128)S(1)}, bf16[768,8192]{1,0:T(8,128)(2,1)S(1)}, bf16[7,48,4224]{2,1,0:T(8,128)(2,1)S(1)}) custom-call(bf16[768,8192]{1,0:T(8,128)(2,1)} %all-gather.2.cloned.1.call-done.weight_ref, bf16[48,4096]{1,0:T(8,128)(2,1)} %copy-done.2, bf16[48,4096]{1,0:T(8,128)(2,1)} %collective-permute-done.8.refs_1_, ...), custom_call_target="tpu_custom_call" | custom-call | flops 2415919104 | bytes 25165824 | tf_op jit(solution)/shard_map/pallas_call | solution.py:200
  94.9 1.9 %shard_map.108.carried = f32[768,384]{1,0:T(8,128)S(1)} custom-call(bf16[768,8192]{1,0:T(8,128)(2,1)S(1)} %get-tuple-element.51.weight_ref, bf16[48,4096]{1,0:T(8,128)(2,1)S(1)} %collective-permute-done.17.far_ref, f32[768,384]{1,0:T(8,128)S(1)} %get-tuple-element.56.carried_ref), custom_call_target="tpu_custom_call" | custom-call | flops 805306368 | bytes 6291456 | tf_op jit(solution)/shard_map/pallas_call | solution.py:236
  96.9 4.2 %shard_map.109 = (bf16[192,384]{1,0:T(8,128)(2,1)S(1)}, bf16[192,384]{1,0:T(8,128)(2,1)S(1)}, bf16[192,384]{1,0:T(8,128)(2,1)S(1)}, bf16[192,384]{1,0:T(8,128)(2,1)S(1)}) custom-call(s32[3]{0:T(128)S(1)} %copy-done.4, bf16[768,8192]{1,0:T(8,128)(2,1)S(1)} %get-tuple-element.51.weight_ref, bf16[7,48,4224]{2,1,0:T(8,128)(2,1)S(1)} %get-tuple-element.52.near_ref, ...), custom_call_target="tpu_custom_call" | custom-call | flops 2415919104 | bytes 9437184 | tf_op jit(solution)/shard_map/pallas_call | solution.py:294
  101.8 1.5 %collective-permute-start.19 = (bf16[192,384]{1,0:T(8,128)(2,1)S(1)}, bf16[192,384]{1,0:T(8,128)(2,1)S(1)}, u32[]{:S(2)}, u32[]{:S(2)}) collective-permute-start(bf16[192,384]{1,0:T(8,128)(2,1)S(1)} %get-tuple-element.61), channel_id=1, source_target_pairs={{0,2},{1,3},{2,0},{3,1},{4,6},{5,7},{6,4},{7,5},{8,10},{9,11},{10,... | collective-permute-start | bytes 442376 | tf_op jit(solution)/shard_map/ppermute | solution.py:45
  103.3 1.8 %collective-permute-start.20 = (bf16[192,384]{1,0:T(8,128)(2,1)S(1)}, bf16[192,384]{1,0:T(8,128)(2,1)S(1)}, u32[]{:S(2)}, u32[]{:S(2)}) collective-permute-start(bf16[192,384]{1,0:T(8,128)(2,1)S(1)} %get-tuple-element.62), channel_id=1, source_target_pairs={{0,3},{1,0},{2,1},{3,2},{4,7},{5,4},{6,5},{7,6},{8,11},{9,8},{10,9... | collective-permute-start | bytes 442376 | tf_op jit(solution)/shard_map/ppermute | solution.py:45
  105.1 2.5 %collective-permute-done.18.refs_1_ = bf16[192,384]{1,0:T(8,128)(2,1)S(1)} collective-permute-done((bf16[192,384]{1,0:T(8,128)(2,1)S(1)}, bf16[192,384]{1,0:T(8,128)(2,1)S(1)}, u32[]{:S(2)}, u32[]{:S(2)}) %collective-permute-start.18) | collective-permute-done | bytes 147488 | tf_op jit(solution)/shard_map/ppermute | solution.py:45
  107.6 1.9 %collective-permute-done.19.refs_2_ = bf16[192,384]{1,0:T(8,128)(2,1)S(1)} collective-permute-done((bf16[192,384]{1,0:T(8,128)(2,1)S(1)}, bf16[192,384]{1,0:T(8,128)(2,1)S(1)}, u32[]{:S(2)}, u32[]{:S(2)}) %collective-permute-start.19) | collective-permute-done | bytes 147488 | tf_op jit(solution)/shard_map/ppermute | solution.py:45
  109.5 0.9 collective-permute-done.20.refs_3_
  110.4 1.2 %shard_map.110 = (bf16[3,1,2,16,512]{4,3,2,1,0:T(8,128)(2,1)}, bf16[3,1,2,16,512]{4,3,2,1,0:T(8,128)(2,1)}, bf16[3,1,2,64,512]{4,3,2,1,0:T(8,128)(2,1)}) custom-call(bf16[512,512]{1,0:T(8,128)(2,1)S(1)} %copy-done, bf16[192,384]{1,0:T(8,128)(2,1)S(1)} %get-tuple-element.59.refs_0_, bf16[192,384]{1,0:T(8,128)(2,1)S(1)} %collective-permute-done.18.refs_1_, ...), custom_call_target="tpu_custom_call" | custom-call | tf_op jit(solution)/shard_map/pallas_call | solution.py:353
  (60 shorter events, 2.8 us)
Async XLA Ops:
  7.2 77.6 %all-gather.2.cloned.1.call-start = ((), (), s32[]{:S(2)}) async-start(), calls=%async_computation | async-start | bytes 14155776 | tf_op jit(solution)/shard_map/all_gather | solution.py:396
  10.4 10.6 %copy-start.13 = (s32[8]{0:T(128)S(1)}, s32[8]{0:T(128)}, u32[]{:S(2)}) copy-start(s32[8]{0:T(128)} %constant.81) | copy-start | bytes 100
  10.4 22.3 %copy-start.12 = (s32[512]{0:T(512)S(1)}, s32[512]{0:T(512)}, u32[]{:S(2)}) copy-start(s32[512]{0:T(512)} %param.10) | copy-start | bytes 6148
  10.4 3.7 %collective-permute-start.2 = (bf16[48,4096]{1,0:T(8,128)(2,1)S(1)}, bf16[48,4096]{1,0:T(8,128)(2,1)S(1)}, u32[]{:S(2)}, u32[]{:S(2)}) collective-permute-start(bf16[48,4096]{1,0:T(8,128)(2,1)S(1)} %get-tuple-element.34.own_ref), channel_id=1, source_target_pairs={{32,64},{64,96},{33,65},{65,97},{34,66},{66,98},{35,67},{67,99},{3... | collective-permute-start | bytes 1179656 | tf_op jit(solution)/shard_map/ppermute | solution.py:403
  11.1 3.0 %collective-permute-start.3 = (bf16[48,4096]{1,0:T(8,128)(2,1)S(1)}, bf16[48,4096]{1,0:T(8,128)(2,1)S(1)}, u32[]{:S(2)}, u32[]{:S(2)}) collective-permute-start(bf16[48,4096]{1,0:T(8,128)(2,1)S(1)} %get-tuple-element.34.own_ref), channel_id=1, source_target_pairs={{32,96},{33,97},{34,98},{35,99},{36,100},{37,101},{38,102},{39,103... | collective-permute-start | bytes 1179656 | tf_op jit(solution)/shard_map/ppermute | solution.py:402
  11.8 9.2 %collective-permute-start = (bf16[48,4096]{1,0:T(8,128)(2,1)S(1)}, bf16[48,4096]{1,0:T(8,128)(2,1)S(1)}, u32[]{:S(2)}, u32[]{:S(2)}) collective-permute-start(bf16[48,4096]{1,0:T(8,128)(2,1)S(1)} %get-tuple-element.33.own_ref), channel_id=1, source_target_pairs={{32,64},{64,96},{33,65},{65,97},{34,66},{66,98},{35,67},{67,99},{3... | collective-permute-start | bytes 1179656 | tf_op jit(solution)/shard_map/ppermute | solution.py:403
  12.5 8.5 %collective-permute-start.1 = (bf16[48,4096]{1,0:T(8,128)(2,1)S(1)}, bf16[48,4096]{1,0:T(8,128)(2,1)S(1)}, u32[]{:S(2)}, u32[]{:S(2)}) collective-permute-start(bf16[48,4096]{1,0:T(8,128)(2,1)S(1)} %get-tuple-element.33.own_ref), channel_id=1, source_target_pairs={{32,96},{33,97},{34,98},{35,99},{36,100},{37,101},{38,102},{39,103... | collective-permute-start | bytes 1179656 | tf_op jit(solution)/shard_map/ppermute | solution.py:402
  14.5 73.2 %copy-start.2 = (bf16[48,4096]{1,0:T(8,128)(2,1)}, bf16[48,4096]{1,0:T(8,128)(2,1)S(1)}, u32[]{:S(2)}) copy-start(bf16[48,4096]{1,0:T(8,128)(2,1)S(1)} %get-tuple-element.44.refs_0_) | copy-start | bytes 1179652
  14.5 15.4 %collective-permute-start.8 = (bf16[48,4096]{1,0:T(8,128)(2,1)S(1)}, bf16[48,4096]{1,0:T(8,128)(2,1)}, u32[]{:S(2)}, u32[]{:S(2)}) collective-permute-start(bf16[48,4096]{1,0:T(8,128)(2,1)S(1)} %get-tuple-element.44.refs_0_), channel_id=1, source_target_pairs={{0,4},{1,5},{2,6},{3,7},{4,8},{5,9},{6,10},{7,11},{8,12},{9,13},{1... | collective-permute-start | bytes 1179656 | tf_op jit(solution)/shard_map/ppermute | solution.py:40
  17.0 12.9 %collective-permute-start.9 = (bf16[48,4096]{1,0:T(8,128)(2,1)S(1)}, bf16[48,4096]{1,0:T(8,128)(2,1)}, u32[]{:S(2)}, u32[]{:S(2)}) collective-permute-start(bf16[48,4096]{1,0:T(8,128)(2,1)S(1)} %get-tuple-element.44.refs_0_), channel_id=1, source_target_pairs={{0,28},{1,29},{2,30},{3,31},{4,0},{5,1},{6,2},{7,3},{8,4},{9,5},{1... | collective-permute-start | bytes 1179656 | tf_op jit(solution)/shard_map/ppermute | solution.py:40
  21.5 66.2 %copy-start.1 = (bf16[48,4224]{1,0:T(8,128)(2,1)}, bf16[48,4224]{1,0:T(8,128)(2,1)S(1)}, u32[]{:S(2)}) copy-start(bf16[48,4224]{1,0:T(8,128)(2,1)S(1)} %shard_map.105.refs_7_) | copy-start | bytes 1216516
  21.5 17.0 %collective-permute-start.4 = (bf16[48,4224]{1,0:T(8,128)(2,1)S(1)}, bf16[48,4224]{1,0:T(8,128)(2,1)S(1)}, u32[]{:S(2)}, u32[]{:S(2)}) collective-permute-start(bf16[48,4224]{1,0:T(8,128)(2,1)S(1)} %shard_map.105.refs_7_), channel_id=1, source_target_pairs={{0,4},{1,5},{2,6},{3,7},{4,8},{5,9},{6,10},{7,11},{8,12},{9,13},{1... | collective-permute-start | bytes 1216520 | tf_op jit(solution)/shard_map/ppermute | solution.py:40
  21.6 17.0 %collective-permute-start.5 = (bf16[48,4224]{1,0:T(8,128)(2,1)S(1)}, bf16[48,4224]{1,0:T(8,128)(2,1)S(1)}, u32[]{:S(2)}, u32[]{:S(2)}) collective-permute-start(bf16[48,4224]{1,0:T(8,128)(2,1)S(1)} %shard_map.105.refs_7_), channel_id=1, source_target_pairs={{0,28},{1,29},{2,30},{3,31},{4,0},{5,1},{6,2},{7,3},{8,4},{9,5},{1... | collective-permute-start | bytes 1216520 | tf_op jit(solution)/shard_map/ppermute | solution.py:40
  29.9 17.1 %collective-permute-start.10 = (bf16[48,4096]{1,0:T(8,128)(2,1)}, bf16[48,4096]{1,0:T(8,128)(2,1)S(1)}, u32[]{:S(2)}, u32[]{:S(2)}) collective-permute-start(bf16[48,4096]{1,0:T(8,128)(2,1)} %collective-permute-done.8.refs_1_), channel_id=1, source_target_pairs={{0,4},{1,5},{2,6},{3,7},{4,8},{5,9},{6,10},{7,11},{8,12},{9,13},{1... | collective-permute-start | bytes 1179656 | tf_op jit(solution)/shard_map/ppermute | solution.py:40
  29.9 17.1 %collective-permute-start.11 = (bf16[48,4096]{1,0:T(8,128)(2,1)}, bf16[48,4096]{1,0:T(8,128)(2,1)}, u32[]{:S(2)}, u32[]{:S(2)}) collective-permute-start(bf16[48,4096]{1,0:T(8,128)(2,1)} %collective-permute-done.9.refs_6_), channel_id=1, source_target_pairs={{0,28},{1,29},{2,30},{3,31},{4,0},{5,1},{6,2},{7,3},{8,4},{9,5},{1... | collective-permute-start | bytes 1179656 | tf_op jit(solution)/shard_map/ppermute | solution.py:40
  38.6 49.2 %copy-start.5 = (bf16[48,4224]{1,0:T(8,128)(2,1)}, bf16[48,4224]{1,0:T(8,128)(2,1)S(1)}, u32[]{:S(2)}) copy-start(bf16[48,4224]{1,0:T(8,128)(2,1)S(1)} %collective-permute-done.4.refs_8_) | copy-start | bytes 1216516
  38.6 49.2 %copy-start.6 = (bf16[48,4224]{1,0:T(8,128)(2,1)}, bf16[48,4224]{1,0:T(8,128)(2,1)S(1)}, u32[]{:S(2)}) copy-start(bf16[48,4224]{1,0:T(8,128)(2,1)S(1)} %collective-permute-done.5.refs_13_) | copy-start | bytes 1216516
  38.6 17.1 %collective-permute-start.6 = (bf16[48,4224]{1,0:T(8,128)(2,1)S(1)}, bf16[48,4224]{1,0:T(8,128)(2,1)S(1)}, u32[]{:S(2)}, u32[]{:S(2)}) collective-permute-start(bf16[48,4224]{1,0:T(8,128)(2,1)S(1)} %collective-permute-done.4.refs_8_), channel_id=1, source_target_pairs={{0,4},{1,5},{2,6},{3,7},{4,8},{5,9},{6,10},{7,11},{8,12},{9,13},{1... | collective-permute-start | bytes 1216520 | tf_op jit(solution)/shard_map/ppermute | solution.py:40
  38.7 17.0 %collective-permute-start.7 = (bf16[48,4224]{1,0:T(8,128)(2,1)S(1)}, bf16[48,4224]{1,0:T(8,128)(2,1)S(1)}, u32[]{:S(2)}, u32[]{:S(2)}) collective-permute-start(bf16[48,4224]{1,0:T(8,128)(2,1)S(1)} %collective-permute-done.5.refs_13_), channel_id=1, source_target_pairs={{0,28},{1,29},{2,30},{3,31},{4,0},{5,1},{6,2},{7,3},{8,4},{9,5},{1... | collective-permute-start | bytes 1216520 | tf_op jit(solution)/shard_map/ppermute | solution.py:40
  47.0 17.1 %copy-start.10 = (bf16[48,4096]{1,0:T(8,128)(2,1)}, bf16[48,4096]{1,0:T(8,128)(2,1)S(1)}, u32[]{:S(2)}) copy-start(bf16[48,4096]{1,0:T(8,128)(2,1)S(1)} %collective-permute-done.10.refs_2_) | copy-start | bytes 1179652
  47.0 17.1 %collective-permute-start.12 = (bf16[48,4096]{1,0:T(8,128)(2,1)S(1)}, bf16[48,4096]{1,0:T(8,128)(2,1)}, u32[]{:S(2)}, u32[]{:S(2)}) collective-permute-start(bf16[48,4096]{1,0:T(8,128)(2,1)S(1)} %collective-permute-done.10.refs_2_), channel_id=1, source_target_pairs={{0,4},{1,5},{2,6},{3,7},{4,8},{5,9},{6,10},{7,11},{8,12},{9,13},{1... | collective-permute-start | bytes 1179656 | tf_op jit(solution)/shard_map/ppermute | solution.py:40
  47.0 17.1 %collective-permute-start.13 = (bf16[48,4096]{1,0:T(8,128)(2,1)}, bf16[48,4096]{1,0:T(8,128)(2,1)}, u32[]{:S(2)}, u32[]{:S(2)}) collective-permute-start(bf16[48,4096]{1,0:T(8,128)(2,1)} %collective-permute-done.11.refs_5_), channel_id=1, source_target_pairs={{0,28},{1,29},{2,30},{3,31},{4,0},{5,1},{6,2},{7,3},{8,4},{9,5},{1... | collective-permute-start | bytes 1179656 | tf_op jit(solution)/shard_map/ppermute | solution.py:40
  55.7 32.1 %copy-start.7 = (bf16[48,4224]{1,0:T(8,128)(2,1)}, bf16[48,4224]{1,0:T(8,128)(2,1)S(1)}, u32[]{:S(2)}) copy-start(bf16[48,4224]{1,0:T(8,128)(2,1)S(1)} %collective-permute-done.6.refs_9_) | copy-start | bytes 1216516
  55.7 32.1 %copy-start.8 = (bf16[48,4224]{1,0:T(8,128)(2,1)}, bf16[48,4224]{1,0:T(8,128)(2,1)S(1)}, u32[]{:S(2)}) copy-start(bf16[48,4224]{1,0:T(8,128)(2,1)S(1)} %collective-permute-done.7.refs_12_) | copy-start | bytes 1216516
  55.7 17.1 %collective-permute-start.14 = (bf16[48,4224]{1,0:T(8,128)(2,1)S(1)}, bf16[48,4224]{1,0:T(8,128)(2,1)S(1)}, u32[]{:S(2)}, u32[]{:S(2)}) collective-permute-start(bf16[48,4224]{1,0:T(8,128)(2,1)S(1)} %collective-permute-done.6.refs_9_), channel_id=1, source_target_pairs={{0,4},{1,5},{2,6},{3,7},{4,8},{5,9},{6,10},{7,11},{8,12},{9,13},{1... | collective-permute-start | bytes 1216520 | tf_op jit(solution)/shard_map/ppermute | solution.py:40
  55.8 17.8 %collective-permute-start.15 = (bf16[48,4224]{1,0:T(8,128)(2,1)S(1)}, bf16[48,4224]{1,0:T(8,128)(2,1)}, u32[]{:S(2)}, u32[]{:S(2)}) collective-permute-start(bf16[48,4224]{1,0:T(8,128)(2,1)S(1)} %collective-permute-done.7.refs_12_), channel_id=1, source_target_pairs={{0,28},{1,29},{2,30},{3,31},{4,0},{5,1},{6,2},{7,3},{8,4},{9,5},{1... | collective-permute-start | bytes 1216520 | tf_op jit(solution)/shard_map/ppermute | solution.py:40
  64.1 30.7 %collective-permute-start.17 = (bf16[48,4096]{1,0:T(8,128)(2,1)}, bf16[48,4096]{1,0:T(8,128)(2,1)S(1)}, u32[]{:S(2)}, u32[]{:S(2)}) collective-permute-start(bf16[48,4096]{1,0:T(8,128)(2,1)} %collective-permute-done.12.refs_3_), channel_id=1, source_target_pairs={{0,4},{1,5},{2,6},{3,7},{4,8},{5,9},{6,10},{7,11},{8,12},{9,13},{1... | collective-permute-start | bytes 1179656 | tf_op jit(solution)/shard_map/ppermute | solution.py:40
  84.7 12.1 %collective-permute-start.16 = (bf16[48,4224]{1,0:T(8,128)(2,1)}, bf16[48,4224]{1,0:T(8,128)(2,1)S(1)}, u32[]{:S(2)}, u32[]{:S(2)}) collective-permute-start(bf16[48,4224]{1,0:T(8,128)(2,1)} %collective-permute-done.15.refs_11_), channel_id=1, source_target_pairs={{0,28},{1,29},{2,30},{3,31},{4,0},{5,1},{6,2},{7,3},{8,4},{9,5},{1... | collective-permute-start | bytes 1216520 | tf_op jit(solution)/shard_map/ppermute | solution.py:40
  96.9 13.6 %copy-start = (bf16[512,512]{1,0:T(8,128)(2,1)S(1)}, bf16[512,512]{1,0:T(8,128)(2,1)}, u32[]{:S(2)}) copy-start(bf16[512,512]{1,0:T(8,128)(2,1)} %shard_map.106.chosen_ref) | copy-start | bytes 1572868
  101.1 6.5 %collective-permute-start.18 = (bf16[192,384]{1,0:T(8,128)(2,1)S(1)}, bf16[192,384]{1,0:T(8,128)(2,1)S(1)}, u32[]{:S(2)}, u32[]{:S(2)}) collective-permute-start(bf16[192,384]{1,0:T(8,128)(2,1)S(1)} %get-tuple-element.60), channel_id=1, source_target_pairs={{0,1},{1,2},{2,3},{3,0},{4,5},{5,6},{6,7},{7,4},{8,9},{9,10},{10,1... | collective-permute-start | bytes 442376 | tf_op jit(solution)/shard_map/ppermute | solution.py:45
  101.8 7.7 %collective-permute-start.19 = (bf16[192,384]{1,0:T(8,128)(2,1)S(1)}, bf16[192,384]{1,0:T(8,128)(2,1)S(1)}, u32[]{:S(2)}, u32[]{:S(2)}) collective-permute-start(bf16[192,384]{1,0:T(8,128)(2,1)S(1)} %get-tuple-element.61), channel_id=1, source_target_pairs={{0,2},{1,3},{2,0},{3,1},{4,6},{5,7},{6,4},{7,5},{8,10},{9,11},{10,... | collective-permute-start | bytes 442376 | tf_op jit(solution)/shard_map/ppermute | solution.py:45
  103.3 7.2 %collective-permute-start.20 = (bf16[192,384]{1,0:T(8,128)(2,1)S(1)}, bf16[192,384]{1,0:T(8,128)(2,1)S(1)}, u32[]{:S(2)}, u32[]{:S(2)}) collective-permute-start(bf16[192,384]{1,0:T(8,128)(2,1)S(1)} %get-tuple-element.62), channel_id=1, source_target_pairs={{0,3},{1,0},{2,1},{3,2},{4,7},{5,4},{6,5},{7,6},{8,11},{9,8},{10,9... | collective-permute-start | bytes 442376 | tf_op jit(solution)/shard_map/ppermute | solution.py:45
  (4 other events, 11.8 us)
Sparse Core Ops, SparseCore 0:
  10.6 74.1 all-gather.1

commit v3 on v2

--- a/solution.py
+++ b/solution.py
@@ -25,9 +25,11 @@
 LANES = NZ * SHARD
 PARTS = 2
 PART = DIM // PARTS
+STEP = 1024
 MEBI = 1024 * 1024
 VMEM_PROJECT = 16 * MEBI
-EXTRA = 128
+TILE = 128
+HIGH_ROWS = ROWS * (HALF // TILE) + SHARD
 ORDER = (0, 1, 2, 3, 5, 6, 7, 4)
 CHUNK = 512
 WEIGHT_GROUPS = [
@@ -72,10 +74,10 @@
 
 
 def split(place, rows, query, key, value):
-    steps = HALF // PART
+    steps = 1
 
     def mine(count):
-        return pl.BlockSpec((1, 1, count, PART), lambda k, p: (0, p[0], 0, k))
+        return pl.BlockSpec((1, 1, count, HALF), lambda k, p: (0, p[0], 0, k))
 
     return pl.pallas_call(
         split_kernel,
@@ -88,15 +90,15 @@
             num_scalar_prefetch=1,
             grid=(2 * steps,),
             in_specs=[
-                pl.BlockSpec((ROWS, PART), lambda k, p: (0, k)),
+                pl.BlockSpec((ROWS, HALF), lambda k, p: (0, k)),
                 mine(Q),
                 mine(KV),
                 mine(KV),
             ],
             out_specs=[
-                pl.BlockSpec((ROWS, PART), lambda k, p: (0, jnp.minimum(k, steps - 1))),
-                pl.BlockSpec((ROWS, PART), lambda k, p: (0, jnp.maximum(k - steps, 0))),
-                pl.BlockSpec((SIDE, PART), lambda k, p: (0, k)),
+                pl.BlockSpec((ROWS, HALF), lambda k, p: (0, jnp.minimum(k, steps - 1))),
+                pl.BlockSpec((ROWS, HALF), lambda k, p: (0, jnp.maximum(k - steps, 0))),
+                pl.BlockSpec((SIDE, HALF), lambda k, p: (0, k)),
             ],
         ),
         compiler_params=pltpu.CompilerParams(vmem_limit_bytes=16 * MEBI),
@@ -106,8 +108,10 @@
     )(place, *(pltpu.with_memory_space_constraint(x, pltpu.HBM) for x in (rows, query, key, value)))
 
 
-def weigh_kernel(first, own_ref, one_ref, two_ref, back_ref, gain_ref, *refs):
+def weigh_kernel(first, own_ref, two_ref, one_ref, back_ref, gain_ref, *refs):
     out_ref = refs[0] if first else refs[1]
+    lane = lax.broadcasted_iota(jnp.int32, (SHARD, TILE), 1)
+    scales = jnp.zeros((SHARD, TILE), jnp.float32)
     for t in range(STEPS):
         rows = slice(t * SHARD, (t + 1) * SHARD)
         back = back_ref[rows]
@@ -117,25 +121,31 @@
             own, one, two = (ref[rows, at].astype(jnp.float32) for ref in (own_ref, one_ref, two_ref))
             wide = jnp.where(back == 2, two, jnp.where(back == 1, one, own))
             squares += wide * wide
-            out_ref[rows, at] = (wide * gain_ref[:, at].astype(jnp.float32)).astype(jnp.bfloat16)
+            weighed = (wide * gain_ref[:, at].astype(jnp.float32)).astype(jnp.bfloat16)
+            if first:
+                out_ref[rows, at] = weighed
+                continue
+            for column in range(0, CHUNK, TILE):
+                target = (start + column) // TILE * ROWS + t * SHARD
+                out_ref[target : target + SHARD, :] = weighed[:, column : column + TILE]
         square = jnp.sum(squares, axis=-1, keepdims=True)
         if first:
             refs[1][rows] = square
             continue
         rest = lax.rsqrt((refs[0][rows] + square) / DIM + EPS)
-        lane = lax.broadcasted_iota(jnp.int32, (SHARD, EXTRA), 1)
-        tail = jnp.zeros((SHARD, EXTRA), jnp.float32)
         for i in range(3):
             term = rest.astype(jnp.bfloat16).astype(jnp.float32)
-            tail = jnp.where(lane == i, term, tail)
+            scales = jnp.where(lane == 3 * t + i, term, scales)
             rest = rest - term
-        out_ref[rows, HALF:] = tail.astype(jnp.bfloat16)
+    if not first:
+        out_ref[HIGH_ROWS - SHARD :, :] = scales.astype(jnp.bfloat16)
 
 
 def weigh_rows(states, back, gain, earlier):
     whole = pl.BlockSpec(memory_space=pltpu.VMEM)
     first = earlier is None
-    out_shape = [jax.ShapeDtypeStruct((ROWS, HALF + (0 if first else EXTRA)), jnp.bfloat16)]
+    shape = (ROWS, HALF) if first else (HIGH_ROWS, TILE)
+    out_shape = [jax.ShapeDtypeStruct(shape, jnp.bfloat16)]
     if first:
         out_shape.append(jax.ShapeDtypeStruct((ROWS, 1), jnp.float32))
     operands = [*states, back, gain] + ([] if first else [earlier])
@@ -170,19 +180,19 @@
     low_refs, high_refs = refs[:near], refs[near : 2 * near]
     total, weight_out, high_out, low, sems = refs[2 * near :]
     waiting = []
-    for part in range(HALF // PART):
-        at = slice(part * PART, (part + 1) * PART)
+    for part in range(HALF // STEP):
+        at = slice(part * STEP, (part + 1) * STEP)
         pairs = [(weight_ref.at[:, at], weight_out.at[:, at])]
         pairs += [(ref.at[:, at], low.at[i, :, at]) for i, ref in enumerate(low_refs)]
         waiting.append(copies(pairs, sems.at[part]))
     pairs = [(weight_ref.at[:, HALF:], weight_out.at[:, HALF:])]
     pairs += [(ref, high_out.at[i]) for i, ref in enumerate(high_refs)]
-    waiting.append(copies(pairs, sems.at[HALF // PART]))
-    for part in range(HALF // PART):
+    waiting.append(copies(pairs, sems.at[HALF // STEP]))
+    for part in range(HALF // STEP):
         for copy in waiting[part]:
             copy.wait()
-        at = slice(part * PART, (part + 1) * PART)
-        nothing = jnp.zeros((SHARD, PART), jnp.bfloat16)
+        at = slice(part * STEP, (part + 1) * STEP)
+        nothing = jnp.zeros((SHARD, STEP), jnp.bfloat16)
         rows = ordered(lambda i, rows: low[i, rows, at] if i < near else nothing)
         product = times(weight_out[:, at], rows)
         if part == 0:
@@ -202,13 +212,13 @@
         out_shape=[
             jax.ShapeDtypeStruct((NY * COLS, lanes), jnp.float32),
             jax.ShapeDtypeStruct(weight.shape, jnp.bfloat16),
-            jax.ShapeDtypeStruct((near, ROWS, HALF + EXTRA), jnp.bfloat16),
+            jax.ShapeDtypeStruct((near, HIGH_ROWS, TILE), jnp.bfloat16),
         ],
         in_specs=[pl.BlockSpec(memory_space=pltpu.HBM)] * len(operands),
         out_specs=[pl.BlockSpec(memory_space=pltpu.VMEM)] * 3,
         scratch_shapes=[
             pltpu.VMEM((near, ROWS, HALF), jnp.bfloat16),
-            pltpu.SemaphoreType.DMA((HALF // PART + 1, NZ)),
+            pltpu.SemaphoreType.DMA((HALF // STEP + 1, NZ)),
         ],
         compiler_params=pltpu.CompilerParams(vmem_limit_bytes=VMEM_PROJECT),
         cost_estimate=pl.CostEstimate(
@@ -250,18 +260,22 @@
 def last_kernel(place_ref, weight_ref, near_ref, far_ref, carried, cos_ref, sin_ref, *refs):
     *outs, total = refs
 
-    def part(first, width):
-        at = slice(first, first + width)
-        return ordered(
-            lambda i, rows: near_ref[i, rows, at] if i < NZ - 1 else far_ref[rows, at]
-        )
-
-    for first in range(0, HALF, PART):
-        at = HALF + first
-        product = times(weight_ref[:, at : at + PART], part(first, PART))
-        total[...] = (carried if first == 0 else total)[...] + product
-    ones = jnp.where(lax.broadcasted_iota(jnp.int32, (8, EXTRA), 1) < 3, 1.0, 0.0)
-    scale = times(ones.astype(jnp.bfloat16), part(HALF, EXTRA))[0:1]
+    def tile(i, first):
+        at = slice(first, first + SHARD)
+        return near_ref[i, at] if i < NZ - 1 else far_ref[at]
+
+    def piece(i, rows):
+        tiles = [tile(i, column * ROWS + rows.start) for column in range(HALF // TILE)]
+        return jnp.concatenate(tiles, axis=1)
+
+    total[...] = carried[...] + times(weight_ref[:, HALF:], ordered(piece))
+    scales = jnp.concatenate([tile(i, HIGH_ROWS - SHARD) for i in range(NZ)], axis=0)
+    lane = lax.broadcasted_iota(jnp.int32, (8, TILE), 1)
+    scale = []
+    for t in range(STEPS):
+        ones = jnp.where(lane // 3 == t, 1.0, 0.0).astype(jnp.bfloat16)
+        scale.append(times(ones, scales)[0:1])
+    scale = jnp.concatenate(scale, axis=1)
     y = place_ref[1]
 
     for by in range(NY):
@@ -316,11 +330,11 @@
     for i, d in enumerate(ORDER):
         distance = jnp.where(group == i, d, distance)
     plane = lax.rem(z + NZ - distance, NZ)
-    for by in range(NY):
+    for slot, by in enumerate((0, 2, 1, 3)):
         source = lax.rem(y + NY - by, NY)
         at = plane * (NY * SHARD) + source * SHARD + lane % SHARD
         chosen = jnp.where(at == column, 1.0, 0.0).astype(jnp.bfloat16)
-        out_ref[by * LANES : (by + 1) * LANES, :] = chosen
+        out_ref[slot * LANES : (slot + 1) * LANES, :] = chosen
 
 
 def choose_places(place):
@@ -401,7 +415,7 @@
     for mine in own:
         two = lax.ppermute(mine, "section", [(1, 3)])
         one = lax.ppermute(mine, "section", [(1, 2), (2, 3)])
-        moved.append((mine, one, two))
+        moved.append((mine, two, one))
     low, square = weigh_rows(moved[0], back, norm_gain[:, :HALF], None)
     (high,) = weigh_rows(moved[1], back, norm_gain[:, HALF:], square)
 
@@ -425,7 +439,7 @@
     carried, weight, near = project_first(weight, low[:-1], high[:-1])
     carried = project_second(weight, low[-1], carried)
     outs = project_last(place, weight, near, high[-1], carried, cosine, sine)
-    pieces = [outs[0], shift_y(outs[1], 1), shift_y(outs[2], 2), shift_y(outs[3], -1)]
+    pieces = [outs[0], shift_y(outs[2], 2), shift_y(outs[1], 1), shift_y(outs[3], -1)]
     return tuple(place_outputs(chosen, pieces))
 
 

time: 120 us -> 119 us (level)
  transfers between devices with their start and end apart: 22 -> 22, of which waited for: 10 -> 9; matrix products, arithmetic and copies ran while one was open for 1% -> 1% of each run, Pallas kernels for 10% -> 9%
where the time goes in v3:
time: 119 us
  waiting for transfers between devices  51.7 us (43%)
  starting transfers between devices  30.5 us (26%)
  Pallas kernels  19.5 us (16%)
  between operations  14.3 us (12%)
  other arithmetic  1.53 us (1%)
    ppermute x14, waiting for transfers between devices, shift_z(): return lax.ppermute(value, 'tensor', pairs)  34.8 us
    ppermute x14, starting transfers between devices, shift_z(): return lax.ppermute(value, 'tensor', pairs)  23.1 us
    all_gather x1, waiting for transfers between devices, on_device(): lax.all_gather(half, ('dp', 'tensor'), axis_index_groups=WEIGHT_GROUPS, t...  11.7 us
    pallas_call x1, Pallas kernels, project_first(): pl.pallas_call(first_kernel, out_shape=[jax.ShapeDtypeStruct((NY * COLS,...  6.52 us
    ppermute x3, waiting for transfers between devices, shift_y(): return lax.ppermute(value, 'tensor', pairs)  5.31 us
    ppermute x3, starting transfers between devices, shift_y(): return lax.ppermute(value, 'tensor', pairs)  4.59 us
    pallas_call x1, Pallas kernels, project_last(): pl.pallas_call(last_kernel, out_shape=[jax.ShapeDtypeStruct((COLS, lanes)...  4.25 us
    pallas_call x1, Pallas kernels, split(): pl.pallas_call(split_kernel, out_shape=[jax.ShapeDtypeStruct((ROWS, HALF)...  3.12 us
  transfers between devices with their start and end apart: 22, of which 9 were waited for; matrix products, arithmetic and copies ran while one was open for 1% of the time, Pallas kernels for 9%

profile of v3, /device:TPU:1, one launch (start us, length us, event | category | flops | bytes accessed | tf_op | source)
XLA Modules:
  0.0 118.6 jit_solution(15918598203525000208)
XLA Ops:
  7.3 3.1 %shard_map.103 = (bf16[48,4096]{1,0:T(8,128)(2,1)S(1)}, bf16[48,4096]{1,0:T(8,128)(2,1)S(1)}, bf16[96,8192]{1,0:T(8,128)(2,1)}) custom-call(s32[3]{0:T(128)S(1)} %pad_add_fusion.place_ref, bf16[48,8192]{1,0:T(8,128)(2,1)} %bitcast.6, bf16[1,2,64,8192]{3,2,1,0:T(8,128)(2,1)} %query_ref.1, bf16[1,2,16,8192]{3,2,1,0:T(8,128)(2,1)} %key_ref.1, ...), custom_call_target="tpu_custom_call" | custom-call | bytes 4718592 | tf_op jit(solution)/shard_map/pallas_call | solution.py:82
  10.5 0.7 collective-permute-start.2
  11.2 0.7 collective-permute-start.3
  11.9 0.7 collective-permute-start
  12.6 0.7 collective-permute-start.1
  13.3 0.8 minimum_subtract_fusion
  14.6 2.5 %collective-permute-start.8 = (bf16[48,4096]{1,0:T(8,128)(2,1)S(1)}, bf16[48,4096]{1,0:T(8,128)(2,1)S(1)}, u32[]{:S(2)}, u32[]{:S(2)}) collective-permute-start(bf16[48,4096]{1,0:T(8,128)(2,1)S(1)} %get-tuple-element.44.refs_0_), channel_id=1, source_target_pairs={{0,4},{1,5},{2,6},{3,7},{4,8},{5,9},{6,10},{7,11},{8,12},{9,13},{1... | collective-permute-start | bytes 1179656 | tf_op jit(solution)/shard_map/ppermute | solution.py:42
  17.0 4.0 %collective-permute-start.9 = (bf16[48,4096]{1,0:T(8,128)(2,1)S(1)}, bf16[48,4096]{1,0:T(8,128)(2,1)}, u32[]{:S(2)}, u32[]{:S(2)}) collective-permute-start(bf16[48,4096]{1,0:T(8,128)(2,1)S(1)} %get-tuple-element.44.refs_0_), channel_id=1, source_target_pairs={{0,28},{1,29},{2,30},{3,31},{4,0},{5,1},{6,2},{7,3},{8,4},{9,5},{1... | collective-permute-start | bytes 1179656 | tf_op jit(solution)/shard_map/ppermute | solution.py:42
  21.1 0.5 shard_map.105.refs_7_
  21.6 2.7 %collective-permute-start.5 = (bf16[1552,128]{1,0:T(8,128)(2,1)S(1)}, bf16[1552,128]{1,0:T(8,128)(2,1)S(1)}, u32[]{:S(2)}, u32[]{:S(2)}) collective-permute-start(bf16[1552,128]{1,0:T(8,128)(2,1)S(1)} %shard_map.105.refs_7_), channel_id=1, source_target_pairs={{0,28},{1,29},{2,30},{3,31},{4,0},{5,1},{6,2},{7,3},{8,4},{9,5},{1... | collective-permute-start | bytes 1191944 | tf_op jit(solution)/shard_map/ppermute | solution.py:42
  24.5 5.3 %collective-permute-done.8.refs_1_ = bf16[48,4096]{1,0:T(8,128)(2,1)S(1)} collective-permute-done((bf16[48,4096]{1,0:T(8,128)(2,1)S(1)}, bf16[48,4096]{1,0:T(8,128)(2,1)S(1)}, u32[]{:S(2)}, u32[]{:S(2)}) %collective-permute-start.8) | collective-permute-done | bytes 393248 | tf_op jit(solution)/shard_map/ppermute | solution.py:42
  29.8 2.7 %collective-permute-start.11 = (bf16[48,4096]{1,0:T(8,128)(2,1)}, bf16[48,4096]{1,0:T(8,128)(2,1)}, u32[]{:S(2)}, u32[]{:S(2)}) collective-permute-start(bf16[48,4096]{1,0:T(8,128)(2,1)} %collective-permute-done.9.refs_6_), channel_id=1, source_target_pairs={{0,28},{1,29},{2,30},{3,31},{4,0},{5,1},{6,2},{7,3},{8,4},{9,5},{1... | collective-permute-start | bytes 1179656 | tf_op jit(solution)/shard_map/ppermute | solution.py:42
  32.7 5.8 %collective-permute-done.4.refs_8_ = bf16[1552,128]{1,0:T(8,128)(2,1)S(1)} collective-permute-done((bf16[1552,128]{1,0:T(8,128)(2,1)S(1)}, bf16[1552,128]{1,0:T(8,128)(2,1)S(1)}, u32[]{:S(2)}, u32[]{:S(2)}) %collective-permute-start.4) | collective-permute-done | bytes 397344 | tf_op jit(solution)/shard_map/ppermute | solution.py:42
  38.5 2.7 %collective-permute-start.7 = (bf16[1552,128]{1,0:T(8,128)(2,1)S(1)}, bf16[1552,128]{1,0:T(8,128)(2,1)S(1)}, u32[]{:S(2)}, u32[]{:S(2)}) collective-permute-start(bf16[1552,128]{1,0:T(8,128)(2,1)S(1)} %collective-permute-done.5.refs_13_), channel_id=1, source_target_pairs={{0,28},{1,29},{2,30},{3,31},{4,0},{5,1},{6,2},{7,3},{8,4},{9,5},{1... | collective-permute-start | bytes 1191944 | tf_op jit(solution)/shard_map/ppermute | solution.py:42
  41.2 5.7 %collective-permute-done.10.refs_2_ = bf16[48,4096]{1,0:T(8,128)(2,1)S(1)} collective-permute-done((bf16[48,4096]{1,0:T(8,128)(2,1)S(1)}, bf16[48,4096]{1,0:T(8,128)(2,1)S(1)}, u32[]{:S(2)}, u32[]{:S(2)}) %collective-permute-start.10) | collective-permute-done | bytes 393248 | tf_op jit(solution)/shard_map/ppermute | solution.py:42
  46.9 2.7 %collective-permute-start.13 = (bf16[48,4096]{1,0:T(8,128)(2,1)}, bf16[48,4096]{1,0:T(8,128)(2,1)}, u32[]{:S(2)}, u32[]{:S(2)}) collective-permute-start(bf16[48,4096]{1,0:T(8,128)(2,1)} %collective-permute-done.11.refs_5_), channel_id=1, source_target_pairs={{0,28},{1,29},{2,30},{3,31},{4,0},{5,1},{6,2},{7,3},{8,4},{9,5},{1... | collective-permute-start | bytes 1179656 | tf_op jit(solution)/shard_map/ppermute | solution.py:42
  50.0 1.6 %shard_map.106.chosen_ref = bf16[512,512]{1,0:T(8,128)(2,1)} custom-call(s32[3]{0:T(128)} %copy-done.3), custom_call_target="tpu_custom_call" | custom-call | tf_op jit(solution)/shard_map/pallas_call | solution.py:341
  51.6 3.8 %collective-permute-done.6.refs_9_ = bf16[1552,128]{1,0:T(8,128)(2,1)S(1)} collective-permute-done((bf16[1552,128]{1,0:T(8,128)(2,1)S(1)}, bf16[1552,128]{1,0:T(8,128)(2,1)S(1)}, u32[]{:S(2)}, u32[]{:S(2)}) %collective-permute-start.6) | collective-permute-done | bytes 397344 | tf_op jit(solution)/shard_map/ppermute | solution.py:42
  55.5 2.7 %collective-permute-start.15 = (bf16[1552,128]{1,0:T(8,128)(2,1)S(1)}, bf16[1552,128]{1,0:T(8,128)(2,1)S(1)}, u32[]{:S(2)}, u32[]{:S(2)}) collective-permute-start(bf16[1552,128]{1,0:T(8,128)(2,1)S(1)} %collective-permute-done.7.refs_12_), channel_id=1, source_target_pairs={{0,28},{1,29},{2,30},{3,31},{4,0},{5,1},{6,2},{7,3},{8,4},{9,5},{1... | collective-permute-start | bytes 1191944 | tf_op jit(solution)/shard_map/ppermute | solution.py:42
  58.2 5.7 %collective-permute-done.12.refs_3_ = bf16[48,4096]{1,0:T(8,128)(2,1)} collective-permute-done((bf16[48,4096]{1,0:T(8,128)(2,1)S(1)}, bf16[48,4096]{1,0:T(8,128)(2,1)}, u32[]{:S(2)}, u32[]{:S(2)}) %collective-permute-start.12) | collective-permute-done | bytes 393248 | tf_op jit(solution)/shard_map/ppermute | solution.py:42
  63.8 8.5 %collective-permute-done.14.refs_10_ = bf16[1552,128]{1,0:T(8,128)(2,1)S(1)} collective-permute-done((bf16[1552,128]{1,0:T(8,128)(2,1)S(1)}, bf16[1552,128]{1,0:T(8,128)(2,1)S(1)}, u32[]{:S(2)}, u32[]{:S(2)}) %collective-permute-start.14) | collective-permute-done | bytes 397344 | tf_op jit(solution)/shard_map/ppermute | solution.py:42
  72.3 0.8 copy-done.10
  73.1 11.7 %all-gather.2.cloned.1.call-done.weight_ref = bf16[768,8192]{1,0:T(8,128)(2,1)} async-done(((bf16[96,8192]{1,0:T(8,128)(2,1)}), bf16[768,8192]{1,0:T(8,128)(2,1)}) %all-gather.2.cloned.1.call-update) | async-done | bytes 12582928 | tf_op jit(solution)/shard_map/all_gather | solution.py:410
  84.8 3.0 %collective-permute-start.16 = (bf16[1552,128]{1,0:T(8,128)(2,1)S(1)}, bf16[1552,128]{1,0:T(8,128)(2,1)S(1)}, u32[]{:S(2)}, u32[]{:S(2)}) collective-permute-start(bf16[1552,128]{1,0:T(8,128)(2,1)S(1)} %collective-permute-done.15.refs_11_), channel_id=1, source_target_pairs={{0,28},{1,29},{2,30},{3,31},{4,0},{5,1},{6,2},{7,3},{8,4},{9,5},{1... | collective-permute-start | bytes 1191944 | tf_op jit(solution)/shard_map/ppermute | solution.py:42
  87.8 6.5 %shard_map.107 = (f32[768,384]{1,0:T(8,128)S(1)}, bf16[768,8192]{1,0:T(8,128)(2,1)S(1)}, bf16[7,1552,128]{2,1,0:T(8,128)(2,1)S(1)}) custom-call(bf16[768,8192]{1,0:T(8,128)(2,1)} %all-gather.2.cloned.1.call-done.weight_ref, bf16[48,4096]{1,0:T(8,128)(2,1)} %copy-done.2, bf16[48,4096]{1,0:T(8,128)(2,1)} %copy-done.11, bf16[48,4096]{1,0:T(8,128)(2,1)} %copy-done.12, ...), custom_call_target="tpu_custom_call" | custom-call | flops 2415919104 | bytes 25165824 | tf_op jit(solution)/shard_map/pallas_call | solution.py:210
  94.4 1.9 %shard_map.108.carried = f32[768,384]{1,0:T(8,128)S(1)} custom-call(bf16[768,8192]{1,0:T(8,128)(2,1)S(1)} %get-tuple-element.51.weight_ref, bf16[48,4096]{1,0:T(8,128)(2,1)S(1)} %collective-permute-done.17.far_ref, f32[768,384]{1,0:T(8,128)S(1)} %get-tuple-element.56.carried_ref), custom_call_target="tpu_custom_call" | custom-call | flops 805306368 | bytes 6291456 | tf_op jit(solution)/shard_map/pallas_call | solution.py:246
  96.4 4.3 %shard_map.109 = (bf16[192,384]{1,0:T(8,128)(2,1)S(1)}, bf16[192,384]{1,0:T(8,128)(2,1)S(1)}, bf16[192,384]{1,0:T(8,128)(2,1)S(1)}, bf16[192,384]{1,0:T(8,128)(2,1)S(1)}) custom-call(s32[3]{0:T(128)S(1)} %copy-done.4, bf16[768,8192]{1,0:T(8,128)(2,1)S(1)} %get-tuple-element.51.weight_ref, bf16[7,1552,128]{2,1,0:T(8,128)(2,1)S(1)} %get-tuple-element.52.near_ref, ...), custom_call_target="tpu_custom_call" | custom-call | flops 2415919104 | bytes 9437184 | tf_op jit(solution)/shard_map/pallas_call | solution.py:308
  100.6 1.9 %collective-permute-start.18 = (bf16[192,384]{1,0:T(8,128)(2,1)S(1)}, bf16[192,384]{1,0:T(8,128)(2,1)S(1)}, u32[]{:S(2)}, u32[]{:S(2)}) collective-permute-start(bf16[192,384]{1,0:T(8,128)(2,1)S(1)} %get-tuple-element.60), channel_id=1, source_target_pairs={{0,2},{1,3},{2,0},{3,1},{4,6},{5,7},{6,4},{7,5},{8,10},{9,11},{10,... | collective-permute-start | bytes 442376 | tf_op jit(solution)/shard_map/ppermute | solution.py:47
  102.5 2.7 %collective-permute-start.20 = (bf16[192,384]{1,0:T(8,128)(2,1)S(1)}, bf16[192,384]{1,0:T(8,128)(2,1)S(1)}, u32[]{:S(2)}, u32[]{:S(2)}) collective-permute-start(bf16[192,384]{1,0:T(8,128)(2,1)S(1)} %get-tuple-element.62), channel_id=1, source_target_pairs={{0,3},{1,0},{2,1},{3,2},{4,7},{5,4},{6,5},{7,6},{8,11},{9,8},{10,9... | collective-permute-start | bytes 442376 | tf_op jit(solution)/shard_map/ppermute | solution.py:47
  105.2 1.5 %collective-permute-done.18.refs_1_ = bf16[192,384]{1,0:T(8,128)(2,1)S(1)} collective-permute-done((bf16[192,384]{1,0:T(8,128)(2,1)S(1)}, bf16[192,384]{1,0:T(8,128)(2,1)S(1)}, u32[]{:S(2)}, u32[]{:S(2)}) %collective-permute-start.18) | collective-permute-done | bytes 147488 | tf_op jit(solution)/shard_map/ppermute | solution.py:47
  106.7 3.8 %collective-permute-done.19.refs_2_ = bf16[192,384]{1,0:T(8,128)(2,1)S(1)} collective-permute-done((bf16[192,384]{1,0:T(8,128)(2,1)S(1)}, bf16[192,384]{1,0:T(8,128)(2,1)S(1)}, u32[]{:S(2)}, u32[]{:S(2)}) %collective-permute-start.19) | collective-permute-done | bytes 147488 | tf_op jit(solution)/shard_map/ppermute | solution.py:47
  110.5 1.2 %shard_map.110 = (bf16[3,1,2,16,512]{4,3,2,1,0:T(8,128)(2,1)}, bf16[3,1,2,16,512]{4,3,2,1,0:T(8,128)(2,1)}, bf16[3,1,2,64,512]{4,3,2,1,0:T(8,128)(2,1)}) custom-call(bf16[512,512]{1,0:T(8,128)(2,1)S(1)} %copy-done, bf16[192,384]{1,0:T(8,128)(2,1)S(1)} %get-tuple-element.59.refs_0_, bf16[192,384]{1,0:T(8,128)(2,1)S(1)} %collective-permute-done.18.refs_1_, ...), custom_call_target="tpu_custom_call" | custom-call | tf_op jit(solution)/shard_map/pallas_call | solution.py:367
  (64 shorter events, 1.8 us)
Async XLA Ops:
  7.2 77.6 %all-gather.2.cloned.1.call-start = ((), (), s32[]{:S(2)}) async-start(), calls=%async_computation | async-start | bytes 14155776 | tf_op jit(solution)/shard_map/all_gather | solution.py:410
  10.4 22.1 %copy-start.14 = (s32[512]{0:T(512)S(1)}, s32[512]{0:T(512)}, u32[]{:S(2)}) copy-start(s32[512]{0:T(512)} %param.10) | copy-start | bytes 6148
  10.5 3.7 %collective-permute-start.2 = (bf16[48,4096]{1,0:T(8,128)(2,1)S(1)}, bf16[48,4096]{1,0:T(8,128)(2,1)S(1)}, u32[]{:S(2)}, u32[]{:S(2)}) collective-permute-start(bf16[48,4096]{1,0:T(8,128)(2,1)S(1)} %get-tuple-element.34.own_ref), channel_id=1, source_target_pairs={{32,96},{33,97},{34,98},{35,99},{36,100},{37,101},{38,102},{39,103... | collective-permute-start | bytes 1179656 | tf_op jit(solution)/shard_map/ppermute | solution.py:416
  11.2 3.0 %collective-permute-start.3 = (bf16[48,4096]{1,0:T(8,128)(2,1)S(1)}, bf16[48,4096]{1,0:T(8,128)(2,1)S(1)}, u32[]{:S(2)}, u32[]{:S(2)}) collective-permute-start(bf16[48,4096]{1,0:T(8,128)(2,1)S(1)} %get-tuple-element.34.own_ref), channel_id=1, source_target_pairs={{32,64},{64,96},{33,65},{65,97},{34,66},{66,98},{35,67},{67,99},{3... | collective-permute-start | bytes 1179656 | tf_op jit(solution)/shard_map/ppermute | solution.py:417
  11.9 9.2 %collective-permute-start = (bf16[48,4096]{1,0:T(8,128)(2,1)S(1)}, bf16[48,4096]{1,0:T(8,128)(2,1)S(1)}, u32[]{:S(2)}, u32[]{:S(2)}) collective-permute-start(bf16[48,4096]{1,0:T(8,128)(2,1)S(1)} %get-tuple-element.33.own_ref), channel_id=1, source_target_pairs={{32,96},{33,97},{34,98},{35,99},{36,100},{37,101},{38,102},{39,103... | collective-permute-start | bytes 1179656 | tf_op jit(solution)/shard_map/ppermute | solution.py:416
  12.6 8.5 %collective-permute-start.1 = (bf16[48,4096]{1,0:T(8,128)(2,1)S(1)}, bf16[48,4096]{1,0:T(8,128)(2,1)S(1)}, u32[]{:S(2)}, u32[]{:S(2)}) collective-permute-start(bf16[48,4096]{1,0:T(8,128)(2,1)S(1)} %get-tuple-element.33.own_ref), channel_id=1, source_target_pairs={{32,64},{64,96},{33,65},{65,97},{34,66},{66,98},{35,67},{67,99},{3... | collective-permute-start | bytes 1179656 | tf_op jit(solution)/shard_map/ppermute | solution.py:417
  14.6 73.2 %copy-start.2 = (bf16[48,4096]{1,0:T(8,128)(2,1)}, bf16[48,4096]{1,0:T(8,128)(2,1)S(1)}, u32[]{:S(2)}) copy-start(bf16[48,4096]{1,0:T(8,128)(2,1)S(1)} %get-tuple-element.44.refs_0_) | copy-start | bytes 1179652
  14.6 15.3 %collective-permute-start.8 = (bf16[48,4096]{1,0:T(8,128)(2,1)S(1)}, bf16[48,4096]{1,0:T(8,128)(2,1)S(1)}, u32[]{:S(2)}, u32[]{:S(2)}) collective-permute-start(bf16[48,4096]{1,0:T(8,128)(2,1)S(1)} %get-tuple-element.44.refs_0_), channel_id=1, source_target_pairs={{0,4},{1,5},{2,6},{3,7},{4,8},{5,9},{6,10},{7,11},{8,12},{9,13},{1... | collective-permute-start | bytes 1179656 | tf_op jit(solution)/shard_map/ppermute | solution.py:42
  17.0 12.8 %collective-permute-start.9 = (bf16[48,4096]{1,0:T(8,128)(2,1)S(1)}, bf16[48,4096]{1,0:T(8,128)(2,1)}, u32[]{:S(2)}, u32[]{:S(2)}) collective-permute-start(bf16[48,4096]{1,0:T(8,128)(2,1)S(1)} %get-tuple-element.44.refs_0_), channel_id=1, source_target_pairs={{0,28},{1,29},{2,30},{3,31},{4,0},{5,1},{6,2},{7,3},{8,4},{9,5},{1... | collective-permute-start | bytes 1179656 | tf_op jit(solution)/shard_map/ppermute | solution.py:42
  21.5 66.3 %copy-start.1 = (bf16[1552,128]{1,0:T(8,128)(2,1)}, bf16[1552,128]{1,0:T(8,128)(2,1)S(1)}, u32[]{:S(2)}) copy-start(bf16[1552,128]{1,0:T(8,128)(2,1)S(1)} %shard_map.105.refs_7_) | copy-start | bytes 1191940
  21.6 16.9 %collective-permute-start.4 = (bf16[1552,128]{1,0:T(8,128)(2,1)S(1)}, bf16[1552,128]{1,0:T(8,128)(2,1)S(1)}, u32[]{:S(2)}, u32[]{:S(2)}) collective-permute-start(bf16[1552,128]{1,0:T(8,128)(2,1)S(1)} %shard_map.105.refs_7_), channel_id=1, source_target_pairs={{0,4},{1,5},{2,6},{3,7},{4,8},{5,9},{6,10},{7,11},{8,12},{9,13},{1... | collective-permute-start | bytes 1191944 | tf_op jit(solution)/shard_map/ppermute | solution.py:42
  21.6 16.8 %collective-permute-start.5 = (bf16[1552,128]{1,0:T(8,128)(2,1)S(1)}, bf16[1552,128]{1,0:T(8,128)(2,1)S(1)}, u32[]{:S(2)}, u32[]{:S(2)}) collective-permute-start(bf16[1552,128]{1,0:T(8,128)(2,1)S(1)} %shard_map.105.refs_7_), channel_id=1, source_target_pairs={{0,28},{1,29},{2,30},{3,31},{4,0},{5,1},{6,2},{7,3},{8,4},{9,5},{1... | collective-permute-start | bytes 1191944 | tf_op jit(solution)/shard_map/ppermute | solution.py:42
  29.8 25.6 %copy-start.11 = (bf16[48,4096]{1,0:T(8,128)(2,1)}, bf16[48,4096]{1,0:T(8,128)(2,1)S(1)}, u32[]{:S(2)}) copy-start(bf16[48,4096]{1,0:T(8,128)(2,1)S(1)} %collective-permute-done.8.refs_1_) | copy-start | bytes 1179652
  29.8 17.0 %collective-permute-start.10 = (bf16[48,4096]{1,0:T(8,128)(2,1)S(1)}, bf16[48,4096]{1,0:T(8,128)(2,1)S(1)}, u32[]{:S(2)}, u32[]{:S(2)}) collective-permute-start(bf16[48,4096]{1,0:T(8,128)(2,1)S(1)} %collective-permute-done.8.refs_1_), channel_id=1, source_target_pairs={{0,4},{1,5},{2,6},{3,7},{4,8},{5,9},{6,10},{7,11},{8,12},{9,13},{1... | collective-permute-start | bytes 1179656 | tf_op jit(solution)/shard_map/ppermute | solution.py:42
  29.8 17.0 %collective-permute-start.11 = (bf16[48,4096]{1,0:T(8,128)(2,1)}, bf16[48,4096]{1,0:T(8,128)(2,1)}, u32[]{:S(2)}, u32[]{:S(2)}) collective-permute-start(bf16[48,4096]{1,0:T(8,128)(2,1)} %collective-permute-done.9.refs_6_), channel_id=1, source_target_pairs={{0,28},{1,29},{2,30},{3,31},{4,0},{5,1},{6,2},{7,3},{8,4},{9,5},{1... | collective-permute-start | bytes 1179656 | tf_op jit(solution)/shard_map/ppermute | solution.py:42
  38.4 49.4 %copy-start.5 = (bf16[1552,128]{1,0:T(8,128)(2,1)}, bf16[1552,128]{1,0:T(8,128)(2,1)S(1)}, u32[]{:S(2)}) copy-start(bf16[1552,128]{1,0:T(8,128)(2,1)S(1)} %collective-permute-done.4.refs_8_) | copy-start | bytes 1191940
  38.4 49.4 %copy-start.6 = (bf16[1552,128]{1,0:T(8,128)(2,1)}, bf16[1552,128]{1,0:T(8,128)(2,1)S(1)}, u32[]{:S(2)}) copy-start(bf16[1552,128]{1,0:T(8,128)(2,1)S(1)} %collective-permute-done.5.refs_13_) | copy-start | bytes 1191940
  38.5 16.9 %collective-permute-start.6 = (bf16[1552,128]{1,0:T(8,128)(2,1)S(1)}, bf16[1552,128]{1,0:T(8,128)(2,1)S(1)}, u32[]{:S(2)}, u32[]{:S(2)}) collective-permute-start(bf16[1552,128]{1,0:T(8,128)(2,1)S(1)} %collective-permute-done.4.refs_8_), channel_id=1, source_target_pairs={{0,4},{1,5},{2,6},{3,7},{4,8},{5,9},{6,10},{7,11},{8,12},{9,13},{1... | collective-permute-start | bytes 1191944 | tf_op jit(solution)/shard_map/ppermute | solution.py:42
  38.5 16.9 %collective-permute-start.7 = (bf16[1552,128]{1,0:T(8,128)(2,1)S(1)}, bf16[1552,128]{1,0:T(8,128)(2,1)S(1)}, u32[]{:S(2)}, u32[]{:S(2)}) collective-permute-start(bf16[1552,128]{1,0:T(8,128)(2,1)S(1)} %collective-permute-done.5.refs_13_), channel_id=1, source_target_pairs={{0,28},{1,29},{2,30},{3,31},{4,0},{5,1},{6,2},{7,3},{8,4},{9,5},{1... | collective-permute-start | bytes 1191944 | tf_op jit(solution)/shard_map/ppermute | solution.py:42
  46.9 16.9 %copy-start.12 = (bf16[48,4096]{1,0:T(8,128)(2,1)}, bf16[48,4096]{1,0:T(8,128)(2,1)S(1)}, u32[]{:S(2)}) copy-start(bf16[48,4096]{1,0:T(8,128)(2,1)S(1)} %collective-permute-done.10.refs_2_) | copy-start | bytes 1179652
  46.9 16.9 %collective-permute-start.12 = (bf16[48,4096]{1,0:T(8,128)(2,1)S(1)}, bf16[48,4096]{1,0:T(8,128)(2,1)}, u32[]{:S(2)}, u32[]{:S(2)}) collective-permute-start(bf16[48,4096]{1,0:T(8,128)(2,1)S(1)} %collective-permute-done.10.refs_2_), channel_id=1, source_target_pairs={{0,4},{1,5},{2,6},{3,7},{4,8},{5,9},{6,10},{7,11},{8,12},{9,13},{1... | collective-permute-start | bytes 1179656 | tf_op jit(solution)/shard_map/ppermute | solution.py:42
  46.9 16.9 %collective-permute-start.13 = (bf16[48,4096]{1,0:T(8,128)(2,1)}, bf16[48,4096]{1,0:T(8,128)(2,1)}, u32[]{:S(2)}, u32[]{:S(2)}) collective-permute-start(bf16[48,4096]{1,0:T(8,128)(2,1)} %collective-permute-done.11.refs_5_), channel_id=1, source_target_pairs={{0,28},{1,29},{2,30},{3,31},{4,0},{5,1},{6,2},{7,3},{8,4},{9,5},{1... | collective-permute-start | bytes 1179656 | tf_op jit(solution)/shard_map/ppermute | solution.py:42
  55.4 32.4 %copy-start.7 = (bf16[1552,128]{1,0:T(8,128)(2,1)}, bf16[1552,128]{1,0:T(8,128)(2,1)S(1)}, u32[]{:S(2)}) copy-start(bf16[1552,128]{1,0:T(8,128)(2,1)S(1)} %collective-permute-done.6.refs_9_) | copy-start | bytes 1191940
  55.4 32.4 %copy-start.8 = (bf16[1552,128]{1,0:T(8,128)(2,1)}, bf16[1552,128]{1,0:T(8,128)(2,1)S(1)}, u32[]{:S(2)}) copy-start(bf16[1552,128]{1,0:T(8,128)(2,1)S(1)} %collective-permute-done.7.refs_12_) | copy-start | bytes 1191940
  55.4 16.9 %collective-permute-start.14 = (bf16[1552,128]{1,0:T(8,128)(2,1)S(1)}, bf16[1552,128]{1,0:T(8,128)(2,1)S(1)}, u32[]{:S(2)}, u32[]{:S(2)}) collective-permute-start(bf16[1552,128]{1,0:T(8,128)(2,1)S(1)} %collective-permute-done.6.refs_9_), channel_id=1, source_target_pairs={{0,4},{1,5},{2,6},{3,7},{4,8},{5,9},{6,10},{7,11},{8,12},{9,13},{1... | collective-permute-start | bytes 1191944 | tf_op jit(solution)/shard_map/ppermute | solution.py:42
  55.5 17.6 %collective-permute-start.15 = (bf16[1552,128]{1,0:T(8,128)(2,1)S(1)}, bf16[1552,128]{1,0:T(8,128)(2,1)S(1)}, u32[]{:S(2)}, u32[]{:S(2)}) collective-permute-start(bf16[1552,128]{1,0:T(8,128)(2,1)S(1)} %collective-permute-done.7.refs_12_), channel_id=1, source_target_pairs={{0,28},{1,29},{2,30},{3,31},{4,0},{5,1},{6,2},{7,3},{8,4},{9,5},{1... | collective-permute-start | bytes 1191944 | tf_op jit(solution)/shard_map/ppermute | solution.py:42
  63.8 30.5 %collective-permute-start.17 = (bf16[48,4096]{1,0:T(8,128)(2,1)}, bf16[48,4096]{1,0:T(8,128)(2,1)S(1)}, u32[]{:S(2)}, u32[]{:S(2)}) collective-permute-start(bf16[48,4096]{1,0:T(8,128)(2,1)} %collective-permute-done.12.refs_3_), channel_id=1, source_target_pairs={{0,4},{1,5},{2,6},{3,7},{4,8},{5,9},{6,10},{7,11},{8,12},{9,13},{1... | collective-permute-start | bytes 1179656 | tf_op jit(solution)/shard_map/ppermute | solution.py:42
  73.1 14.7 %copy-start.9 = (bf16[1552,128]{1,0:T(8,128)(2,1)}, bf16[1552,128]{1,0:T(8,128)(2,1)S(1)}, u32[]{:S(2)}) copy-start(bf16[1552,128]{1,0:T(8,128)(2,1)S(1)} %collective-permute-done.15.refs_11_) | copy-start | bytes 1191940
  84.8 11.6 %collective-permute-start.16 = (bf16[1552,128]{1,0:T(8,128)(2,1)S(1)}, bf16[1552,128]{1,0:T(8,128)(2,1)S(1)}, u32[]{:S(2)}, u32[]{:S(2)}) collective-permute-start(bf16[1552,128]{1,0:T(8,128)(2,1)S(1)} %collective-permute-done.15.refs_11_), channel_id=1, source_target_pairs={{0,28},{1,29},{2,30},{3,31},{4,0},{5,1},{6,2},{7,3},{8,4},{9,5},{1... | collective-permute-start | bytes 1191944 | tf_op jit(solution)/shard_map/ppermute | solution.py:42
  100.6 6.1 %collective-permute-start.18 = (bf16[192,384]{1,0:T(8,128)(2,1)S(1)}, bf16[192,384]{1,0:T(8,128)(2,1)S(1)}, u32[]{:S(2)}, u32[]{:S(2)}) collective-permute-start(bf16[192,384]{1,0:T(8,128)(2,1)S(1)} %get-tuple-element.60), channel_id=1, source_target_pairs={{0,2},{1,3},{2,0},{3,1},{4,6},{5,7},{6,4},{7,5},{8,10},{9,11},{10,... | collective-permute-start | bytes 442376 | tf_op jit(solution)/shard_map/ppermute | solution.py:47
  102.5 8.0 %collective-permute-start.19 = (bf16[192,384]{1,0:T(8,128)(2,1)S(1)}, bf16[192,384]{1,0:T(8,128)(2,1)S(1)}, u32[]{:S(2)}, u32[]{:S(2)}) collective-permute-start(bf16[192,384]{1,0:T(8,128)(2,1)S(1)} %get-tuple-element.61), channel_id=1, source_target_pairs={{0,1},{1,2},{2,3},{3,0},{4,5},{5,6},{6,7},{7,4},{8,9},{9,10},{10,1... | collective-permute-start | bytes 442376 | tf_op jit(solution)/shard_map/ppermute | solution.py:47
  102.5 8.0 %collective-permute-start.20 = (bf16[192,384]{1,0:T(8,128)(2,1)S(1)}, bf16[192,384]{1,0:T(8,128)(2,1)S(1)}, u32[]{:S(2)}, u32[]{:S(2)}) collective-permute-start(bf16[192,384]{1,0:T(8,128)(2,1)S(1)} %get-tuple-element.62), channel_id=1, source_target_pairs={{0,3},{1,0},{2,1},{3,2},{4,7},{5,4},{6,5},{7,6},{8,11},{9,8},{10,9... | collective-permute-start | bytes 442376 | tf_op jit(solution)/shard_map/ppermute | solution.py:47
  (6 other events, 39.9 us)
Sparse Core Ops, SparseCore 0:
  10.6 74.1 all-gather.1

commit v4 on v3

--- a/solution.py
+++ b/solution.py
@@ -206,7 +206,8 @@
 def project_first(weight, low, high):
     near = NZ - 1
     lanes = STEPS * LANES
-    operands = [pltpu.with_memory_space_constraint(x, pltpu.HBM) for x in (weight, *low, *high)]
+    fixed = [pltpu.with_memory_space_constraint(x, pltpu.HBM) for x in (weight, *low, *high)]
+    operands = [high[i - near - 1] if i == near + 4 else x for i, x in enumerate(fixed)]
     return pl.pallas_call(
         first_kernel,
         out_shape=[
@@ -214,7 +215,10 @@
             jax.ShapeDtypeStruct(weight.shape, jnp.bfloat16),
             jax.ShapeDtypeStruct((near, HIGH_ROWS, TILE), jnp.bfloat16),
         ],
-        in_specs=[pl.BlockSpec(memory_space=pltpu.HBM)] * len(operands),
+        in_specs=[
+            pl.BlockSpec(memory_space=pl.ANY if i == near + 4 else pltpu.HBM)
+            for i in range(len(operands))
+        ],
         out_specs=[pl.BlockSpec(memory_space=pltpu.VMEM)] * 3,
         scratch_shapes=[
             pltpu.VMEM((near, ROWS, HALF), jnp.bfloat16),

time: 119 us -> 119 us (level)
  transfers between devices with their start and end apart: 22 -> 22, of which waited for: 9 -> 10; matrix products, arithmetic and copies ran while one was open for 1% -> 1% of each run, Pallas kernels for 9% -> 9%
where the time goes in v4:
time: 119 us
  waiting for transfers between devices  52.5 us (44%)
  starting transfers between devices  30.5 us (26%)
  Pallas kernels  19.5 us (16%)
  between operations  14.3 us (12%)
  other arithmetic  1.53 us (1%)
    ppermute x14, waiting for transfers between devices, shift_z(): return lax.ppermute(value, 'tensor', pairs)  35 us
    ppermute x14, starting transfers between devices, shift_z(): return lax.ppermute(value, 'tensor', pairs)  23.1 us
    all_gather x1, waiting for transfers between devices, on_device(): lax.all_gather(half, ('dp', 'tensor'), axis_index_groups=WEIGHT_GROUPS, t...  12.4 us
    pallas_call x1, Pallas kernels, project_first(): pl.pallas_call(first_kernel, out_shape=[jax.ShapeDtypeStruct((NY * COLS,...  6.46 us
    ppermute x3, waiting for transfers between devices, shift_y(): return lax.ppermute(value, 'tensor', pairs)  5.08 us
    ppermute x3, starting transfers between devices, shift_y(): return lax.ppermute(value, 'tensor', pairs)  4.59 us
    pallas_call x1, Pallas kernels, project_last(): pl.pallas_call(last_kernel, out_shape=[jax.ShapeDtypeStruct((COLS, lanes)...  4.24 us
    pallas_call x1, Pallas kernels, split(): pl.pallas_call(split_kernel, out_shape=[jax.ShapeDtypeStruct((ROWS, HALF)...  3.14 us
  transfers between devices with their start and end apart: 22, of which 10 were waited for; matrix products, arithmetic and copies ran while one was open for 1% of the time, Pallas kernels for 9%

profile of v4, /device:TPU:1, one launch (start us, length us, event | category | flops | bytes accessed | tf_op | source)
XLA Modules:
  0.0 118.5 jit_solution(9234013146894874570)
XLA Ops:
  7.3 3.1 %shard_map.103 = (bf16[48,4096]{1,0:T(8,128)(2,1)S(1)}, bf16[48,4096]{1,0:T(8,128)(2,1)S(1)}, bf16[96,8192]{1,0:T(8,128)(2,1)}) custom-call(s32[3]{0:T(128)S(1)} %pad_add_fusion.place_ref, bf16[48,8192]{1,0:T(8,128)(2,1)} %bitcast.6, bf16[1,2,64,8192]{3,2,1,0:T(8,128)(2,1)} %query_ref.1, bf16[1,2,16,8192]{3,2,1,0:T(8,128)(2,1)} %key_ref.1, ...), custom_call_target="tpu_custom_call" | custom-call | bytes 4718592 | tf_op jit(solution)/shard_map/pallas_call | solution.py:82
  10.5 0.7 collective-permute-start.2
  11.2 0.7 collective-permute-start.3
  11.9 0.7 collective-permute-start
  12.6 0.7 collective-permute-start.1
  13.3 0.8 minimum_subtract_fusion
  14.6 2.5 %collective-permute-start.8 = (bf16[48,4096]{1,0:T(8,128)(2,1)S(1)}, bf16[48,4096]{1,0:T(8,128)(2,1)}, u32[]{:S(2)}, u32[]{:S(2)}) collective-permute-start(bf16[48,4096]{1,0:T(8,128)(2,1)S(1)} %get-tuple-element.44.refs_0_), channel_id=1, source_target_pairs={{0,4},{1,5},{2,6},{3,7},{4,8},{5,9},{6,10},{7,11},{8,12},{9,13},{1... | collective-permute-start | bytes 1179656 | tf_op jit(solution)/shard_map/ppermute | solution.py:42
  17.1 4.0 %collective-permute-start.9 = (bf16[48,4096]{1,0:T(8,128)(2,1)S(1)}, bf16[48,4096]{1,0:T(8,128)(2,1)}, u32[]{:S(2)}, u32[]{:S(2)}) collective-permute-start(bf16[48,4096]{1,0:T(8,128)(2,1)S(1)} %get-tuple-element.44.refs_0_), channel_id=1, source_target_pairs={{0,28},{1,29},{2,30},{3,31},{4,0},{5,1},{6,2},{7,3},{8,4},{9,5},{1... | collective-permute-start | bytes 1179656 | tf_op jit(solution)/shard_map/ppermute | solution.py:42
  21.1 0.5 shard_map.105.refs_7_
  21.7 2.7 %collective-permute-start.5 = (bf16[1552,128]{1,0:T(8,128)(2,1)S(1)}, bf16[1552,128]{1,0:T(8,128)(2,1)S(1)}, u32[]{:S(2)}, u32[]{:S(2)}) collective-permute-start(bf16[1552,128]{1,0:T(8,128)(2,1)S(1)} %shard_map.105.refs_7_), channel_id=1, source_target_pairs={{0,28},{1,29},{2,30},{3,31},{4,0},{5,1},{6,2},{7,3},{8,4},{9,5},{1... | collective-permute-start | bytes 1191944 | tf_op jit(solution)/shard_map/ppermute | solution.py:42
  24.5 5.4 %collective-permute-done.8.refs_1_ = bf16[48,4096]{1,0:T(8,128)(2,1)} collective-permute-done((bf16[48,4096]{1,0:T(8,128)(2,1)S(1)}, bf16[48,4096]{1,0:T(8,128)(2,1)}, u32[]{:S(2)}, u32[]{:S(2)}) %collective-permute-start.8) | collective-permute-done | bytes 393248 | tf_op jit(solution)/shard_map/ppermute | solution.py:42
  30.0 2.7 %collective-permute-start.11 = (bf16[48,4096]{1,0:T(8,128)(2,1)}, bf16[48,4096]{1,0:T(8,128)(2,1)}, u32[]{:S(2)}, u32[]{:S(2)}) collective-permute-start(bf16[48,4096]{1,0:T(8,128)(2,1)} %collective-permute-done.9.refs_6_), channel_id=1, source_target_pairs={{0,28},{1,29},{2,30},{3,31},{4,0},{5,1},{6,2},{7,3},{8,4},{9,5},{1... | collective-permute-start | bytes 1179656 | tf_op jit(solution)/shard_map/ppermute | solution.py:42
  32.8 5.7 %collective-permute-done.4.refs_8_ = bf16[1552,128]{1,0:T(8,128)(2,1)S(1)} collective-permute-done((bf16[1552,128]{1,0:T(8,128)(2,1)S(1)}, bf16[1552,128]{1,0:T(8,128)(2,1)S(1)}, u32[]{:S(2)}, u32[]{:S(2)}) %collective-permute-start.4) | collective-permute-done | bytes 397344 | tf_op jit(solution)/shard_map/ppermute | solution.py:42
  38.6 2.7 %collective-permute-start.7 = (bf16[1552,128]{1,0:T(8,128)(2,1)S(1)}, bf16[1552,128]{1,0:T(8,128)(2,1)S(1)}, u32[]{:S(2)}, u32[]{:S(2)}) collective-permute-start(bf16[1552,128]{1,0:T(8,128)(2,1)S(1)} %collective-permute-done.5.refs_13_), channel_id=1, source_target_pairs={{0,28},{1,29},{2,30},{3,31},{4,0},{5,1},{6,2},{7,3},{8,4},{9,5},{1... | collective-permute-start | bytes 1191944 | tf_op jit(solution)/shard_map/ppermute | solution.py:42
  41.2 5.7 %collective-permute-done.10.refs_2_ = bf16[48,4096]{1,0:T(8,128)(2,1)S(1)} collective-permute-done((bf16[48,4096]{1,0:T(8,128)(2,1)}, bf16[48,4096]{1,0:T(8,128)(2,1)S(1)}, u32[]{:S(2)}, u32[]{:S(2)}) %collective-permute-start.10) | collective-permute-done | bytes 393248 | tf_op jit(solution)/shard_map/ppermute | solution.py:42
  46.9 2.7 %collective-permute-start.13 = (bf16[48,4096]{1,0:T(8,128)(2,1)}, bf16[48,4096]{1,0:T(8,128)(2,1)}, u32[]{:S(2)}, u32[]{:S(2)}) collective-permute-start(bf16[48,4096]{1,0:T(8,128)(2,1)} %collective-permute-done.11.refs_5_), channel_id=1, source_target_pairs={{0,28},{1,29},{2,30},{3,31},{4,0},{5,1},{6,2},{7,3},{8,4},{9,5},{1... | collective-permute-start | bytes 1179656 | tf_op jit(solution)/shard_map/ppermute | solution.py:42
  49.6 0.4 multiply_sine_fusion
  50.0 1.6 %shard_map.106.chosen_ref = bf16[512,512]{1,0:T(8,128)(2,1)} custom-call(s32[3]{0:T(128)} %copy-done.3), custom_call_target="tpu_custom_call" | custom-call | tf_op jit(solution)/shard_map/pallas_call | solution.py:345
  51.6 3.8 %collective-permute-done.6.refs_9_ = bf16[1552,128]{1,0:T(8,128)(2,1)S(1)} collective-permute-done((bf16[1552,128]{1,0:T(8,128)(2,1)S(1)}, bf16[1552,128]{1,0:T(8,128)(2,1)S(1)}, u32[]{:S(2)}, u32[]{:S(2)}) %collective-permute-start.6) | collective-permute-done | bytes 397344 | tf_op jit(solution)/shard_map/ppermute | solution.py:42
  55.5 2.7 %collective-permute-start.15 = (bf16[1552,128]{1,0:T(8,128)(2,1)S(1)}, bf16[1552,128]{1,0:T(8,128)(2,1)}, u32[]{:S(2)}, u32[]{:S(2)}) collective-permute-start(bf16[1552,128]{1,0:T(8,128)(2,1)S(1)} %collective-permute-done.7.refs_12_), channel_id=1, source_target_pairs={{0,28},{1,29},{2,30},{3,31},{4,0},{5,1},{6,2},{7,3},{8,4},{9,5},{1... | collective-permute-start | bytes 1191944 | tf_op jit(solution)/shard_map/ppermute | solution.py:42
  58.2 5.7 %collective-permute-done.12.refs_3_ = bf16[48,4096]{1,0:T(8,128)(2,1)} collective-permute-done((bf16[48,4096]{1,0:T(8,128)(2,1)S(1)}, bf16[48,4096]{1,0:T(8,128)(2,1)}, u32[]{:S(2)}, u32[]{:S(2)}) %collective-permute-start.12) | collective-permute-done | bytes 393248 | tf_op jit(solution)/shard_map/ppermute | solution.py:42
  63.8 8.5 %collective-permute-done.14.refs_10_ = bf16[1552,128]{1,0:T(8,128)(2,1)S(1)} collective-permute-done((bf16[1552,128]{1,0:T(8,128)(2,1)S(1)}, bf16[1552,128]{1,0:T(8,128)(2,1)S(1)}, u32[]{:S(2)}, u32[]{:S(2)}) %collective-permute-start.14) | collective-permute-done | bytes 397344 | tf_op jit(solution)/shard_map/ppermute | solution.py:42
  72.3 12.4 %all-gather.2.cloned.1.call-done.weight_ref = bf16[768,8192]{1,0:T(8,128)(2,1)} async-done(((bf16[96,8192]{1,0:T(8,128)(2,1)}), bf16[768,8192]{1,0:T(8,128)(2,1)}) %all-gather.2.cloned.1.call-update) | async-done | bytes 12582928 | tf_op jit(solution)/shard_map/all_gather | solution.py:414
  84.8 3.0 %collective-permute-start.16 = (bf16[1552,128]{1,0:T(8,128)(2,1)}, bf16[1552,128]{1,0:T(8,128)(2,1)S(1)}, u32[]{:S(2)}, u32[]{:S(2)}) collective-permute-start(bf16[1552,128]{1,0:T(8,128)(2,1)} %collective-permute-done.15.refs_11_), channel_id=1, source_target_pairs={{0,28},{1,29},{2,30},{3,31},{4,0},{5,1},{6,2},{7,3},{8,4},{9,5},{1... | collective-permute-start | bytes 1191944 | tf_op jit(solution)/shard_map/ppermute | solution.py:42
  87.8 6.5 %shard_map.107 = (f32[768,384]{1,0:T(8,128)S(1)}, bf16[768,8192]{1,0:T(8,128)(2,1)S(1)}, bf16[7,1552,128]{2,1,0:T(8,128)(2,1)S(1)}) custom-call(bf16[768,8192]{1,0:T(8,128)(2,1)} %all-gather.2.cloned.1.call-done.weight_ref, bf16[48,4096]{1,0:T(8,128)(2,1)} %copy-done.2, bf16[48,4096]{1,0:T(8,128)(2,1)} %collective-permute-done.8.refs_1_, ...), custom_call_target="tpu_custom_call" | custom-call | flops 2415919104 | bytes 25165824 | tf_op jit(solution)/shard_map/pallas_call | solution.py:211
  94.3 1.9 %shard_map.108.carried = f32[768,384]{1,0:T(8,128)S(1)} custom-call(bf16[768,8192]{1,0:T(8,128)(2,1)S(1)} %get-tuple-element.51.weight_ref, bf16[48,4096]{1,0:T(8,128)(2,1)S(1)} %collective-permute-done.17.far_ref, f32[768,384]{1,0:T(8,128)S(1)} %get-tuple-element.56.carried_ref), custom_call_target="tpu_custom_call" | custom-call | flops 805306368 | bytes 6291456 | tf_op jit(solution)/shard_map/pallas_call | solution.py:250
  96.5 4.2 %shard_map.109 = (bf16[192,384]{1,0:T(8,128)(2,1)S(1)}, bf16[192,384]{1,0:T(8,128)(2,1)S(1)}, bf16[192,384]{1,0:T(8,128)(2,1)S(1)}, bf16[192,384]{1,0:T(8,128)(2,1)S(1)}) custom-call(s32[3]{0:T(128)S(1)} %copy-done.4, bf16[768,8192]{1,0:T(8,128)(2,1)S(1)} %get-tuple-element.51.weight_ref, bf16[7,1552,128]{2,1,0:T(8,128)(2,1)S(1)} %get-tuple-element.52.near_ref, ...), custom_call_target="tpu_custom_call" | custom-call | flops 2415919104 | bytes 9437184 | tf_op jit(solution)/shard_map/pallas_call | solution.py:312
  100.7 1.9 %collective-permute-start.18 = (bf16[192,384]{1,0:T(8,128)(2,1)S(1)}, bf16[192,384]{1,0:T(8,128)(2,1)S(1)}, u32[]{:S(2)}, u32[]{:S(2)}) collective-permute-start(bf16[192,384]{1,0:T(8,128)(2,1)S(1)} %get-tuple-element.60), channel_id=1, source_target_pairs={{0,2},{1,3},{2,0},{3,1},{4,6},{5,7},{6,4},{7,5},{8,10},{9,11},{10,... | collective-permute-start | bytes 442376 | tf_op jit(solution)/shard_map/ppermute | solution.py:47
  102.6 2.7 %collective-permute-start.20 = (bf16[192,384]{1,0:T(8,128)(2,1)S(1)}, bf16[192,384]{1,0:T(8,128)(2,1)S(1)}, u32[]{:S(2)}, u32[]{:S(2)}) collective-permute-start(bf16[192,384]{1,0:T(8,128)(2,1)S(1)} %get-tuple-element.62), channel_id=1, source_target_pairs={{0,3},{1,0},{2,1},{3,2},{4,7},{5,4},{6,5},{7,6},{8,11},{9,8},{10,9... | collective-permute-start | bytes 442376 | tf_op jit(solution)/shard_map/ppermute | solution.py:47
  105.3 1.0 collective-permute-done.18.refs_1_
  106.3 4.1 %collective-permute-done.19.refs_2_ = bf16[192,384]{1,0:T(8,128)(2,1)S(1)} collective-permute-done((bf16[192,384]{1,0:T(8,128)(2,1)S(1)}, bf16[192,384]{1,0:T(8,128)(2,1)S(1)}, u32[]{:S(2)}, u32[]{:S(2)}) %collective-permute-start.19) | collective-permute-done | bytes 147488 | tf_op jit(solution)/shard_map/ppermute | solution.py:47
  110.4 1.2 %shard_map.110 = (bf16[3,1,2,16,512]{4,3,2,1,0:T(8,128)(2,1)}, bf16[3,1,2,16,512]{4,3,2,1,0:T(8,128)(2,1)}, bf16[3,1,2,64,512]{4,3,2,1,0:T(8,128)(2,1)}) custom-call(bf16[512,512]{1,0:T(8,128)(2,1)S(1)} %copy-done, bf16[192,384]{1,0:T(8,128)(2,1)S(1)} %get-tuple-element.59.refs_0_, bf16[192,384]{1,0:T(8,128)(2,1)S(1)} %collective-permute-done.18.refs_1_, ...), custom_call_target="tpu_custom_call" | custom-call | tf_op jit(solution)/shard_map/pallas_call | solution.py:371
  (58 shorter events, 1.5 us)
Async XLA Ops:
  7.2 77.6 %all-gather.2.cloned.1.call-start = ((), (), s32[]{:S(2)}) async-start(), calls=%async_computation | async-start | bytes 14155776 | tf_op jit(solution)/shard_map/all_gather | solution.py:414
  10.4 13.9 %copy-start.12 = (s32[8]{0:T(128)S(1)}, s32[8]{0:T(128)}, u32[]{:S(2)}) copy-start(s32[8]{0:T(128)} %constant.81) | copy-start | bytes 100
  10.5 22.2 %copy-start.11 = (s32[512]{0:T(512)S(1)}, s32[512]{0:T(512)}, u32[]{:S(2)}) copy-start(s32[512]{0:T(512)} %param.10) | copy-start | bytes 6148
  10.5 3.7 %collective-permute-start.2 = (bf16[48,4096]{1,0:T(8,128)(2,1)S(1)}, bf16[48,4096]{1,0:T(8,128)(2,1)S(1)}, u32[]{:S(2)}, u32[]{:S(2)}) collective-permute-start(bf16[48,4096]{1,0:T(8,128)(2,1)S(1)} %get-tuple-element.34.own_ref), channel_id=1, source_target_pairs={{32,96},{33,97},{34,98},{35,99},{36,100},{37,101},{38,102},{39,103... | collective-permute-start | bytes 1179656 | tf_op jit(solution)/shard_map/ppermute | solution.py:420
  11.2 3.0 %collective-permute-start.3 = (bf16[48,4096]{1,0:T(8,128)(2,1)S(1)}, bf16[48,4096]{1,0:T(8,128)(2,1)S(1)}, u32[]{:S(2)}, u32[]{:S(2)}) collective-permute-start(bf16[48,4096]{1,0:T(8,128)(2,1)S(1)} %get-tuple-element.34.own_ref), channel_id=1, source_target_pairs={{32,64},{64,96},{33,65},{65,97},{34,66},{66,98},{35,67},{67,99},{3... | collective-permute-start | bytes 1179656 | tf_op jit(solution)/shard_map/ppermute | solution.py:421
  11.9 9.2 %collective-permute-start = (bf16[48,4096]{1,0:T(8,128)(2,1)S(1)}, bf16[48,4096]{1,0:T(8,128)(2,1)S(1)}, u32[]{:S(2)}, u32[]{:S(2)}) collective-permute-start(bf16[48,4096]{1,0:T(8,128)(2,1)S(1)} %get-tuple-element.33.own_ref), channel_id=1, source_target_pairs={{32,96},{33,97},{34,98},{35,99},{36,100},{37,101},{38,102},{39,103... | collective-permute-start | bytes 1179656 | tf_op jit(solution)/shard_map/ppermute | solution.py:420
  12.6 8.5 %collective-permute-start.1 = (bf16[48,4096]{1,0:T(8,128)(2,1)S(1)}, bf16[48,4096]{1,0:T(8,128)(2,1)S(1)}, u32[]{:S(2)}, u32[]{:S(2)}) collective-permute-start(bf16[48,4096]{1,0:T(8,128)(2,1)S(1)} %get-tuple-element.33.own_ref), channel_id=1, source_target_pairs={{32,64},{64,96},{33,65},{65,97},{34,66},{66,98},{35,67},{67,99},{3... | collective-permute-start | bytes 1179656 | tf_op jit(solution)/shard_map/ppermute | solution.py:421
  14.6 73.2 %copy-start.2 = (bf16[48,4096]{1,0:T(8,128)(2,1)}, bf16[48,4096]{1,0:T(8,128)(2,1)S(1)}, u32[]{:S(2)}) copy-start(bf16[48,4096]{1,0:T(8,128)(2,1)S(1)} %get-tuple-element.44.refs_0_) | copy-start | bytes 1179652
  14.6 15.4 %collective-permute-start.8 = (bf16[48,4096]{1,0:T(8,128)(2,1)S(1)}, bf16[48,4096]{1,0:T(8,128)(2,1)}, u32[]{:S(2)}, u32[]{:S(2)}) collective-permute-start(bf16[48,4096]{1,0:T(8,128)(2,1)S(1)} %get-tuple-element.44.refs_0_), channel_id=1, source_target_pairs={{0,4},{1,5},{2,6},{3,7},{4,8},{5,9},{6,10},{7,11},{8,12},{9,13},{1... | collective-permute-start | bytes 1179656 | tf_op jit(solution)/shard_map/ppermute | solution.py:42
  17.1 12.9 %collective-permute-start.9 = (bf16[48,4096]{1,0:T(8,128)(2,1)S(1)}, bf16[48,4096]{1,0:T(8,128)(2,1)}, u32[]{:S(2)}, u32[]{:S(2)}) collective-permute-start(bf16[48,4096]{1,0:T(8,128)(2,1)S(1)} %get-tuple-element.44.refs_0_), channel_id=1, source_target_pairs={{0,28},{1,29},{2,30},{3,31},{4,0},{5,1},{6,2},{7,3},{8,4},{9,5},{1... | collective-permute-start | bytes 1179656 | tf_op jit(solution)/shard_map/ppermute | solution.py:42
  21.6 66.3 %copy-start.1 = (bf16[1552,128]{1,0:T(8,128)(2,1)}, bf16[1552,128]{1,0:T(8,128)(2,1)S(1)}, u32[]{:S(2)}) copy-start(bf16[1552,128]{1,0:T(8,128)(2,1)S(1)} %shard_map.105.refs_7_) | copy-start | bytes 1191940
  21.6 16.9 %collective-permute-start.4 = (bf16[1552,128]{1,0:T(8,128)(2,1)S(1)}, bf16[1552,128]{1,0:T(8,128)(2,1)S(1)}, u32[]{:S(2)}, u32[]{:S(2)}) collective-permute-start(bf16[1552,128]{1,0:T(8,128)(2,1)S(1)} %shard_map.105.refs_7_), channel_id=1, source_target_pairs={{0,4},{1,5},{2,6},{3,7},{4,8},{5,9},{6,10},{7,11},{8,12},{9,13},{1... | collective-permute-start | bytes 1191944 | tf_op jit(solution)/shard_map/ppermute | solution.py:42
  21.7 16.8 %collective-permute-start.5 = (bf16[1552,128]{1,0:T(8,128)(2,1)S(1)}, bf16[1552,128]{1,0:T(8,128)(2,1)S(1)}, u32[]{:S(2)}, u32[]{:S(2)}) collective-permute-start(bf16[1552,128]{1,0:T(8,128)(2,1)S(1)} %shard_map.105.refs_7_), channel_id=1, source_target_pairs={{0,28},{1,29},{2,30},{3,31},{4,0},{5,1},{6,2},{7,3},{8,4},{9,5},{1... | collective-permute-start | bytes 1191944 | tf_op jit(solution)/shard_map/ppermute | solution.py:42
  30.0 16.9 %collective-permute-start.10 = (bf16[48,4096]{1,0:T(8,128)(2,1)}, bf16[48,4096]{1,0:T(8,128)(2,1)S(1)}, u32[]{:S(2)}, u32[]{:S(2)}) collective-permute-start(bf16[48,4096]{1,0:T(8,128)(2,1)} %collective-permute-done.8.refs_1_), channel_id=1, source_target_pairs={{0,4},{1,5},{2,6},{3,7},{4,8},{5,9},{6,10},{7,11},{8,12},{9,13},{1... | collective-permute-start | bytes 1179656 | tf_op jit(solution)/shard_map/ppermute | solution.py:42
  30.0 16.9 %collective-permute-start.11 = (bf16[48,4096]{1,0:T(8,128)(2,1)}, bf16[48,4096]{1,0:T(8,128)(2,1)}, u32[]{:S(2)}, u32[]{:S(2)}) collective-permute-start(bf16[48,4096]{1,0:T(8,128)(2,1)} %collective-permute-done.9.refs_6_), channel_id=1, source_target_pairs={{0,28},{1,29},{2,30},{3,31},{4,0},{5,1},{6,2},{7,3},{8,4},{9,5},{1... | collective-permute-start | bytes 1179656 | tf_op jit(solution)/shard_map/ppermute | solution.py:42
  38.5 49.4 %copy-start.5 = (bf16[1552,128]{1,0:T(8,128)(2,1)}, bf16[1552,128]{1,0:T(8,128)(2,1)S(1)}, u32[]{:S(2)}) copy-start(bf16[1552,128]{1,0:T(8,128)(2,1)S(1)} %collective-permute-done.4.refs_8_) | copy-start | bytes 1191940
  38.5 49.4 %copy-start.6 = (bf16[1552,128]{1,0:T(8,128)(2,1)}, bf16[1552,128]{1,0:T(8,128)(2,1)S(1)}, u32[]{:S(2)}) copy-start(bf16[1552,128]{1,0:T(8,128)(2,1)S(1)} %collective-permute-done.5.refs_13_) | copy-start | bytes 1191940
  38.5 16.9 %collective-permute-start.6 = (bf16[1552,128]{1,0:T(8,128)(2,1)S(1)}, bf16[1552,128]{1,0:T(8,128)(2,1)S(1)}, u32[]{:S(2)}, u32[]{:S(2)}) collective-permute-start(bf16[1552,128]{1,0:T(8,128)(2,1)S(1)} %collective-permute-done.4.refs_8_), channel_id=1, source_target_pairs={{0,4},{1,5},{2,6},{3,7},{4,8},{5,9},{6,10},{7,11},{8,12},{9,13},{1... | collective-permute-start | bytes 1191944 | tf_op jit(solution)/shard_map/ppermute | solution.py:42
  38.6 16.9 %collective-permute-start.7 = (bf16[1552,128]{1,0:T(8,128)(2,1)S(1)}, bf16[1552,128]{1,0:T(8,128)(2,1)S(1)}, u32[]{:S(2)}, u32[]{:S(2)}) collective-permute-start(bf16[1552,128]{1,0:T(8,128)(2,1)S(1)} %collective-permute-done.5.refs_13_), channel_id=1, source_target_pairs={{0,28},{1,29},{2,30},{3,31},{4,0},{5,1},{6,2},{7,3},{8,4},{9,5},{1... | collective-permute-start | bytes 1191944 | tf_op jit(solution)/shard_map/ppermute | solution.py:42
  46.9 16.9 %copy-start.9 = (bf16[48,4096]{1,0:T(8,128)(2,1)}, bf16[48,4096]{1,0:T(8,128)(2,1)S(1)}, u32[]{:S(2)}) copy-start(bf16[48,4096]{1,0:T(8,128)(2,1)S(1)} %collective-permute-done.10.refs_2_) | copy-start | bytes 1179652
  46.9 16.9 %collective-permute-start.12 = (bf16[48,4096]{1,0:T(8,128)(2,1)S(1)}, bf16[48,4096]{1,0:T(8,128)(2,1)}, u32[]{:S(2)}, u32[]{:S(2)}) collective-permute-start(bf16[48,4096]{1,0:T(8,128)(2,1)S(1)} %collective-permute-done.10.refs_2_), channel_id=1, source_target_pairs={{0,4},{1,5},{2,6},{3,7},{4,8},{5,9},{6,10},{7,11},{8,12},{9,13},{1... | collective-permute-start | bytes 1179656 | tf_op jit(solution)/shard_map/ppermute | solution.py:42
  46.9 16.9 %collective-permute-start.13 = (bf16[48,4096]{1,0:T(8,128)(2,1)}, bf16[48,4096]{1,0:T(8,128)(2,1)}, u32[]{:S(2)}, u32[]{:S(2)}) collective-permute-start(bf16[48,4096]{1,0:T(8,128)(2,1)} %collective-permute-done.11.refs_5_), channel_id=1, source_target_pairs={{0,28},{1,29},{2,30},{3,31},{4,0},{5,1},{6,2},{7,3},{8,4},{9,5},{1... | collective-permute-start | bytes 1179656 | tf_op jit(solution)/shard_map/ppermute | solution.py:42
  55.4 32.4 %copy-start.7 = (bf16[1552,128]{1,0:T(8,128)(2,1)}, bf16[1552,128]{1,0:T(8,128)(2,1)S(1)}, u32[]{:S(2)}) copy-start(bf16[1552,128]{1,0:T(8,128)(2,1)S(1)} %collective-permute-done.6.refs_9_) | copy-start | bytes 1191940
  55.4 32.4 %copy-start.8 = (bf16[1552,128]{1,0:T(8,128)(2,1)}, bf16[1552,128]{1,0:T(8,128)(2,1)S(1)}, u32[]{:S(2)}) copy-start(bf16[1552,128]{1,0:T(8,128)(2,1)S(1)} %collective-permute-done.7.refs_12_) | copy-start | bytes 1191940
  55.4 16.9 %collective-permute-start.14 = (bf16[1552,128]{1,0:T(8,128)(2,1)S(1)}, bf16[1552,128]{1,0:T(8,128)(2,1)S(1)}, u32[]{:S(2)}, u32[]{:S(2)}) collective-permute-start(bf16[1552,128]{1,0:T(8,128)(2,1)S(1)} %collective-permute-done.6.refs_9_), channel_id=1, source_target_pairs={{0,4},{1,5},{2,6},{3,7},{4,8},{5,9},{6,10},{7,11},{8,12},{9,13},{1... | collective-permute-start | bytes 1191944 | tf_op jit(solution)/shard_map/ppermute | solution.py:42
  55.5 16.8 %collective-permute-start.15 = (bf16[1552,128]{1,0:T(8,128)(2,1)S(1)}, bf16[1552,128]{1,0:T(8,128)(2,1)}, u32[]{:S(2)}, u32[]{:S(2)}) collective-permute-start(bf16[1552,128]{1,0:T(8,128)(2,1)S(1)} %collective-permute-done.7.refs_12_), channel_id=1, source_target_pairs={{0,28},{1,29},{2,30},{3,31},{4,0},{5,1},{6,2},{7,3},{8,4},{9,5},{1... | collective-permute-start | bytes 1191944 | tf_op jit(solution)/shard_map/ppermute | solution.py:42
  63.8 30.5 %collective-permute-start.17 = (bf16[48,4096]{1,0:T(8,128)(2,1)}, bf16[48,4096]{1,0:T(8,128)(2,1)S(1)}, u32[]{:S(2)}, u32[]{:S(2)}) collective-permute-start(bf16[48,4096]{1,0:T(8,128)(2,1)} %collective-permute-done.12.refs_3_), channel_id=1, source_target_pairs={{0,4},{1,5},{2,6},{3,7},{4,8},{5,9},{6,10},{7,11},{8,12},{9,13},{1... | collective-permute-start | bytes 1179656 | tf_op jit(solution)/shard_map/ppermute | solution.py:42
  84.8 11.7 %collective-permute-start.16 = (bf16[1552,128]{1,0:T(8,128)(2,1)}, bf16[1552,128]{1,0:T(8,128)(2,1)S(1)}, u32[]{:S(2)}, u32[]{:S(2)}) collective-permute-start(bf16[1552,128]{1,0:T(8,128)(2,1)} %collective-permute-done.15.refs_11_), channel_id=1, source_target_pairs={{0,28},{1,29},{2,30},{3,31},{4,0},{5,1},{6,2},{7,3},{8,4},{9,5},{1... | collective-permute-start | bytes 1191944 | tf_op jit(solution)/shard_map/ppermute | solution.py:42
  96.5 13.9 %copy-start = (bf16[512,512]{1,0:T(8,128)(2,1)S(1)}, bf16[512,512]{1,0:T(8,128)(2,1)}, u32[]{:S(2)}) copy-start(bf16[512,512]{1,0:T(8,128)(2,1)} %shard_map.106.chosen_ref) | copy-start | bytes 1572868
  100.7 5.6 %collective-permute-start.18 = (bf16[192,384]{1,0:T(8,128)(2,1)S(1)}, bf16[192,384]{1,0:T(8,128)(2,1)S(1)}, u32[]{:S(2)}, u32[]{:S(2)}) collective-permute-start(bf16[192,384]{1,0:T(8,128)(2,1)S(1)} %get-tuple-element.60), channel_id=1, source_target_pairs={{0,2},{1,3},{2,0},{3,1},{4,6},{5,7},{6,4},{7,5},{8,10},{9,11},{10,... | collective-permute-start | bytes 442376 | tf_op jit(solution)/shard_map/ppermute | solution.py:47
  102.6 7.8 %collective-permute-start.19 = (bf16[192,384]{1,0:T(8,128)(2,1)S(1)}, bf16[192,384]{1,0:T(8,128)(2,1)S(1)}, u32[]{:S(2)}, u32[]{:S(2)}) collective-permute-start(bf16[192,384]{1,0:T(8,128)(2,1)S(1)} %get-tuple-element.61), channel_id=1, source_target_pairs={{0,1},{1,2},{2,3},{3,0},{4,5},{5,6},{6,7},{7,4},{8,9},{9,10},{10,1... | collective-permute-start | bytes 442376 | tf_op jit(solution)/shard_map/ppermute | solution.py:47
  102.6 7.8 %collective-permute-start.20 = (bf16[192,384]{1,0:T(8,128)(2,1)S(1)}, bf16[192,384]{1,0:T(8,128)(2,1)S(1)}, u32[]{:S(2)}, u32[]{:S(2)}) collective-permute-start(bf16[192,384]{1,0:T(8,128)(2,1)S(1)} %get-tuple-element.62), channel_id=1, source_target_pairs={{0,3},{1,0},{2,1},{3,2},{4,7},{5,4},{6,5},{7,6},{8,11},{9,8},{10,9... | collective-permute-start | bytes 442376 | tf_op jit(solution)/shard_map/ppermute | solution.py:47
  (3 other events, 11.3 us)
Sparse Core Ops, SparseCore 0:
  10.6 74.1 all-gather.1
